TPU v7x, 32 devices: a whole 2x2x4 slice. The times are simulated.
32 devices in a mesh: fine: 16 (over z, y, x), coarse: 2 (over core).
Axes of the slice: x: 2, y: 2, z: 4, core: 2. Of those that a mesh axis runs over, the one named last changes fastest.
Arguments:
- load_cases: bfloat16 [32, 16, 1024], P(('fine', 'coarse')), may hold values from -6 to 6
- dual_ops: bfloat16 [32, 1024, 1024], P(('fine', 'coarse')), as said below
- coarse_basis: bfloat16 [32, 48, 1024], P(('fine', 'coarse')), may hold values from -0.4375 to 0.4375
- factor_blocks: float32 [32, 4, 48, 48], P(('fine', 'coarse')), may hold values from -0.4375 to 0.4375
- pattern: int32 [32, 4], P(('fine', 'coarse')), may hold values from 0 to 31
- partners: int32 [32, 6], P(('fine', 'coarse')), may hold values from 0 to 15, as said below
- row_counts: int32 [32, 8], P(('fine', 'coarse')), may hold values from 0 to 128, as said below
Outputs:
- multipliers: float32 [32, 16, 1024], P(('fine', 'coarse'))
- residual: float32 [32, 16, 1024], P(('fine', 'coarse'))
Inputs may be any that keep to these rules, and one draw needn't show every extreme that they name: Each layer gives each in-layer block index b its own odd distance d_b, the distances being 1, 3, up to 11 in some order: the subdomain at an even in-layer index i faces (i + d_b) modulo the number of in-layer indices, one at an odd index faces (i - d_b) modulo that number. So the partner of a subdomain's partner is itself, and a subdomain's 6 partners are distinct and differ from itself. `row_counts`: facing blocks have equal counts; blocks 6 of the first layer and 7 of the last layer are 0. `dual_ops`: each subdomain's matrix is symmetric positive definite.
All inputs are finite; a program needn't handle non-finite values.
Results may differ from a plain program's by a relative error of at most 0.0041.
Values may be sent and summed in bfloat16 or wider, within the bound.
No kernel may reach another device: no remote copies, remote signals or barrier semaphores. Data moves between devices by JAX's collectives and lax.ppermute only.
A program may use at most 64 MiB of HBM per device.

v0:
```python
import functools

import jax
import jax.numpy as jnp
from jax import lax
from jax.experimental import pallas as pl
from jax.experimental.pallas import tpu as pltpu
from jax.sharding import PartitionSpec as P

PLANES = 6
AXES = ("fine", "coarse")
LANES = 128
HALF = 64
BF16 = jnp.bfloat16
F32 = jnp.float32
GAMMA = 48
DELTA = 49


def lane_ids(rows):
    return lax.broadcasted_iota(jnp.int32, (rows, LANES), 1)


def dot(a, b):
    return lax.dot_general(a, b, (((1,), (0,)), ((), ())), preferred_element_type=F32)


def facing_subs(sizes, partners_ref):
    fine_count, coarse_count = sizes
    fine = lax.axis_index("fine")
    coarse = lax.axis_index("coarse")
    me = fine * coarse_count + coarse
    subs = [partners_ref[0, b] * coarse_count + coarse for b in range(PLANES)]
    subs.append(jnp.where(coarse > 0, me - 1, me))
    subs.append(jnp.where(coarse < coarse_count - 1, me + 1, me))
    return subs


def slot_of(sizes, partner):
    fine_count = sizes[0]
    fine = lax.axis_index("fine")
    ahead = jnp.where(fine % 2 == 0, partner - fine, fine - partner)
    ahead = jnp.where(ahead < 0, ahead + fine_count, ahead)
    return (ahead - 1) // 2


def live_mask(counts_ref, block):
    return (lane_ids(1) < counts_ref[0, block]).astype(F32)


def post_blocks(out_ref, targets, rows):
    cases = rows.shape[0]
    for block, target in enumerate(targets):
        out_ref[target, :cases, :] = rows[:, block * LANES : (block + 1) * LANES]


def fetch(pairs, sems):
    copies = [pltpu.make_async_copy(source, target, sems.at[i]) for i, (source, target) in enumerate(pairs)]
    for copy in copies:
        copy.start()
    return copies


def pack_kernel(sizes, layers, partners_ref, counts_ref, pattern_ref, loads_ref, basis_ref, factors_ref,
                partners_out, counts_out, loads_out, basis_out, *refs):
    outs, partners_smem, pattern_smem, factors_vmem, sems = refs[:-4], *refs[-4:]
    copies = fetch(
        [(partners_ref, partners_smem), (pattern_ref, pattern_smem), (loads_ref, loads_out), (basis_ref, basis_out),
         (factors_ref, factors_vmem), (partners_ref, partners_out), (counts_ref, counts_out)],
        sems,
    )
    for copy in copies:
        copy.wait()
    terms, modes = factors_vmem.shape[1:3]
    gap = jnp.zeros((modes, HALF - modes), F32)
    parts = []
    for term in range(terms):
        whole = factors_vmem[0, term]
        high = whole.astype(BF16).astype(F32)
        parts.append(jnp.concatenate([high, gap, whole - high, gap], axis=1))
    factors = jnp.concatenate(parts, axis=0).astype(BF16)
    row = lax.broadcasted_iota(jnp.int32, (16, LANES), 0)
    ids = jnp.zeros((16, LANES), F32)
    for term in range(terms):
        sub = pattern_smem[0, term]
        ids = jnp.where(row == term, (sub // 16).astype(F32), ids)
        ids = jnp.where(row == 8 + term, (sub % 16).astype(F32), ids)
    ids = ids.astype(BF16)
    slots = [slot_of(sizes, partners_smem[0, b]) for b in range(PLANES)]
    wanted = []
    for slot in range(PLANES):
        wanted.append(sum(jnp.where(slots[b] == slot, b, 0) for b in range(PLANES)))
    if layers == 1:
        wanted.append(jnp.where(lax.axis_index("coarse") == 0, PLANES + 1, PLANES))
    else:
        wanted += [PLANES, PLANES + 1]
    places = layout_of(terms, modes)
    for out_ref, block in zip(outs, wanted):
        out_ref[places["factors"], :] = factors
        out_ref[places["ids"], :] = ids
        start = block * LANES
        if not isinstance(start, int):
            start = pl.multiple_of(start, LANES)
        out_ref[places["basis"], :] = basis_out[0, :, pl.ds(start, LANES)]
        out_ref[places["loads"], :] = loads_out[0, :, pl.ds(start, LANES)]


def layout_of(terms, modes):
    sizes = (("factors", terms * modes), ("basis", modes), ("ids", 16), ("loads", 16))
    places, start = {}, 0
    for name, rows in sizes:
        places[name] = slice(start, start + rows)
        start += rows
    return places


def dual_kernel(dual_ref, after_ref, out_ref, sems):
    for copy in fetch([(dual_ref, out_ref)], sems):
        copy.wait()


def difference(counts_ref, mine, facing):
    result, ours, theirs = [], [], []
    for block, other in enumerate(facing):
        mask = live_mask(counts_ref, block)
        left = mine[:, block * LANES : (block + 1) * LANES].astype(F32) * mask
        right = other.astype(F32) * mask
        result.append(left - right)
        ours.append(left.astype(BF16))
        theirs.append(right.astype(BF16))
    return result, ours, theirs


def first_restrict_kernel(sizes, dims, layers, partners_ref, counts_ref, loads_ref, basis_ref, *refs):
    near_refs, (out_ref, message_ref, scratch_ref) = refs[: PLANES + layers], refs[-3:]
    span = layout_of(*dims)["loads"]
    for slot in range(PLANES):
        scratch_ref[slot] = near_refs[slot][span, :]
    facing = [scratch_ref[slot_of(sizes, partners_ref[0, b])] for b in range(PLANES)]
    facing += [near_refs[PLANES][span, :], near_refs[-1][span, :]]
    restrict(counts_ref, loads_ref[0], facing, basis_ref, None, out_ref, message_ref)


def restrict_kernel(sizes, partners_ref, counts_ref, mine_ref, basis_ref, sums_ref, arrived_ref, out_ref, message_ref):
    facing = [arrived_ref[target] for target in facing_subs(sizes, partners_ref)]
    restrict(counts_ref, mine_ref[...], facing, basis_ref, sums_ref, out_ref, message_ref)


def restrict(counts_ref, mine, facing, basis_ref, sums_ref, out_ref, message_ref):
    modes = basis_ref.shape[1]
    cases = mine.shape[0]
    result, ours, theirs = difference(counts_ref, mine, facing)
    for block, values in enumerate(result):
        out_ref[:, block * LANES : (block + 1) * LANES] = values
    both = jnp.concatenate([jnp.concatenate(ours, axis=1), jnp.concatenate(theirs, axis=1)], axis=0)
    basis = basis_ref[0]
    gap = jnp.zeros((HALF - modes, basis.shape[1]), BF16)
    twice = jnp.concatenate([basis, gap, basis, gap], axis=0)
    coefficients = lax.dot_general(both, twice, (((1,), (1,)), ((), ())), preferred_element_type=F32)
    coefficients = coefficients[:cases] - coefficients[cases:]
    half = cases // 2
    message = jnp.where(lane_ids(half) < HALF, coefficients[:half], coefficients[half:])
    if sums_ref is not None:
        message = message + sums_ref[...]
    message_ref[...] = jnp.broadcast_to(message[None], message_ref.shape)


def solve(coeffs, near, terms, modes):
    half = 8
    places = layout_of(terms, modes)
    high = coeffs.astype(BF16)
    low = (coeffs - high.astype(F32)).astype(BF16)
    table = jnp.concatenate([high, low], axis=1)
    chunks = coeffs.shape[0] // LANES
    lanes = lane_ids(half).astype(F32)
    step = lax.broadcasted_iota(jnp.int32, (half, LANES), 0).astype(F32)
    picks = []
    for packed in near:
        ids = packed[places["ids"], :].astype(F32)
        ids = (ids[:8] * 16.0 + ids[8:]) * float(half)
        for term in range(terms):
            target = ids[term : term + 1] + step
            picks.append(
                jnp.concatenate([(target == lanes + float(LANES * c)).astype(F32) for c in range(chunks)], axis=1)
            )
    picks = jnp.concatenate(picks, axis=0).astype(BF16)
    picked = dot(picks, table)
    left = lane_ids(half) < HALF
    gap = jnp.zeros((HALF - modes, LANES), BF16)
    solutions = []
    for index, packed in enumerate(near):
        sides = []
        for part in range(2):
            columns = []
            for pair in range(0, terms, 2):
                first, second = [
                    picked[(index * terms + term) * half : (index * terms + term + 1) * half, part * LANES : (part + 1) * LANES]
                    for term in (pair, pair + 1)
                ]
                top = jnp.where(left, first, pltpu.roll(second, HALF, 1))
                bottom = jnp.where(left, pltpu.roll(first, HALF, 1), second)
                columns.append(jnp.concatenate([top, bottom], axis=0))
            sides.append(jnp.concatenate(columns, axis=1))
        rows = jnp.concatenate(sides, axis=0).astype(BF16)
        factors = []
        for term in range(terms):
            factors += [packed[term * modes : (term + 1) * modes, :], gap]
        product = dot(rows, jnp.concatenate(factors, axis=0))
        product = product[: 2 * half] + product[2 * half :]
        product = product + pltpu.roll(product, HALF, 1)
        solutions.append(product[:, :modes].astype(BF16))
    return solutions


def advance(sizes, dims, partners_ref, counts_ref, coeffs, residual, near_refs, basis_ref, dual_ref, theirs_ref,
            direction_ref, applied_ref):
    terms, modes = dims
    span = layout_of(terms, modes)["basis"]
    near = [ref[...] for ref in near_refs]
    solutions = solve(coeffs, near, terms, modes)
    mine = dot(solutions[0], basis_ref[0]).astype(BF16).astype(F32)
    for index, packed in enumerate(near[1:]):
        theirs_ref[index] = dot(solutions[index + 1], packed[span, :]).astype(BF16).astype(F32)
    pieces = []
    for block in range(PLANES + 2):
        if block < PLANES:
            place = slot_of(sizes, partners_ref[0, block])
        else:
            place = min(block, len(near) - 2)
        here = slice(block * LANES, (block + 1) * LANES)
        pieces.append(residual[:, here] + live_mask(counts_ref, block) * (mine[:, here] - theirs_ref[place]))
    direction = jnp.concatenate(pieces, axis=1)
    direction_ref[...] = direction
    applied = dot(direction.astype(BF16), dual_ref[0]).astype(BF16)
    applied_ref[...] = applied
    gamma = jnp.sum(residual * direction, axis=1, keepdims=True)
    delta = 2.0 * jnp.sum(direction * applied.astype(F32), axis=1, keepdims=True)
    half = gamma.shape[0] // 2
    lanes = lane_ids(half)
    sums = jnp.zeros((half, LANES), F32)
    for lane, values in ((GAMMA, gamma), (DELTA, delta)):
        sums = jnp.where(lanes == lane, values[:half], sums)
        sums = jnp.where(lanes == HALF + lane, values[half:], sums)
    return applied, sums


def first_kernel(sizes, dims, count, partners_ref, counts_ref, coeffs_ref, residual_ref, basis_ref, dual_ref, *refs):
    near_refs = refs[:count]
    message_ref, direction_ref, applied_ref, sums_ref, theirs_ref = refs[count:]
    applied, sums = advance(
        sizes, dims, partners_ref, counts_ref, coeffs_ref[...], residual_ref[...], near_refs, basis_ref, dual_ref,
        theirs_ref, direction_ref, applied_ref,
    )
    message_ref[...] = jnp.zeros_like(message_ref)
    post_blocks(message_ref, facing_subs(sizes, partners_ref), applied)
    sums_ref[...] = sums


def steps_from(totals):
    low = totals[:, GAMMA : GAMMA + 1] / totals[:, DELTA : DELTA + 1]
    high = totals[:, HALF + GAMMA : HALF + GAMMA + 1] / totals[:, HALF + DELTA : HALF + DELTA + 1]
    return low, high


def second_kernel(sizes, dims, count, partners_ref, counts_ref, coeffs_ref, change_ref, residual_ref, image_ref,
                  before_ref, basis_ref, dual_ref, *refs):
    near_refs = refs[:count]
    message_ref, residual_out, multipliers_out, direction_ref, applied_ref, theirs_ref = refs[count:]
    half = residual_ref.shape[0] // 2
    change = change_ref[...].reshape(-1, half, LANES)
    low, high = steps_from(jnp.sum(change, axis=0))
    step = jnp.concatenate([low, high], axis=0)
    packed_step = jnp.where(lane_ids(half) < HALF, low, high)
    coeffs = coeffs_ref[...] - (change * packed_step[None]).reshape(coeffs_ref.shape)
    residual = residual_ref[...] - step * image_ref[...]
    residual_out[...] = residual
    multipliers_out[...] = step * before_ref[...]
    applied, sums = advance(
        sizes, dims, partners_ref, counts_ref, coeffs, residual, near_refs, basis_ref, dual_ref, theirs_ref,
        direction_ref, applied_ref,
    )
    top = sums.astype(BF16).astype(F32)
    middle = (sums - top).astype(BF16).astype(F32)
    bottom = sums - top - middle
    coded = (top + pltpu.roll(middle, 2, 1) + pltpu.roll(bottom, 4, 1)).astype(BF16)
    cases = applied.shape[0]
    message_ref[:, :cases, :] = jnp.zeros((message_ref.shape[0], cases, LANES), BF16)
    message_ref[:, cases:, :] = jnp.broadcast_to(coded[None], (message_ref.shape[0], half, LANES))
    post_blocks(message_ref, facing_subs(sizes, partners_ref), applied)


def last_kernel(sizes, partners_ref, counts_ref, arrived_ref, applied_ref, residual_ref, multipliers_ref, direction_ref,
                multipliers_out, residual_out):
    cases = applied_ref.shape[0]
    totals = jnp.sum(arrived_ref[:, cases:, :].astype(F32), axis=0)
    totals = totals + pltpu.roll(totals, LANES - 2, 1) + pltpu.roll(totals, LANES - 4, 1)
    step = jnp.concatenate(steps_from(totals), axis=0)
    facing = [arrived_ref[target, :cases, :] for target in facing_subs(sizes, partners_ref)]
    image, _, _ = difference(counts_ref, applied_ref[...], facing)
    fine = lax.axis_index("fine")
    for block in range(PLANES + 2):
        span = slice(block * LANES, (block + 1) * LANES)
        if block < PLANES:
            sign = jnp.where(fine < partners_ref[0, block], 1.0, -1.0).astype(F32)
        else:
            sign = -1.0 if block == PLANES else 1.0
        multipliers_out[0, :, span] = sign * (multipliers_ref[:, span] + step * direction_ref[:, span])
        residual_out[0, :, span] = sign * (residual_ref[:, span] - step * image[block])


SMEM = pl.BlockSpec(memory_space=pltpu.SMEM)
VMEM = pl.BlockSpec(memory_space=pltpu.VMEM)


HBM = pl.BlockSpec(memory_space=pltpu.HBM)
ANY = pl.BlockSpec(memory_space=pl.ANY)


def call(kernel, name, scalars, arrays, outs, scratch=(), far=(), after=()):
    return pl.pallas_call(
        kernel,
        name=name,
        out_shape=[jax.ShapeDtypeStruct(shape, dtype) for shape, dtype in outs],
        in_specs=[SMEM] * len(scalars) + [VMEM] * len(arrays) + [HBM] * len(far) + [ANY] * len(after),
        out_specs=[VMEM] * len(outs),
        scratch_shapes=list(scratch),
        compiler_params=pltpu.CompilerParams(vmem_limit_bytes=40 * 1024 * 1024),
    )(*scalars, *arrays, *far, *after)


def body(load_cases, dual_ops, coarse_basis, factor_blocks, pattern, partners, row_counts):
    cases, width = load_cases.shape[1:]
    terms, modes = factor_blocks.shape[1:3]
    fine_count = lax.axis_size("fine")
    coarse_count = lax.axis_size("coarse")
    subs = fine_count * coarse_count
    sizes = (fine_count, coarse_count)
    dims = (terms, modes)
    half = cases // 2
    layers = 1 if coarse_count == 2 else 2

    def swap_all(message):
        return lax.all_to_all(message, AXES, 0, 0, tiled=True)

    def swap_layers(messages):
        if layers == 1:
            return [lax.ppermute(messages[0], "coarse", [(0, 1), (1, 0)])]
        up = [(i, i + 1) for i in range(coarse_count - 1)]
        return [lax.ppermute(messages[1], "coarse", up), lax.ppermute(messages[0], "coarse", [(j, i) for i, j in up])]

    def swap_slot(packed, slot):
        distance = 2 * slot + 1
        pairs = [(i, (i + distance if i % 2 == 0 else i - distance) % fine_count) for i in range(fine_count)]
        return lax.ppermute(packed, "fine", pairs)

    rows = ((cases, width), F32)
    half_rows = ((cases, width), BF16)
    coded = ((subs, half, LANES), F32)
    dma = pltpu.SemaphoreType.DMA

    message_rows = layout_of(terms, modes)["loads"].stop
    partners, row_counts, loads, basis, *packed = call(
        functools.partial(pack_kernel, sizes, layers),
        "pack_setup",
        (),
        (),
        [(partners.shape, jnp.int32), (row_counts.shape, jnp.int32), (load_cases.shape, BF16), (coarse_basis.shape, BF16)]
        + [((message_rows, LANES), BF16)] * (PLANES + layers),
        [pltpu.SMEM(partners.shape, jnp.int32), pltpu.SMEM(pattern.shape, jnp.int32),
         pltpu.VMEM(factor_blocks.shape, F32), dma((7,))],
        (partners, row_counts, pattern, load_cases, coarse_basis, factor_blocks),
    )
    received = [swap_slot(packed[slot], slot) for slot in range(PLANES)] + swap_layers(packed[PLANES:])
    near = [packed[-1]] + received
    count = len(near)
    theirs = [pltpu.VMEM((count - 1, cases, LANES), F32)]

    scalars = (partners, row_counts)
    residual, message = call(
        functools.partial(first_restrict_kernel, sizes, dims, layers),
        "restrict_residual",
        scalars,
        (loads, basis, *received),
        [rows, coded],
        [pltpu.VMEM((PLANES, cases, LANES), BF16)],
    )
    coeffs = swap_all(message).reshape(subs * half, LANES)
    [dual] = call(dual_kernel, "fetch_dual", (), (), [(dual_ops.shape, BF16)], [dma((1,))], (dual_ops,), (residual,))

    message, direction, applied, sums = call(
        functools.partial(first_kernel, sizes, dims, count),
        "first_direction",
        scalars,
        (coeffs, residual, basis, dual, *near),
        [((subs, cases, LANES), BF16), rows, half_rows, ((half, LANES), F32)],
        theirs,
    )
    arrived = swap_all(message)
    image, message = call(
        functools.partial(restrict_kernel, sizes),
        "restrict_image",
        scalars,
        (applied, basis, sums, arrived),
        [rows, coded],
    )
    change = swap_all(message).reshape(subs * half, LANES)

    message, residual, multipliers, direction, applied = call(
        functools.partial(second_kernel, sizes, dims, count),
        "second_direction",
        scalars,
        (coeffs, change, residual, image, direction, basis, dual, *near),
        [((subs, cases + half, LANES), BF16), rows, rows, rows, half_rows],
        theirs,
    )
    arrived = swap_all(message)
    out = ((1, cases, width), F32)
    multipliers, residual = call(
        functools.partial(last_kernel, sizes),
        "finish",
        scalars,
        (arrived, applied, residual, multipliers, direction),
        [out, out],
    )
    return multipliers, residual


def solution(mesh):
    rows = P(AXES, None, None)
    return jax.shard_map(
        body,
        mesh=mesh,
        in_specs=(rows, rows, rows, P(AXES, None, None, None), P(AXES, None), P(AXES, None), P(AXES, None)),
        out_specs=(rows, rows),
        check_vma=False,
    )
```

profile of v0, /device:TPU:1, one launch (start us, length us, event | category | flops | bytes accessed | tf_op | source)
XLA Modules:
  0.0 76.0 jit_solution(6922999948965342155)
XLA Ops:
  0.6 0.0 copy-start.1
  0.6 0.9 %copy-done.1 = bf16[1,48,1024]{2,1,0:T(8,128)(2,1)S(1)} copy-done((bf16[1,48,1024]{2,1,0:T(8,128)(2,1)S(1)}, bf16[1,48,1024]{2,1,0:T(8,128)(2,1)}, u32[]{:S(2)}) %copy-start.1) | copy-done | bytes 98328
  1.5 0.0 copy-start.2
  1.5 0.9 %copy-done.2 = f32[1,4,48,48]{3,2,1,0:T(8,128)S(1)} copy-done((f32[1,4,48,48]{3,2,1,0:T(8,128)S(1)}, f32[1,4,48,48]{3,2,1,0:T(8,128)}, u32[]{:S(2)}) %copy-start.2) | copy-done | bytes 36888
  2.4 0.0 copy-start.3
  2.4 0.8 copy-done.3
  3.2 0.0 copy-start.4
  3.2 0.7 copy-done.4
  3.8 0.0 copy-start.5
  3.8 0.7 copy-done.5
  4.5 0.0 copy-start.6
  4.5 0.7 copy-done.6
  5.1 0.7 pack_setup.1
  5.9 2.1 %collective-permute-start = (bf16[272,128]{1,0:T(8,128)(2,1)S(1)}, bf16[272,128]{1,0:T(8,128)(2,1)S(1)}, u32[]{:S(2)}, u32[]{:S(2)}) collective-permute-start(bf16[272,128]{1,0:T(8,128)(2,1)S(1)} %get-tuple-element.30), channel_id=1, source_target_pairs={{0,2},{2,0},{4,6},{6,4},{8,10},{10,8},{12,14},{14,12},{16,18},{18,... | collective-permute-start | bytes 208904 | tf_op jit(solution)/shard_map/ppermute | solution.py:354
  8.0 1.2 %collective-permute-start.1 = (bf16[272,128]{1,0:T(8,128)(2,1)S(1)}, bf16[272,128]{1,0:T(8,128)(2,1)S(1)}, u32[]{:S(2)}, u32[]{:S(2)}) collective-permute-start(bf16[272,128]{1,0:T(8,128)(2,1)S(1)} %get-tuple-element.31), channel_id=1, source_target_pairs={{0,6},{2,28},{4,10},{6,0},{8,14},{10,4},{12,18},{14,8},{16,22},{18... | collective-permute-start | bytes 208904 | tf_op jit(solution)/shard_map/ppermute | solution.py:354
  9.2 2.1 %collective-permute-start.2 = (bf16[272,128]{1,0:T(8,128)(2,1)S(1)}, bf16[272,128]{1,0:T(8,128)(2,1)S(1)}, u32[]{:S(2)}, u32[]{:S(2)}) collective-permute-start(bf16[272,128]{1,0:T(8,128)(2,1)S(1)} %get-tuple-element.32), channel_id=1, source_target_pairs={{0,10},{2,24},{4,14},{6,28},{8,18},{10,0},{12,22},{14,4},{16,26},{... | collective-permute-start | bytes 208904 | tf_op jit(solution)/shard_map/ppermute | solution.py:354
  11.3 1.2 %collective-permute-start.3 = (bf16[272,128]{1,0:T(8,128)(2,1)S(1)}, bf16[272,128]{1,0:T(8,128)(2,1)S(1)}, u32[]{:S(2)}, u32[]{:S(2)}) collective-permute-start(bf16[272,128]{1,0:T(8,128)(2,1)S(1)} %get-tuple-element.33), channel_id=1, source_target_pairs={{0,14},{2,20},{4,18},{6,24},{8,22},{10,28},{12,26},{14,0},{16,30},... | collective-permute-start | bytes 208904 | tf_op jit(solution)/shard_map/ppermute | solution.py:354
  12.5 2.1 %collective-permute-start.4 = (bf16[272,128]{1,0:T(8,128)(2,1)S(1)}, bf16[272,128]{1,0:T(8,128)(2,1)S(1)}, u32[]{:S(2)}, u32[]{:S(2)}) collective-permute-start(bf16[272,128]{1,0:T(8,128)(2,1)S(1)} %get-tuple-element.34), channel_id=1, source_target_pairs={{0,18},{2,16},{4,22},{6,20},{8,26},{10,24},{12,30},{14,28},{16,2},... | collective-permute-start | bytes 208904 | tf_op jit(solution)/shard_map/ppermute | solution.py:354
  14.6 0.0 collective-permute-done.refs_0_.refs_1_
  14.6 2.1 %collective-permute-start.5 = (bf16[272,128]{1,0:T(8,128)(2,1)S(1)}, bf16[272,128]{1,0:T(8,128)(2,1)S(1)}, u32[]{:S(2)}, u32[]{:S(2)}) collective-permute-start(bf16[272,128]{1,0:T(8,128)(2,1)S(1)} %get-tuple-element.35), channel_id=1, source_target_pairs={{0,22},{2,12},{4,26},{6,16},{8,30},{10,20},{12,2},{14,24},{16,6},{... | collective-permute-start | bytes 208904 | tf_op jit(solution)/shard_map/ppermute | solution.py:354
  16.8 0.0 collective-permute-done.1.refs_1_.refs_2_
  16.8 2.4 %collective-permute-start.6 = (bf16[272,128]{1,0:T(8,128)(2,1)S(1)}, bf16[272,128]{1,0:T(8,128)(2,1)S(1)}, u32[]{:S(2)}, u32[]{:S(2)}) collective-permute-start(bf16[272,128]{1,0:T(8,128)(2,1)S(1)} %get-tuple-element.36.refs_0_), channel_id=1, source_target_pairs={{0,1},{1,0},{2,3},{3,2},{4,5},{5,4},{6,7},{7,6},{8,9},{9,8},{10,11... | collective-permute-start | bytes 208904 | tf_op jit(solution)/shard_map/ppermute | solution.py:347
  19.1 0.0 collective-permute-done.2.refs_2_.refs_3_
  19.1 0.0 collective-permute-done.3.refs_3_.refs_4_
  19.1 3.0 %collective-permute-done.4.refs_4_.refs_5_ = bf16[272,128]{1,0:T(8,128)(2,1)S(1)} collective-permute-done((bf16[272,128]{1,0:T(8,128)(2,1)S(1)}, bf16[272,128]{1,0:T(8,128)(2,1)S(1)}, u32[]{:S(2)}, u32[]{:S(2)}) %collective-permute-start.4) | collective-permute-done | bytes 69664 | tf_op jit(solution)/shard_map/ppermute | solution.py:354
  22.1 0.7 collective-permute-done.5.refs_5_.refs_6_
  22.8 0.0 collective-permute-done.6.refs_6_.refs_7_
  22.8 1.4 %restrict_residual.1 = (f32[16,1024]{1,0:T(8,128)S(1)}, f32[32,8,128]{2,1,0:T(8,128)}) custom-call(s32[1,6]{1,0:T(1,128)S(1)} %get-tuple-element.26.partners_ref, s32[1,8]{1,0:T(1,128)S(1)} %get-tuple-element.27.counts_ref, bf16[1,16,1024]{2,1,0:T(8,128)(2,1)S(1)} %get-tuple-element.28.loads_ref, bf16[1,48,1024]{2,1,0:T(8,128)(2,1)S(1)} %get-tuple-element.29.basis_ref, ...), custom_call_target="tpu_custom_call" | custom-call | tf_op jit(solution)/shard_map/restrict_residual/pallas_call | solution.py:320
  24.2 6.7 %all-to-all-start = ((f32[32,8,128]{2,1,0:T(8,128)}), f32[32,8,128]{2,1,0:T(8,128)S(1)}, u32[]{:S(2)}, u32[]{:S(2)}) async-start(f32[32,8,128]{2,1,0:T(8,128)} %get-tuple-element.37), calls=%async_computation | async-start | bytes 262144 | tf_op jit(solution)/shard_map/all_to_all | solution.py:343
  30.9 0.0 copy-start
  30.9 1.6 %copy-done = bf16[1,1024,1024]{2,1,0:T(8,128)(2,1)S(1)} copy-done((bf16[1,1024,1024]{2,1,0:T(8,128)(2,1)S(1)}, bf16[1,1024,1024]{2,1,0:T(8,128)(2,1)}, u32[]{:S(2)}) %copy-start) | copy-done | bytes 2097176
  32.5 0.1 fetch_dual.1.dual_ref
  32.6 6.4 %all-to-all-done = f32[32,8,128]{2,1,0:T(8,128)S(1)} async-done(((f32[32,8,128]{2,1,0:T(8,128)}), f32[32,8,128]{2,1,0:T(8,128)S(1)}, u32[]{:S(2)}, u32[]{:S(2)}) %all-to-all-start) | async-done | bytes 131104 | tf_op jit(solution)/shard_map/all_to_all | solution.py:343
  39.1 1.7 %first_direction.1 = (bf16[32,16,128]{2,1,0:T(8,128)(2,1)S(1)}, f32[16,1024]{1,0:T(8,128)S(1)}, bf16[16,1024]{1,0:T(8,128)(2,1)S(1)}, f32[8,128]{1,0:T(8,128)S(1)}) custom-call(s32[1,6]{1,0:T(1,128)S(1)} %get-tuple-element.26.partners_ref, s32[1,8]{1,0:T(1,128)S(1)} %get-tuple-element.27.counts_ref, f32[256,128]{1,0:T(8,128)S(1)} %bitcast.2, ...), custom_call_target="tpu_custom_call" | custom-call | tf_op jit(solution)/shard_map/first_direction/pallas_call | solution.py:320
  40.8 10.0 %all_to_all.20.arrived_ref = bf16[32,16,128]{2,1,0:T(8,128)(2,1)S(1)} all-to-all(bf16[32,16,128]{2,1,0:T(8,128)(2,1)S(1)} %get-tuple-element.41), channel_id=1, replica_groups=mesh['fine'=16,'coarse'=2] {'fine','coarse'}, dimensions={0} | all-to-all | bytes 262144 | tf_op jit(solution)/shard_map/all_to_all | solution.py:343
  50.8 0.7 restrict_image.1
  51.5 10.0 %all_to_all.21 = f32[32,8,128]{2,1,0:T(8,128)S(1)} all-to-all(f32[32,8,128]{2,1,0:T(8,128)S(1)} %get-tuple-element.42), channel_id=1, replica_groups=mesh['fine'=16,'coarse'=2] {'fine','coarse'}, dimensions={0} | all-to-all | bytes 262144 | tf_op jit(solution)/shard_map/all_to_all | solution.py:343
  61.5 1.9 %second_direction.1 = (bf16[32,24,128]{2,1,0:T(8,128)(2,1)S(1)}, f32[16,1024]{1,0:T(8,128)S(1)}, f32[16,1024]{1,0:T(8,128)S(1)}, f32[16,1024]{1,0:T(8,128)S(1)}, bf16[16,1024]{1,0:T(8,128)(2,1)S(1)}) custom-call(s32[1,6]{1,0:T(1,128)S(1)} %get-tuple-element.26.partners_ref, s32[1,8]{1,0:T(1,128)S(1)} %get-tuple-element.27.counts_ref, ...), custom_call_target="tpu_custom_call" | custom-call | tf_op jit(solution)/shard_map/second_direction/pallas_call | solution.py:320
  63.5 11.0 %all_to_all.22.arrived_ref = bf16[32,24,128]{2,1,0:T(8,128)(2,1)S(1)} all-to-all(bf16[32,24,128]{2,1,0:T(8,128)(2,1)S(1)} %get-tuple-element.45), channel_id=1, replica_groups=mesh['fine'=16,'coarse'=2] {'fine','coarse'}, dimensions={0} | all-to-all | bytes 393216 | tf_op jit(solution)/shard_map/all_to_all | solution.py:343
  74.5 1.5 %finish.1 = (f32[1,16,1024]{2,1,0:T(8,128)}, f32[1,16,1024]{2,1,0:T(8,128)}) custom-call(s32[1,6]{1,0:T(1,128)S(1)} %get-tuple-element.26.partners_ref, s32[1,8]{1,0:T(1,128)S(1)} %get-tuple-element.27.counts_ref, bf16[32,24,128]{2,1,0:T(8,128)(2,1)S(1)} %all_to_all.22.arrived_ref, bf16[16,1024]{1,0:T(8,128)(2,1)S(1)} %get-tuple-element.46.applied_ref, ...), custom_call_target="tpu_custom_call" | custom-call | tf_op jit(solution)/shard_map/finish/pallas_call | solution.py:320
Async XLA Ops:
  0.6 0.9 %copy-start.1 = (bf16[1,48,1024]{2,1,0:T(8,128)(2,1)S(1)}, bf16[1,48,1024]{2,1,0:T(8,128)(2,1)}, u32[]{:S(2)}) copy-start(bf16[1,48,1024]{2,1,0:T(8,128)(2,1)} %basis_ref.1) | copy-start | bytes 294916
  1.5 0.9 %copy-start.2 = (f32[1,4,48,48]{3,2,1,0:T(8,128)S(1)}, f32[1,4,48,48]{3,2,1,0:T(8,128)}, u32[]{:S(2)}) copy-start(f32[1,4,48,48]{3,2,1,0:T(8,128)} %factors_ref.1) | copy-start | bytes 110596
  2.4 0.8 copy-start.3
  3.2 0.7 copy-start.4
  3.8 0.7 copy-start.5
  4.5 0.7 copy-start.6
  5.9 8.8 %collective-permute-start = (bf16[272,128]{1,0:T(8,128)(2,1)S(1)}, bf16[272,128]{1,0:T(8,128)(2,1)S(1)}, u32[]{:S(2)}, u32[]{:S(2)}) collective-permute-start(bf16[272,128]{1,0:T(8,128)(2,1)S(1)} %get-tuple-element.30), channel_id=1, source_target_pairs={{0,2},{2,0},{4,6},{6,4},{8,10},{10,8},{12,14},{14,12},{16,18},{18,... | collective-permute-start | bytes 208904 | tf_op jit(solution)/shard_map/ppermute | solution.py:354
  8.0 8.8 %collective-permute-start.1 = (bf16[272,128]{1,0:T(8,128)(2,1)S(1)}, bf16[272,128]{1,0:T(8,128)(2,1)S(1)}, u32[]{:S(2)}, u32[]{:S(2)}) collective-permute-start(bf16[272,128]{1,0:T(8,128)(2,1)S(1)} %get-tuple-element.31), channel_id=1, source_target_pairs={{0,6},{2,28},{4,10},{6,0},{8,14},{10,4},{12,18},{14,8},{16,22},{18... | collective-permute-start | bytes 208904 | tf_op jit(solution)/shard_map/ppermute | solution.py:354
  9.2 9.9 %collective-permute-start.2 = (bf16[272,128]{1,0:T(8,128)(2,1)S(1)}, bf16[272,128]{1,0:T(8,128)(2,1)S(1)}, u32[]{:S(2)}, u32[]{:S(2)}) collective-permute-start(bf16[272,128]{1,0:T(8,128)(2,1)S(1)} %get-tuple-element.32), channel_id=1, source_target_pairs={{0,10},{2,24},{4,14},{6,28},{8,18},{10,0},{12,22},{14,4},{16,26},{... | collective-permute-start | bytes 208904 | tf_op jit(solution)/shard_map/ppermute | solution.py:354
  11.3 7.8 %collective-permute-start.3 = (bf16[272,128]{1,0:T(8,128)(2,1)S(1)}, bf16[272,128]{1,0:T(8,128)(2,1)S(1)}, u32[]{:S(2)}, u32[]{:S(2)}) collective-permute-start(bf16[272,128]{1,0:T(8,128)(2,1)S(1)} %get-tuple-element.33), channel_id=1, source_target_pairs={{0,14},{2,20},{4,18},{6,24},{8,22},{10,28},{12,26},{14,0},{16,30},... | collective-permute-start | bytes 208904 | tf_op jit(solution)/shard_map/ppermute | solution.py:354
  12.5 9.6 %collective-permute-start.4 = (bf16[272,128]{1,0:T(8,128)(2,1)S(1)}, bf16[272,128]{1,0:T(8,128)(2,1)S(1)}, u32[]{:S(2)}, u32[]{:S(2)}) collective-permute-start(bf16[272,128]{1,0:T(8,128)(2,1)S(1)} %get-tuple-element.34), channel_id=1, source_target_pairs={{0,18},{2,16},{4,22},{6,20},{8,26},{10,24},{12,30},{14,28},{16,2},... | collective-permute-start | bytes 208904 | tf_op jit(solution)/shard_map/ppermute | solution.py:354
  14.6 8.1 %collective-permute-start.5 = (bf16[272,128]{1,0:T(8,128)(2,1)S(1)}, bf16[272,128]{1,0:T(8,128)(2,1)S(1)}, u32[]{:S(2)}, u32[]{:S(2)}) collective-permute-start(bf16[272,128]{1,0:T(8,128)(2,1)S(1)} %get-tuple-element.35), channel_id=1, source_target_pairs={{0,22},{2,12},{4,26},{6,16},{8,30},{10,20},{12,2},{14,24},{16,6},{... | collective-permute-start | bytes 208904 | tf_op jit(solution)/shard_map/ppermute | solution.py:354
  16.8 6.0 %collective-permute-start.6 = (bf16[272,128]{1,0:T(8,128)(2,1)S(1)}, bf16[272,128]{1,0:T(8,128)(2,1)S(1)}, u32[]{:S(2)}, u32[]{:S(2)}) collective-permute-start(bf16[272,128]{1,0:T(8,128)(2,1)S(1)} %get-tuple-element.36.refs_0_), channel_id=1, source_target_pairs={{0,1},{1,0},{2,3},{3,2},{4,5},{5,4},{6,7},{7,6},{8,9},{9,8},{10,11... | collective-permute-start | bytes 208904 | tf_op jit(solution)/shard_map/ppermute | solution.py:347
  24.2 14.9 %all-to-all-start = ((f32[32,8,128]{2,1,0:T(8,128)}), f32[32,8,128]{2,1,0:T(8,128)S(1)}, u32[]{:S(2)}, u32[]{:S(2)}) async-start(f32[32,8,128]{2,1,0:T(8,128)} %get-tuple-element.37), calls=%async_computation | async-start | bytes 262144 | tf_op jit(solution)/shard_map/all_to_all | solution.py:343
  30.9 1.6 %copy-start = (bf16[1,1024,1024]{2,1,0:T(8,128)(2,1)S(1)}, bf16[1,1024,1024]{2,1,0:T(8,128)(2,1)}, u32[]{:S(2)}) copy-start(bf16[1,1024,1024]{2,1,0:T(8,128)(2,1)} %dual_ref.1) | copy-start | bytes 6291460
where the time goes:
time: 76.4 us; the launch traced here: 76 us
  blocking collectives  31 us (41%)
  starting transfers between devices  19.9 us (26%)
  waiting for transfers between devices  10.1 us (13%)
  Pallas kernels  8.14 us (11%)
  local copies, waits for them, and re-layouts  6.09 us (8%)
    all_to_all x3, blocking collectives, swap_all(): return lax.all_to_all(message, AXES, 0, 0, tiled=True)  31 us
    ppermute x6, starting transfers between devices, swap_slot(): return lax.ppermute(packed, 'fine', pairs)  10.9 us
    pallas_call x7, Pallas kernels, call(): pl.pallas_call(kernel, name=name, out_shape=[jax.ShapeDtypeStruct(shape,...  8.14 us
    all_to_all x1, starting transfers between devices, swap_all(): return lax.all_to_all(message, AXES, 0, 0, tiled=True)  6.73 us
    all_to_all x1, waiting for transfers between devices, swap_all(): return lax.all_to_all(message, AXES, 0, 0, tiled=True)  6.44 us
    unnamed x14, local copies, waits for them, and re-layouts  6.09 us
    ppermute x6, waiting for transfers between devices, swap_slot(): return lax.ppermute(packed, 'fine', pairs)  3.66 us
    ppermute x1, starting transfers between devices, swap_layers(): return [lax.ppermute(messages[0], 'coarse', [(0, 1), (1, 0)])]  2.36 us
  transfers between devices with their start and end apart: 8, of which 3 were waited for; matrix products, arithmetic and copies ran while one was open for 0% of the time, Pallas kernels for 0%

commit v1 on v0

--- a/solution.py
+++ b/solution.py
@@ -23,6 +23,21 @@
 
 def dot(a, b):
     return lax.dot_general(a, b, (((1,), (0,)), ((), ())), preferred_element_type=F32)
+
+
+def wanted_blocks(sizes, layers, meta_ref):
+    slots = [slot_of(sizes, meta_ref[0, b]) for b in range(PLANES)]
+    blocks = []
+    for slot in range(PLANES):
+        blocks.append(sum(jnp.where(slots[b] == slot, b, 0) for b in range(PLANES)))
+    if layers == 1:
+        return blocks + [jnp.where(lax.axis_index("coarse") == 0, PLANES + 1, PLANES)]
+    return blocks + [PLANES, PLANES + 1]
+
+
+def lanes_of(block):
+    start = block * LANES
+    return pl.ds(start if isinstance(start, int) else pl.multiple_of(start, LANES), LANES)
 
 
 def facing_subs(sizes, partners_ref):
@@ -45,7 +60,7 @@
 
 
 def live_mask(counts_ref, block):
-    return (lane_ids(1) < counts_ref[0, block]).astype(F32)
+    return (lane_ids(1) < counts_ref[0, PLANES + block]).astype(F32)
 
 
 def post_blocks(out_ref, targets, rows):
@@ -61,48 +76,28 @@
     return copies
 
 
-def pack_kernel(sizes, layers, partners_ref, counts_ref, pattern_ref, loads_ref, basis_ref, factors_ref,
-                partners_out, counts_out, loads_out, basis_out, *refs):
-    outs, partners_smem, pattern_smem, factors_vmem, sems = refs[:-4], *refs[-4:]
-    copies = fetch(
-        [(partners_ref, partners_smem), (pattern_ref, pattern_smem), (loads_ref, loads_out), (basis_ref, basis_out),
-         (factors_ref, factors_vmem), (partners_ref, partners_out), (counts_ref, counts_out)],
-        sems,
-    )
-    for copy in copies:
-        copy.wait()
-    terms, modes = factors_vmem.shape[1:3]
+def pack_kernel(sizes, layers, cases, meta_ref, rows_ref, factors_ref, *outs):
+    terms, modes = factors_ref.shape[1:3]
     gap = jnp.zeros((modes, HALF - modes), F32)
     parts = []
     for term in range(terms):
-        whole = factors_vmem[0, term]
+        whole = factors_ref[0, term]
         high = whole.astype(BF16).astype(F32)
         parts.append(jnp.concatenate([high, gap, whole - high, gap], axis=1))
     factors = jnp.concatenate(parts, axis=0).astype(BF16)
     row = lax.broadcasted_iota(jnp.int32, (16, LANES), 0)
     ids = jnp.zeros((16, LANES), F32)
     for term in range(terms):
-        sub = pattern_smem[0, term]
+        sub = meta_ref[0, 2 * PLANES + 2 + term]
         ids = jnp.where(row == term, (sub // 16).astype(F32), ids)
         ids = jnp.where(row == 8 + term, (sub % 16).astype(F32), ids)
     ids = ids.astype(BF16)
-    slots = [slot_of(sizes, partners_smem[0, b]) for b in range(PLANES)]
-    wanted = []
-    for slot in range(PLANES):
-        wanted.append(sum(jnp.where(slots[b] == slot, b, 0) for b in range(PLANES)))
-    if layers == 1:
-        wanted.append(jnp.where(lax.axis_index("coarse") == 0, PLANES + 1, PLANES))
-    else:
-        wanted += [PLANES, PLANES + 1]
     places = layout_of(terms, modes)
-    for out_ref, block in zip(outs, wanted):
+    for out_ref, block in zip(outs, wanted_blocks(sizes, layers, meta_ref)):
         out_ref[places["factors"], :] = factors
         out_ref[places["ids"], :] = ids
-        start = block * LANES
-        if not isinstance(start, int):
-            start = pl.multiple_of(start, LANES)
-        out_ref[places["basis"], :] = basis_out[0, :, pl.ds(start, LANES)]
-        out_ref[places["loads"], :] = loads_out[0, :, pl.ds(start, LANES)]
+        out_ref[places["loads"], :] = rows_ref[:cases, lanes_of(block)]
+        out_ref[places["basis"], :] = rows_ref[cases:, lanes_of(block)]
 
 
 def layout_of(terms, modes):
@@ -131,37 +126,28 @@
     return result, ours, theirs
 
 
-def first_restrict_kernel(sizes, dims, layers, partners_ref, counts_ref, loads_ref, basis_ref, *refs):
-    near_refs, (out_ref, message_ref, scratch_ref) = refs[: PLANES + layers], refs[-3:]
-    span = layout_of(*dims)["loads"]
+def restrict_kernel(sizes, layers, span, cases, own_loads, meta_ref, rows_ref, *refs):
+    near_refs, refs = refs[: PLANES + layers], refs[PLANES + layers :]
+    out_ref, message_ref, scratch_ref = refs[-3:]
     for slot in range(PLANES):
         scratch_ref[slot] = near_refs[slot][span, :]
-    facing = [scratch_ref[slot_of(sizes, partners_ref[0, b])] for b in range(PLANES)]
+    facing = [scratch_ref[slot_of(sizes, meta_ref[0, b])] for b in range(PLANES)]
     facing += [near_refs[PLANES][span, :], near_refs[-1][span, :]]
-    restrict(counts_ref, loads_ref[0], facing, basis_ref, None, out_ref, message_ref)
-
-
-def restrict_kernel(sizes, partners_ref, counts_ref, mine_ref, basis_ref, sums_ref, arrived_ref, out_ref, message_ref):
-    facing = [arrived_ref[target] for target in facing_subs(sizes, partners_ref)]
-    restrict(counts_ref, mine_ref[...], facing, basis_ref, sums_ref, out_ref, message_ref)
-
-
-def restrict(counts_ref, mine, facing, basis_ref, sums_ref, out_ref, message_ref):
-    modes = basis_ref.shape[1]
-    cases = mine.shape[0]
-    result, ours, theirs = difference(counts_ref, mine, facing)
+    mine = rows_ref[:cases, :] if own_loads else refs[0][...]
+    basis = rows_ref[cases:, :]
+    modes = basis.shape[0]
+    result, ours, theirs = difference(meta_ref, mine, facing)
     for block, values in enumerate(result):
         out_ref[:, block * LANES : (block + 1) * LANES] = values
     both = jnp.concatenate([jnp.concatenate(ours, axis=1), jnp.concatenate(theirs, axis=1)], axis=0)
-    basis = basis_ref[0]
     gap = jnp.zeros((HALF - modes, basis.shape[1]), BF16)
     twice = jnp.concatenate([basis, gap, basis, gap], axis=0)
     coefficients = lax.dot_general(both, twice, (((1,), (1,)), ((), ())), preferred_element_type=F32)
     coefficients = coefficients[:cases] - coefficients[cases:]
     half = cases // 2
     message = jnp.where(lane_ids(half) < HALF, coefficients[:half], coefficients[half:])
-    if sums_ref is not None:
-        message = message + sums_ref[...]
+    if not own_loads:
+        message = message + refs[1][...]
     message_ref[...] = jnp.broadcast_to(message[None], message_ref.shape)
 
 
@@ -212,23 +198,23 @@
     return solutions
 
 
-def advance(sizes, dims, partners_ref, counts_ref, coeffs, residual, near_refs, basis_ref, dual_ref, theirs_ref,
-            direction_ref, applied_ref):
+def advance(sizes, dims, meta_ref, coeffs, residual, near_refs, rows_ref, dual_ref, theirs_ref, direction_ref,
+            applied_ref):
     terms, modes = dims
     span = layout_of(terms, modes)["basis"]
     near = [ref[...] for ref in near_refs]
     solutions = solve(coeffs, near, terms, modes)
-    mine = dot(solutions[0], basis_ref[0]).astype(BF16).astype(F32)
+    mine = dot(solutions[0], rows_ref[residual.shape[0] :, :]).astype(BF16).astype(F32)
     for index, packed in enumerate(near[1:]):
         theirs_ref[index] = dot(solutions[index + 1], packed[span, :]).astype(BF16).astype(F32)
     pieces = []
     for block in range(PLANES + 2):
         if block < PLANES:
-            place = slot_of(sizes, partners_ref[0, block])
+            place = slot_of(sizes, meta_ref[0, block])
         else:
             place = min(block, len(near) - 2)
         here = slice(block * LANES, (block + 1) * LANES)
-        pieces.append(residual[:, here] + live_mask(counts_ref, block) * (mine[:, here] - theirs_ref[place]))
+        pieces.append(residual[:, here] + live_mask(meta_ref, block) * (mine[:, here] - theirs_ref[place]))
     direction = jnp.concatenate(pieces, axis=1)
     direction_ref[...] = direction
     applied = dot(direction.astype(BF16), dual_ref[0]).astype(BF16)
@@ -244,15 +230,16 @@
     return applied, sums
 
 
-def first_kernel(sizes, dims, count, partners_ref, counts_ref, coeffs_ref, residual_ref, basis_ref, dual_ref, *refs):
+def first_kernel(sizes, dims, layers, count, meta_ref, coeffs_ref, residual_ref, rows_ref, dual_ref, *refs):
     near_refs = refs[:count]
-    message_ref, direction_ref, applied_ref, sums_ref, theirs_ref = refs[count:]
-    applied, sums = advance(
-        sizes, dims, partners_ref, counts_ref, coeffs_ref[...], residual_ref[...], near_refs, basis_ref, dual_ref,
-        theirs_ref, direction_ref, applied_ref,
-    )
-    message_ref[...] = jnp.zeros_like(message_ref)
-    post_blocks(message_ref, facing_subs(sizes, partners_ref), applied)
+    direction_ref, applied_ref, sums_ref = refs[count : count + 3]
+    message_refs, theirs_ref = refs[count + 3 : -1], refs[-1]
+    _, sums = advance(
+        sizes, dims, meta_ref, coeffs_ref[...], residual_ref[...], near_refs, rows_ref, dual_ref, theirs_ref,
+        direction_ref, applied_ref,
+    )
+    for message_ref, block in zip(message_refs, wanted_blocks(sizes, layers, meta_ref)):
+        message_ref[...] = applied_ref[:, lanes_of(block)]
     sums_ref[...] = sums
 
 
@@ -262,8 +249,8 @@
     return low, high
 
 
-def second_kernel(sizes, dims, count, partners_ref, counts_ref, coeffs_ref, change_ref, residual_ref, image_ref,
-                  before_ref, basis_ref, dual_ref, *refs):
+def second_kernel(sizes, dims, count, meta_ref, coeffs_ref, change_ref, residual_ref, image_ref, before_ref, rows_ref,
+                  dual_ref, *refs):
     near_refs = refs[:count]
     message_ref, residual_out, multipliers_out, direction_ref, applied_ref, theirs_ref = refs[count:]
     half = residual_ref.shape[0] // 2
@@ -276,8 +263,7 @@
     residual_out[...] = residual
     multipliers_out[...] = step * before_ref[...]
     applied, sums = advance(
-        sizes, dims, partners_ref, counts_ref, coeffs, residual, near_refs, basis_ref, dual_ref, theirs_ref,
-        direction_ref, applied_ref,
+        sizes, dims, meta_ref, coeffs, residual, near_refs, rows_ref, dual_ref, theirs_ref, direction_ref, applied_ref
     )
     top = sums.astype(BF16).astype(F32)
     middle = (sums - top).astype(BF16).astype(F32)
@@ -286,22 +272,22 @@
     cases = applied.shape[0]
     message_ref[:, :cases, :] = jnp.zeros((message_ref.shape[0], cases, LANES), BF16)
     message_ref[:, cases:, :] = jnp.broadcast_to(coded[None], (message_ref.shape[0], half, LANES))
-    post_blocks(message_ref, facing_subs(sizes, partners_ref), applied)
-
-
-def last_kernel(sizes, partners_ref, counts_ref, arrived_ref, applied_ref, residual_ref, multipliers_ref, direction_ref,
+    post_blocks(message_ref, facing_subs(sizes, meta_ref), applied)
+
+
+def last_kernel(sizes, meta_ref, arrived_ref, applied_ref, residual_ref, multipliers_ref, direction_ref,
                 multipliers_out, residual_out):
     cases = applied_ref.shape[0]
     totals = jnp.sum(arrived_ref[:, cases:, :].astype(F32), axis=0)
     totals = totals + pltpu.roll(totals, LANES - 2, 1) + pltpu.roll(totals, LANES - 4, 1)
     step = jnp.concatenate(steps_from(totals), axis=0)
-    facing = [arrived_ref[target, :cases, :] for target in facing_subs(sizes, partners_ref)]
-    image, _, _ = difference(counts_ref, applied_ref[...], facing)
+    facing = [arrived_ref[target, :cases, :] for target in facing_subs(sizes, meta_ref)]
+    image, _, _ = difference(meta_ref, applied_ref[...], facing)
     fine = lax.axis_index("fine")
     for block in range(PLANES + 2):
         span = slice(block * LANES, (block + 1) * LANES)
         if block < PLANES:
-            sign = jnp.where(fine < partners_ref[0, block], 1.0, -1.0).astype(F32)
+            sign = jnp.where(fine < meta_ref[0, block], 1.0, -1.0).astype(F32)
         else:
             sign = -1.0 if block == PLANES else 1.0
         multipliers_out[0, :, span] = sign * (multipliers_ref[:, span] + step * direction_ref[:, span])
@@ -342,75 +328,76 @@
     def swap_all(message):
         return lax.all_to_all(message, AXES, 0, 0, tiled=True)
 
-    def swap_layers(messages):
-        if layers == 1:
-            return [lax.ppermute(messages[0], "coarse", [(0, 1), (1, 0)])]
-        up = [(i, i + 1) for i in range(coarse_count - 1)]
-        return [lax.ppermute(messages[1], "coarse", up), lax.ppermute(messages[0], "coarse", [(j, i) for i, j in up])]
-
-    def swap_slot(packed, slot):
+    def swap_slot(message, slot):
         distance = 2 * slot + 1
         pairs = [(i, (i + distance if i % 2 == 0 else i - distance) % fine_count) for i in range(fine_count)]
-        return lax.ppermute(packed, "fine", pairs)
-
-    rows = ((cases, width), F32)
-    half_rows = ((cases, width), BF16)
+        return lax.ppermute(message, "fine", pairs)
+
+    def swap_blocks(messages):
+        received = [swap_slot(messages[slot], slot) for slot in reversed(range(PLANES))][::-1]
+        if layers == 1:
+            return received + [lax.ppermute(messages[PLANES], "coarse", [(0, 1), (1, 0)])]
+        up = [(i, i + 1) for i in range(coarse_count - 1)]
+        lower = lax.ppermute(messages[PLANES + 1], "coarse", up)
+        return received + [lower, lax.ppermute(messages[PLANES], "coarse", [(j, i) for i, j in up])]
+
+    full = ((cases, width), F32)
+    half_full = ((cases, width), BF16)
     coded = ((subs, half, LANES), F32)
+    block = ((cases, LANES), BF16)
     dma = pltpu.SemaphoreType.DMA
 
-    message_rows = layout_of(terms, modes)["loads"].stop
-    partners, row_counts, loads, basis, *packed = call(
-        functools.partial(pack_kernel, sizes, layers),
+    meta = jnp.concatenate([partners, row_counts, pattern], axis=1)
+    rows = jnp.concatenate([load_cases[0], coarse_basis[0]], axis=0)
+    loads_span = layout_of(terms, modes)["loads"]
+    packed = call(
+        functools.partial(pack_kernel, sizes, layers, cases),
         "pack_setup",
-        (),
-        (),
-        [(partners.shape, jnp.int32), (row_counts.shape, jnp.int32), (load_cases.shape, BF16), (coarse_basis.shape, BF16)]
-        + [((message_rows, LANES), BF16)] * (PLANES + layers),
-        [pltpu.SMEM(partners.shape, jnp.int32), pltpu.SMEM(pattern.shape, jnp.int32),
-         pltpu.VMEM(factor_blocks.shape, F32), dma((7,))],
-        (partners, row_counts, pattern, load_cases, coarse_basis, factor_blocks),
-    )
-    received = [swap_slot(packed[slot], slot) for slot in range(PLANES)] + swap_layers(packed[PLANES:])
+        (meta,),
+        (rows, factor_blocks),
+        [((loads_span.stop, LANES), BF16)] * (PLANES + layers),
+    )
+    received = swap_blocks(packed)
     near = [packed[-1]] + received
     count = len(near)
     theirs = [pltpu.VMEM((count - 1, cases, LANES), F32)]
-
-    scalars = (partners, row_counts)
+    landed = [pltpu.VMEM((PLANES, cases, LANES), BF16)]
+
     residual, message = call(
-        functools.partial(first_restrict_kernel, sizes, dims, layers),
+        functools.partial(restrict_kernel, sizes, layers, loads_span, cases, True),
         "restrict_residual",
-        scalars,
-        (loads, basis, *received),
-        [rows, coded],
-        [pltpu.VMEM((PLANES, cases, LANES), BF16)],
+        (meta,),
+        (rows, *received),
+        [full, coded],
+        landed,
     )
     coeffs = swap_all(message).reshape(subs * half, LANES)
     [dual] = call(dual_kernel, "fetch_dual", (), (), [(dual_ops.shape, BF16)], [dma((1,))], (dual_ops,), (residual,))
 
-    message, direction, applied, sums = call(
-        functools.partial(first_kernel, sizes, dims, count),
+    direction, applied, sums, *messages = call(
+        functools.partial(first_kernel, sizes, dims, layers, count),
         "first_direction",
-        scalars,
-        (coeffs, residual, basis, dual, *near),
-        [((subs, cases, LANES), BF16), rows, half_rows, ((half, LANES), F32)],
+        (meta,),
+        (coeffs, residual, rows, dual, *near),
+        [full, half_full, ((half, LANES), F32)] + [block] * (PLANES + layers),
         theirs,
     )
-    arrived = swap_all(message)
     image, message = call(
-        functools.partial(restrict_kernel, sizes),
+        functools.partial(restrict_kernel, sizes, layers, slice(0, cases), cases, False),
         "restrict_image",
-        scalars,
-        (applied, basis, sums, arrived),
-        [rows, coded],
+        (meta,),
+        (rows, *swap_blocks(messages), applied, sums),
+        [full, coded],
+        landed,
     )
     change = swap_all(message).reshape(subs * half, LANES)
 
     message, residual, multipliers, direction, applied = call(
         functools.partial(second_kernel, sizes, dims, count),
         "second_direction",
-        scalars,
-        (coeffs, change, residual, image, direction, basis, dual, *near),
-        [((subs, cases + half, LANES), BF16), rows, rows, rows, half_rows],
+        (meta,),
+        (coeffs, change, residual, image, direction, rows, dual, *near),
+        [((subs, cases + half, LANES), BF16), full, full, full, half_full],
         theirs,
     )
     arrived = swap_all(message)
@@ -418,7 +405,7 @@
     multipliers, residual = call(
         functools.partial(last_kernel, sizes),
         "finish",
-        scalars,
+        (meta,),
         (arrived, applied, residual, multipliers, direction),
         [out, out],
     )

time: 76.4 us -> 80.5 us (1.054)
  starting transfers between devices: 19.9 us -> 30.1 us
  blocking collectives: 31 us -> 26.2 us
  local copies, waits for them, and re-layouts: 6.09 us -> 2.48 us
  other arithmetic: 0 us -> 1.67 us
    ppermute x7 -> x14, starting transfers between devices: 13.2 us -> 23.4 us  [the longest x12 18.8 us: swap_slot(): return lax.ppermute(message, 'fine', pairs)]
    all_to_all x3 -> x2, blocking collectives: 31 us -> 26.2 us  [swap_all(): return lax.all_to_all(message, AXES, 0, 0, tiled=True)]
    unnamed x14 -> x4, local copies, waits for them, and re-layouts: 6.09 us -> 2.48 us
    concatenate x0 -> x2, other arithmetic: none -> 1.67 us  [the longest x1 0.91 us: body(): rows = jnp.concatenate([load_cases[0], coarse_basis[0]], axis=0)]
    ppermute x7 -> x14, waiting for transfers between devices: 3.66 us -> 4.49 us  [the longest x12 4.46 us: swap_slot(): return lax.ppermute(message, 'fine', pairs)]
  transfers between devices with their start and end apart: 8 -> 15, of which waited for: 3 -> 4; matrix products, arithmetic and copies ran while one was open for 0% -> 0% of each run, Pallas kernels for 0% -> 0%
where the time goes in v1:
time: 80.5 us; the launch traced here: 80.2 us
  starting transfers between devices  30.1 us (37%)
  blocking collectives  26.2 us (33%)
  waiting for transfers between devices  10.9 us (14%)
  Pallas kernels  8.05 us (10%)
  local copies, waits for them, and re-layouts  2.48 us (3%)
  other arithmetic  1.67 us (2%)
    all_to_all x2, blocking collectives, swap_all(): return lax.all_to_all(message, AXES, 0, 0, tiled=True)  26.2 us
    ppermute x12, starting transfers between devices, swap_slot(): return lax.ppermute(message, 'fine', pairs)  18.8 us
    pallas_call x7, Pallas kernels, call(): pl.pallas_call(kernel, name=name, out_shape=[jax.ShapeDtypeStruct(shape,...  8.05 us
    all_to_all x1, starting transfers between devices, swap_all(): return lax.all_to_all(message, AXES, 0, 0, tiled=True)  6.73 us
    all_to_all x1, waiting for transfers between devices, swap_all(): return lax.all_to_all(message, AXES, 0, 0, tiled=True)  6.44 us
    ppermute x2, starting transfers between devices, swap_blocks(): lax.ppermute(messages[PLANES], 'coarse', [(0, 1), (1, 0)])  4.57 us
    ppermute x12, waiting for transfers between devices, swap_slot(): return lax.ppermute(message, 'fine', pairs)  4.46 us
    unnamed x4, local copies, waits for them, and re-layouts  2.48 us
  transfers between devices with their start and end apart: 15, of which 4 were waited for; matrix products, arithmetic and copies ran while one was open for 0% of the time, Pallas kernels for 0%

profile of v1, /device:TPU:1, one launch (start us, length us, event | category | flops | bytes accessed | tf_op | source)
XLA Modules:
  0.0 80.2 jit_solution(2483459337788810277)
XLA Ops:
  0.6 0.9 %pad_maximum_fusion.rows_ref = bf16[64,1024]{1,0:T(8,128)(2,1)S(1)} fusion(bf16[48,1024]{1,0:T(8,128)(2,1)} %bitcast.7, bf16[16,1024]{1,0:T(8,128)(2,1)} %bitcast.8), kind=kLoop, calls=%fused_computation | loop fusion | flops 262144 | bytes 262144 | tf_op jit(solution)/shard_map/concatenate | solution.py:351
  1.5 0.8 pad_add_fusion.meta_ref
  2.3 0.0 copy-start.1
  2.3 0.9 %copy-done.1 = f32[1,4,48,48]{3,2,1,0:T(8,128)S(1)} copy-done((f32[1,4,48,48]{3,2,1,0:T(8,128)S(1)}, f32[1,4,48,48]{3,2,1,0:T(8,128)}, u32[]{:S(2)}) %copy-start.1) | copy-done | bytes 36888
  3.2 0.7 pack_setup.1
  3.9 2.1 %collective-permute-start = (bf16[272,128]{1,0:T(8,128)(2,1)S(1)}, bf16[272,128]{1,0:T(8,128)(2,1)S(1)}, u32[]{:S(2)}, u32[]{:S(2)}) collective-permute-start(bf16[272,128]{1,0:T(8,128)(2,1)S(1)} %get-tuple-element.28), channel_id=1, source_target_pairs={{0,2},{2,0},{4,6},{6,4},{8,10},{10,8},{12,14},{14,12},{16,18},{18,... | collective-permute-start | bytes 208904 | tf_op jit(solution)/shard_map/ppermute | solution.py:334
  6.0 1.2 %collective-permute-start.1 = (bf16[272,128]{1,0:T(8,128)(2,1)S(1)}, bf16[272,128]{1,0:T(8,128)(2,1)S(1)}, u32[]{:S(2)}, u32[]{:S(2)}) collective-permute-start(bf16[272,128]{1,0:T(8,128)(2,1)S(1)} %get-tuple-element.29), channel_id=1, source_target_pairs={{0,6},{2,28},{4,10},{6,0},{8,14},{10,4},{12,18},{14,8},{16,22},{18... | collective-permute-start | bytes 208904 | tf_op jit(solution)/shard_map/ppermute | solution.py:334
  7.2 2.1 %collective-permute-start.2 = (bf16[272,128]{1,0:T(8,128)(2,1)S(1)}, bf16[272,128]{1,0:T(8,128)(2,1)S(1)}, u32[]{:S(2)}, u32[]{:S(2)}) collective-permute-start(bf16[272,128]{1,0:T(8,128)(2,1)S(1)} %get-tuple-element.30), channel_id=1, source_target_pairs={{0,10},{2,24},{4,14},{6,28},{8,18},{10,0},{12,22},{14,4},{16,26},{... | collective-permute-start | bytes 208904 | tf_op jit(solution)/shard_map/ppermute | solution.py:334
  9.3 1.2 %collective-permute-start.3 = (bf16[272,128]{1,0:T(8,128)(2,1)S(1)}, bf16[272,128]{1,0:T(8,128)(2,1)S(1)}, u32[]{:S(2)}, u32[]{:S(2)}) collective-permute-start(bf16[272,128]{1,0:T(8,128)(2,1)S(1)} %get-tuple-element.31), channel_id=1, source_target_pairs={{0,14},{2,20},{4,18},{6,24},{8,22},{10,28},{12,26},{14,0},{16,30},... | collective-permute-start | bytes 208904 | tf_op jit(solution)/shard_map/ppermute | solution.py:334
  10.5 2.1 %collective-permute-start.4 = (bf16[272,128]{1,0:T(8,128)(2,1)S(1)}, bf16[272,128]{1,0:T(8,128)(2,1)S(1)}, u32[]{:S(2)}, u32[]{:S(2)}) collective-permute-start(bf16[272,128]{1,0:T(8,128)(2,1)S(1)} %get-tuple-element.32), channel_id=1, source_target_pairs={{0,18},{2,16},{4,22},{6,20},{8,26},{10,24},{12,30},{14,28},{16,2},... | collective-permute-start | bytes 208904 | tf_op jit(solution)/shard_map/ppermute | solution.py:334
  12.6 0.0 collective-permute-done.refs_0_.refs_1_
  12.6 2.1 %collective-permute-start.5 = (bf16[272,128]{1,0:T(8,128)(2,1)S(1)}, bf16[272,128]{1,0:T(8,128)(2,1)S(1)}, u32[]{:S(2)}, u32[]{:S(2)}) collective-permute-start(bf16[272,128]{1,0:T(8,128)(2,1)S(1)} %get-tuple-element.33), channel_id=1, source_target_pairs={{0,22},{2,12},{4,26},{6,16},{8,30},{10,20},{12,2},{14,24},{16,6},{... | collective-permute-start | bytes 208904 | tf_op jit(solution)/shard_map/ppermute | solution.py:334
  14.7 0.0 collective-permute-done.1.refs_1_.refs_2_
  14.7 2.4 %collective-permute-start.6 = (bf16[272,128]{1,0:T(8,128)(2,1)S(1)}, bf16[272,128]{1,0:T(8,128)(2,1)S(1)}, u32[]{:S(2)}, u32[]{:S(2)}) collective-permute-start(bf16[272,128]{1,0:T(8,128)(2,1)S(1)} %get-tuple-element.34.refs_0_), channel_id=1, source_target_pairs={{0,1},{1,0},{2,3},{3,2},{4,5},{5,4},{6,7},{7,6},{8,9},{9,8},{10,11... | collective-permute-start | bytes 208904 | tf_op jit(solution)/shard_map/ppermute | solution.py:339
  17.1 0.0 collective-permute-done.2.refs_2_.refs_3_
  17.1 0.0 collective-permute-done.3.refs_3_.refs_4_
  17.1 3.0 %collective-permute-done.4.refs_4_.refs_5_ = bf16[272,128]{1,0:T(8,128)(2,1)S(1)} collective-permute-done((bf16[272,128]{1,0:T(8,128)(2,1)S(1)}, bf16[272,128]{1,0:T(8,128)(2,1)S(1)}, u32[]{:S(2)}, u32[]{:S(2)}) %collective-permute-start.4) | collective-permute-done | bytes 69664 | tf_op jit(solution)/shard_map/ppermute | solution.py:334
  20.1 0.7 collective-permute-done.5.refs_5_.refs_6_
  20.8 0.0 collective-permute-done.6.refs_6_.refs_7_
  20.8 1.4 %restrict_residual.1 = (f32[16,1024]{1,0:T(8,128)S(1)}, f32[32,8,128]{2,1,0:T(8,128)}) custom-call(s32[1,18]{1,0:T(1,128)S(1)} %pad_add_fusion.meta_ref, bf16[64,1024]{1,0:T(8,128)(2,1)S(1)} %pad_maximum_fusion.rows_ref, bf16[272,128]{1,0:T(8,128)(2,1)S(1)} %collective-permute-done.refs_0_.refs_1_, ...), custom_call_target="tpu_custom_call" | custom-call | tf_op jit(solution)/shard_map/restrict_residual/pallas_call | solution.py:306
  22.1 6.7 %all-to-all-start = ((f32[32,8,128]{2,1,0:T(8,128)}), f32[32,8,128]{2,1,0:T(8,128)S(1)}, u32[]{:S(2)}, u32[]{:S(2)}) async-start(f32[32,8,128]{2,1,0:T(8,128)} %get-tuple-element.35), calls=%async_computation | async-start | bytes 262144 | tf_op jit(solution)/shard_map/all_to_all | solution.py:329
  28.9 0.0 copy-start
  28.9 1.6 %copy-done = bf16[1,1024,1024]{2,1,0:T(8,128)(2,1)S(1)} copy-done((bf16[1,1024,1024]{2,1,0:T(8,128)(2,1)S(1)}, bf16[1,1024,1024]{2,1,0:T(8,128)(2,1)}, u32[]{:S(2)}) %copy-start) | copy-done | bytes 2097176
  30.5 0.1 fetch_dual.1.dual_ref
  30.6 6.4 %all-to-all-done = f32[32,8,128]{2,1,0:T(8,128)S(1)} async-done(((f32[32,8,128]{2,1,0:T(8,128)}), f32[32,8,128]{2,1,0:T(8,128)S(1)}, u32[]{:S(2)}, u32[]{:S(2)}) %all-to-all-start) | async-done | bytes 131104 | tf_op jit(solution)/shard_map/all_to_all | solution.py:329
  37.1 1.7 %first_direction.1 = (f32[16,1024]{1,0:T(8,128)S(1)}, bf16[16,1024]{1,0:T(8,128)(2,1)S(1)}, f32[8,128]{1,0:T(8,128)S(1)}, bf16[16,128]{1,0:T(8,128)(2,1)S(1)}, b...) custom-call(s32[1,18]{1,0:T(1,128)S(1)} %pad_add_fusion.meta_ref, ...), custom_call_target="tpu_custom_call" | custom-call | tf_op jit(solution)/shard_map/first_direction/pallas_call | solution.py:306
  38.7 0.1 collective-permute-start.7
  38.8 1.2 %collective-permute-start.8 = (bf16[16,128]{1,0:T(8,128)(2,1)S(1)}, bf16[16,128]{1,0:T(8,128)(2,1)S(1)}, u32[]{:S(2)}, u32[]{:S(2)}) collective-permute-start(bf16[16,128]{1,0:T(8,128)(2,1)S(1)} %get-tuple-element.38), channel_id=1, source_target_pairs={{0,6},{2,28},{4,10},{6,0},{8,14},{10,4},{12,18},{14,8},{16,22},{18... | collective-permute-start | bytes 12296 | tf_op jit(solution)/shard_map/ppermute | solution.py:334
  40.0 1.4 %collective-permute-start.9 = (bf16[16,128]{1,0:T(8,128)(2,1)S(1)}, bf16[16,128]{1,0:T(8,128)(2,1)S(1)}, u32[]{:S(2)}, u32[]{:S(2)}) collective-permute-start(bf16[16,128]{1,0:T(8,128)(2,1)S(1)} %get-tuple-element.39), channel_id=1, source_target_pairs={{0,10},{2,24},{4,14},{6,28},{8,18},{10,0},{12,22},{14,4},{16,26},{... | collective-permute-start | bytes 12296 | tf_op jit(solution)/shard_map/ppermute | solution.py:334
  41.4 1.2 %collective-permute-start.10 = (bf16[16,128]{1,0:T(8,128)(2,1)S(1)}, bf16[16,128]{1,0:T(8,128)(2,1)S(1)}, u32[]{:S(2)}, u32[]{:S(2)}) collective-permute-start(bf16[16,128]{1,0:T(8,128)(2,1)S(1)} %get-tuple-element.40), channel_id=1, source_target_pairs={{0,14},{2,20},{4,18},{6,24},{8,22},{10,28},{12,26},{14,0},{16,30},... | collective-permute-start | bytes 12296 | tf_op jit(solution)/shard_map/ppermute | solution.py:334
  42.5 2.0 %collective-permute-start.11 = (bf16[16,128]{1,0:T(8,128)(2,1)S(1)}, bf16[16,128]{1,0:T(8,128)(2,1)S(1)}, u32[]{:S(2)}, u32[]{:S(2)}) collective-permute-start(bf16[16,128]{1,0:T(8,128)(2,1)S(1)} %get-tuple-element.41), channel_id=1, source_target_pairs={{0,18},{2,16},{4,22},{6,20},{8,26},{10,24},{12,30},{14,28},{16,2},... | collective-permute-start | bytes 12296 | tf_op jit(solution)/shard_map/ppermute | solution.py:334
  44.5 0.0 collective-permute-done.7.refs_0_
  44.5 2.1 %collective-permute-start.12 = (bf16[16,128]{1,0:T(8,128)(2,1)S(1)}, bf16[16,128]{1,0:T(8,128)(2,1)S(1)}, u32[]{:S(2)}, u32[]{:S(2)}) collective-permute-start(bf16[16,128]{1,0:T(8,128)(2,1)S(1)} %get-tuple-element.42), channel_id=1, source_target_pairs={{0,22},{2,12},{4,26},{6,16},{8,30},{10,20},{12,2},{14,24},{16,6},{... | collective-permute-start | bytes 12296 | tf_op jit(solution)/shard_map/ppermute | solution.py:334
  46.7 0.0 collective-permute-done.8.refs_1_
  46.7 2.2 %collective-permute-start.13 = (bf16[16,128]{1,0:T(8,128)(2,1)S(1)}, bf16[16,128]{1,0:T(8,128)(2,1)S(1)}, u32[]{:S(2)}, u32[]{:S(2)}) collective-permute-start(bf16[16,128]{1,0:T(8,128)(2,1)S(1)} %get-tuple-element.43), channel_id=1, source_target_pairs={{0,1},{1,0},{2,3},{3,2},{4,5},{5,4},{6,7},{7,6},{8,9},{9,8},{10,11... | collective-permute-start | bytes 12296 | tf_op jit(solution)/shard_map/ppermute | solution.py:339
  48.9 0.0 collective-permute-done.9.refs_2_
  48.9 0.0 collective-permute-done.10.refs_3_
  48.9 0.0 collective-permute-done.11.refs_4_
  48.9 0.8 collective-permute-done.12.refs_5_
  49.7 0.0 collective-permute-done.13.refs_6_
  49.7 0.7 restrict_image.1
  50.5 15.2 %all_to_all.15 = f32[32,8,128]{2,1,0:T(8,128)S(1)} all-to-all(f32[32,8,128]{2,1,0:T(8,128)S(1)} %get-tuple-element.46), channel_id=1, replica_groups=mesh['fine'=16,'coarse'=2] {'fine','coarse'}, dimensions={0} | all-to-all | bytes 262144 | tf_op jit(solution)/shard_map/all_to_all | solution.py:329
  65.7 1.9 %second_direction.1 = (bf16[32,24,128]{2,1,0:T(8,128)(2,1)S(1)}, f32[16,1024]{1,0:T(8,128)S(1)}, f32[16,1024]{1,0:T(8,128)S(1)}, f32[16,1024]{1,0:T(8,128)S(1)}, bf16[16,1024]{1,0:T(8,128)(2,1)S(1)}) custom-call(s32[1,18]{1,0:T(1,128)S(1)} %pad_add_fusion.meta_ref, f32[256,128]{1,0:T(8,128)S(1)} %bitcast.5, f32[256,128]{1,0:T(8,128)S(1)} %bitcast.6, ...), custom_call_target="tpu_custom_call" | custom-call | tf_op jit(solution)/shard_map/second_direction/pallas_call | solution.py:306
  67.6 11.0 %all_to_all.16.arrived_ref = bf16[32,24,128]{2,1,0:T(8,128)(2,1)S(1)} all-to-all(bf16[32,24,128]{2,1,0:T(8,128)(2,1)S(1)} %get-tuple-element.49), channel_id=1, replica_groups=mesh['fine'=16,'coarse'=2] {'fine','coarse'}, dimensions={0} | all-to-all | bytes 393216 | tf_op jit(solution)/shard_map/all_to_all | solution.py:329
  78.6 1.5 %finish.1 = (f32[1,16,1024]{2,1,0:T(8,128)}, f32[1,16,1024]{2,1,0:T(8,128)}) custom-call(s32[1,18]{1,0:T(1,128)S(1)} %pad_add_fusion.meta_ref, bf16[32,24,128]{2,1,0:T(8,128)(2,1)S(1)} %all_to_all.16.arrived_ref, bf16[16,1024]{1,0:T(8,128)(2,1)S(1)} %get-tuple-element.50.applied_ref, f32[16,1024]{1,0:T(8,128)S(1)} %get-tuple-element.51.residual_ref, ...), custom_call_target="tpu_custom_call" | custom-call | tf_op jit(solution)/shard_map/finish/pallas_call | solution.py:306
Async XLA Ops:
  2.3 0.9 %copy-start.1 = (f32[1,4,48,48]{3,2,1,0:T(8,128)S(1)}, f32[1,4,48,48]{3,2,1,0:T(8,128)}, u32[]{:S(2)}) copy-start(f32[1,4,48,48]{3,2,1,0:T(8,128)} %factors_ref.1) | copy-start | bytes 110596
  3.9 8.8 %collective-permute-start = (bf16[272,128]{1,0:T(8,128)(2,1)S(1)}, bf16[272,128]{1,0:T(8,128)(2,1)S(1)}, u32[]{:S(2)}, u32[]{:S(2)}) collective-permute-start(bf16[272,128]{1,0:T(8,128)(2,1)S(1)} %get-tuple-element.28), channel_id=1, source_target_pairs={{0,2},{2,0},{4,6},{6,4},{8,10},{10,8},{12,14},{14,12},{16,18},{18,... | collective-permute-start | bytes 208904 | tf_op jit(solution)/shard_map/ppermute | solution.py:334
  6.0 8.8 %collective-permute-start.1 = (bf16[272,128]{1,0:T(8,128)(2,1)S(1)}, bf16[272,128]{1,0:T(8,128)(2,1)S(1)}, u32[]{:S(2)}, u32[]{:S(2)}) collective-permute-start(bf16[272,128]{1,0:T(8,128)(2,1)S(1)} %get-tuple-element.29), channel_id=1, source_target_pairs={{0,6},{2,28},{4,10},{6,0},{8,14},{10,4},{12,18},{14,8},{16,22},{18... | collective-permute-start | bytes 208904 | tf_op jit(solution)/shard_map/ppermute | solution.py:334
  7.2 9.9 %collective-permute-start.2 = (bf16[272,128]{1,0:T(8,128)(2,1)S(1)}, bf16[272,128]{1,0:T(8,128)(2,1)S(1)}, u32[]{:S(2)}, u32[]{:S(2)}) collective-permute-start(bf16[272,128]{1,0:T(8,128)(2,1)S(1)} %get-tuple-element.30), channel_id=1, source_target_pairs={{0,10},{2,24},{4,14},{6,28},{8,18},{10,0},{12,22},{14,4},{16,26},{... | collective-permute-start | bytes 208904 | tf_op jit(solution)/shard_map/ppermute | solution.py:334
  9.3 7.8 %collective-permute-start.3 = (bf16[272,128]{1,0:T(8,128)(2,1)S(1)}, bf16[272,128]{1,0:T(8,128)(2,1)S(1)}, u32[]{:S(2)}, u32[]{:S(2)}) collective-permute-start(bf16[272,128]{1,0:T(8,128)(2,1)S(1)} %get-tuple-element.31), channel_id=1, source_target_pairs={{0,14},{2,20},{4,18},{6,24},{8,22},{10,28},{12,26},{14,0},{16,30},... | collective-permute-start | bytes 208904 | tf_op jit(solution)/shard_map/ppermute | solution.py:334
  10.5 9.6 %collective-permute-start.4 = (bf16[272,128]{1,0:T(8,128)(2,1)S(1)}, bf16[272,128]{1,0:T(8,128)(2,1)S(1)}, u32[]{:S(2)}, u32[]{:S(2)}) collective-permute-start(bf16[272,128]{1,0:T(8,128)(2,1)S(1)} %get-tuple-element.32), channel_id=1, source_target_pairs={{0,18},{2,16},{4,22},{6,20},{8,26},{10,24},{12,30},{14,28},{16,2},... | collective-permute-start | bytes 208904 | tf_op jit(solution)/shard_map/ppermute | solution.py:334
  12.6 8.1 %collective-permute-start.5 = (bf16[272,128]{1,0:T(8,128)(2,1)S(1)}, bf16[272,128]{1,0:T(8,128)(2,1)S(1)}, u32[]{:S(2)}, u32[]{:S(2)}) collective-permute-start(bf16[272,128]{1,0:T(8,128)(2,1)S(1)} %get-tuple-element.33), channel_id=1, source_target_pairs={{0,22},{2,12},{4,26},{6,16},{8,30},{10,20},{12,2},{14,24},{16,6},{... | collective-permute-start | bytes 208904 | tf_op jit(solution)/shard_map/ppermute | solution.py:334
  14.7 6.0 %collective-permute-start.6 = (bf16[272,128]{1,0:T(8,128)(2,1)S(1)}, bf16[272,128]{1,0:T(8,128)(2,1)S(1)}, u32[]{:S(2)}, u32[]{:S(2)}) collective-permute-start(bf16[272,128]{1,0:T(8,128)(2,1)S(1)} %get-tuple-element.34.refs_0_), channel_id=1, source_target_pairs={{0,1},{1,0},{2,3},{3,2},{4,5},{5,4},{6,7},{7,6},{8,9},{9,8},{10,11... | collective-permute-start | bytes 208904 | tf_op jit(solution)/shard_map/ppermute | solution.py:339
  22.1 14.9 %all-to-all-start = ((f32[32,8,128]{2,1,0:T(8,128)}), f32[32,8,128]{2,1,0:T(8,128)S(1)}, u32[]{:S(2)}, u32[]{:S(2)}) async-start(f32[32,8,128]{2,1,0:T(8,128)} %get-tuple-element.35), calls=%async_computation | async-start | bytes 262144 | tf_op jit(solution)/shard_map/all_to_all | solution.py:329
  28.9 1.6 %copy-start = (bf16[1,1024,1024]{2,1,0:T(8,128)(2,1)S(1)}, bf16[1,1024,1024]{2,1,0:T(8,128)(2,1)}, u32[]{:S(2)}) copy-start(bf16[1,1024,1024]{2,1,0:T(8,128)(2,1)} %dual_ref.1) | copy-start | bytes 6291460
  38.7 5.8 %collective-permute-start.7 = (bf16[16,128]{1,0:T(8,128)(2,1)S(1)}, bf16[16,128]{1,0:T(8,128)(2,1)S(1)}, u32[]{:S(2)}, u32[]{:S(2)}) collective-permute-start(bf16[16,128]{1,0:T(8,128)(2,1)S(1)} %get-tuple-element.37), channel_id=1, source_target_pairs={{0,2},{2,0},{4,6},{6,4},{8,10},{10,8},{12,14},{14,12},{16,18},{18,... | collective-permute-start | bytes 12296 | tf_op jit(solution)/shard_map/ppermute | solution.py:334
  38.8 7.9 %collective-permute-start.8 = (bf16[16,128]{1,0:T(8,128)(2,1)S(1)}, bf16[16,128]{1,0:T(8,128)(2,1)S(1)}, u32[]{:S(2)}, u32[]{:S(2)}) collective-permute-start(bf16[16,128]{1,0:T(8,128)(2,1)S(1)} %get-tuple-element.38), channel_id=1, source_target_pairs={{0,6},{2,28},{4,10},{6,0},{8,14},{10,4},{12,18},{14,8},{16,22},{18... | collective-permute-start | bytes 12296 | tf_op jit(solution)/shard_map/ppermute | solution.py:334
  40.0 8.9 %collective-permute-start.9 = (bf16[16,128]{1,0:T(8,128)(2,1)S(1)}, bf16[16,128]{1,0:T(8,128)(2,1)S(1)}, u32[]{:S(2)}, u32[]{:S(2)}) collective-permute-start(bf16[16,128]{1,0:T(8,128)(2,1)S(1)} %get-tuple-element.39), channel_id=1, source_target_pairs={{0,10},{2,24},{4,14},{6,28},{8,18},{10,0},{12,22},{14,4},{16,26},{... | collective-permute-start | bytes 12296 | tf_op jit(solution)/shard_map/ppermute | solution.py:334
  41.4 7.5 %collective-permute-start.10 = (bf16[16,128]{1,0:T(8,128)(2,1)S(1)}, bf16[16,128]{1,0:T(8,128)(2,1)S(1)}, u32[]{:S(2)}, u32[]{:S(2)}) collective-permute-start(bf16[16,128]{1,0:T(8,128)(2,1)S(1)} %get-tuple-element.40), channel_id=1, source_target_pairs={{0,14},{2,20},{4,18},{6,24},{8,22},{10,28},{12,26},{14,0},{16,30},... | collective-permute-start | bytes 12296 | tf_op jit(solution)/shard_map/ppermute | solution.py:334
  42.5 6.4 %collective-permute-start.11 = (bf16[16,128]{1,0:T(8,128)(2,1)S(1)}, bf16[16,128]{1,0:T(8,128)(2,1)S(1)}, u32[]{:S(2)}, u32[]{:S(2)}) collective-permute-start(bf16[16,128]{1,0:T(8,128)(2,1)S(1)} %get-tuple-element.41), channel_id=1, source_target_pairs={{0,18},{2,16},{4,22},{6,20},{8,26},{10,24},{12,30},{14,28},{16,2},... | collective-permute-start | bytes 12296 | tf_op jit(solution)/shard_map/ppermute | solution.py:334
  44.5 5.2 %collective-permute-start.12 = (bf16[16,128]{1,0:T(8,128)(2,1)S(1)}, bf16[16,128]{1,0:T(8,128)(2,1)S(1)}, u32[]{:S(2)}, u32[]{:S(2)}) collective-permute-start(bf16[16,128]{1,0:T(8,128)(2,1)S(1)} %get-tuple-element.42), channel_id=1, source_target_pairs={{0,22},{2,12},{4,26},{6,16},{8,30},{10,20},{12,2},{14,24},{16,6},{... | collective-permute-start | bytes 12296 | tf_op jit(solution)/shard_map/ppermute | solution.py:334
  46.7 3.0 %collective-permute-start.13 = (bf16[16,128]{1,0:T(8,128)(2,1)S(1)}, bf16[16,128]{1,0:T(8,128)(2,1)S(1)}, u32[]{:S(2)}, u32[]{:S(2)}) collective-permute-start(bf16[16,128]{1,0:T(8,128)(2,1)S(1)} %get-tuple-element.43), channel_id=1, source_target_pairs={{0,1},{1,0},{2,3},{3,2},{4,5},{5,4},{6,7},{7,6},{8,9},{9,8},{10,11... | collective-permute-start | bytes 12296 | tf_op jit(solution)/shard_map/ppermute | solution.py:339

commit v2 on v1

--- a/solution.py
+++ b/solution.py
@@ -56,7 +56,7 @@
     fine = lax.axis_index("fine")
     ahead = jnp.where(fine % 2 == 0, partner - fine, fine - partner)
     ahead = jnp.where(ahead < 0, ahead + fine_count, ahead)
-    return (ahead - 1) // 2
+    return PLANES - 1 - (ahead - 1) // 2
 
 
 def live_mask(counts_ref, block):
@@ -126,15 +126,25 @@
     return result, ours, theirs
 
 
-def restrict_kernel(sizes, layers, span, cases, own_loads, meta_ref, rows_ref, *refs):
-    near_refs, refs = refs[: PLANES + layers], refs[PLANES + layers :]
-    out_ref, message_ref, scratch_ref = refs[-3:]
+def first_restrict_kernel(sizes, dims, layers, meta_ref, rows_ref, *refs):
+    near_refs, (_, out_ref, message_ref, scratch_ref) = refs[: PLANES + layers], refs[PLANES + layers :]
+    span = layout_of(*dims)["loads"]
+    cases = out_ref.shape[0]
     for slot in range(PLANES):
         scratch_ref[slot] = near_refs[slot][span, :]
     facing = [scratch_ref[slot_of(sizes, meta_ref[0, b])] for b in range(PLANES)]
     facing += [near_refs[PLANES][span, :], near_refs[-1][span, :]]
-    mine = rows_ref[:cases, :] if own_loads else refs[0][...]
-    basis = rows_ref[cases:, :]
+    restrict(meta_ref, rows_ref[:cases, :], facing, rows_ref[cases:, :], None, out_ref, message_ref)
+
+
+def restrict_kernel(sizes, meta_ref, rows_ref, arrived_ref, applied_ref, sums_ref, out_ref, message_ref):
+    facing = [arrived_ref[target] for target in facing_subs(sizes, meta_ref)]
+    cases = out_ref.shape[0]
+    restrict(meta_ref, applied_ref[...], facing, rows_ref[cases:, :], sums_ref[...], out_ref, message_ref)
+
+
+def restrict(meta_ref, mine, facing, basis, sums, out_ref, message_ref):
+    cases = mine.shape[0]
     modes = basis.shape[0]
     result, ours, theirs = difference(meta_ref, mine, facing)
     for block, values in enumerate(result):
@@ -146,8 +156,8 @@
     coefficients = coefficients[:cases] - coefficients[cases:]
     half = cases // 2
     message = jnp.where(lane_ids(half) < HALF, coefficients[:half], coefficients[half:])
-    if not own_loads:
-        message = message + refs[1][...]
+    if sums is not None:
+        message = message + sums
     message_ref[...] = jnp.broadcast_to(message[None], message_ref.shape)
 
 
@@ -230,16 +240,15 @@
     return applied, sums
 
 
-def first_kernel(sizes, dims, layers, count, meta_ref, coeffs_ref, residual_ref, rows_ref, dual_ref, *refs):
+def first_kernel(sizes, dims, count, meta_ref, coeffs_ref, residual_ref, rows_ref, dual_ref, *refs):
     near_refs = refs[:count]
-    direction_ref, applied_ref, sums_ref = refs[count : count + 3]
-    message_refs, theirs_ref = refs[count + 3 : -1], refs[-1]
-    _, sums = advance(
+    message_ref, direction_ref, applied_ref, sums_ref, theirs_ref = refs[count:]
+    applied, sums = advance(
         sizes, dims, meta_ref, coeffs_ref[...], residual_ref[...], near_refs, rows_ref, dual_ref, theirs_ref,
         direction_ref, applied_ref,
     )
-    for message_ref, block in zip(message_refs, wanted_blocks(sizes, layers, meta_ref)):
-        message_ref[...] = applied_ref[:, lanes_of(block)]
+    message_ref[...] = jnp.zeros_like(message_ref)
+    post_blocks(message_ref, facing_subs(sizes, meta_ref), applied)
     sums_ref[...] = sums
 
 
@@ -329,12 +338,12 @@
         return lax.all_to_all(message, AXES, 0, 0, tiled=True)
 
     def swap_slot(message, slot):
-        distance = 2 * slot + 1
+        distance = 2 * (PLANES - slot) - 1
         pairs = [(i, (i + distance if i % 2 == 0 else i - distance) % fine_count) for i in range(fine_count)]
         return lax.ppermute(message, "fine", pairs)
 
     def swap_blocks(messages):
-        received = [swap_slot(messages[slot], slot) for slot in reversed(range(PLANES))][::-1]
+        received = [swap_slot(messages[slot], slot) for slot in range(PLANES)]
         if layers == 1:
             return received + [lax.ppermute(messages[PLANES], "coarse", [(0, 1), (1, 0)])]
         up = [(i, i + 1) for i in range(coarse_count - 1)]
@@ -344,7 +353,6 @@
     full = ((cases, width), F32)
     half_full = ((cases, width), BF16)
     coded = ((subs, half, LANES), F32)
-    block = ((cases, LANES), BF16)
     dma = pltpu.SemaphoreType.DMA
 
     meta = jnp.concatenate([partners, row_counts, pattern], axis=1)
@@ -361,34 +369,33 @@
     near = [packed[-1]] + received
     count = len(near)
     theirs = [pltpu.VMEM((count - 1, cases, LANES), F32)]
-    landed = [pltpu.VMEM((PLANES, cases, LANES), BF16)]
-
+
+    [dual] = call(dual_kernel, "fetch_dual", (), (), [(dual_ops.shape, BF16)], [dma((1,))], (dual_ops,), (packed[-1],))
     residual, message = call(
-        functools.partial(restrict_kernel, sizes, layers, loads_span, cases, True),
+        functools.partial(first_restrict_kernel, sizes, dims, layers),
         "restrict_residual",
         (meta,),
         (rows, *received),
         [full, coded],
-        landed,
+        [pltpu.VMEM((PLANES, cases, LANES), BF16)],
+        after=(dual,),
     )
     coeffs = swap_all(message).reshape(subs * half, LANES)
-    [dual] = call(dual_kernel, "fetch_dual", (), (), [(dual_ops.shape, BF16)], [dma((1,))], (dual_ops,), (residual,))
-
-    direction, applied, sums, *messages = call(
-        functools.partial(first_kernel, sizes, dims, layers, count),
+
+    message, direction, applied, sums = call(
+        functools.partial(first_kernel, sizes, dims, count),
         "first_direction",
         (meta,),
         (coeffs, residual, rows, dual, *near),
-        [full, half_full, ((half, LANES), F32)] + [block] * (PLANES + layers),
+        [((subs, cases, LANES), BF16), full, half_full, ((half, LANES), F32)],
         theirs,
     )
     image, message = call(
-        functools.partial(restrict_kernel, sizes, layers, slice(0, cases), cases, False),
+        functools.partial(restrict_kernel, sizes),
         "restrict_image",
         (meta,),
-        (rows, *swap_blocks(messages), applied, sums),
+        (rows, swap_all(message), applied, sums),
         [full, coded],
-        landed,
     )
     change = swap_all(message).reshape(subs * half, LANES)
 

time: 80.5 us -> 72.5 us (0.901)
  blocking collectives: 26.2 us -> 43.5 us
  starting transfers between devices: 30.1 us -> 16 us
  waiting for transfers between devices: 10.9 us -> 0.46 us
    all_to_all x2 -> x4, blocking collectives: 26.2 us -> 43.5 us  [swap_all(): return lax.all_to_all(message, AXES, 0, 0, tiled=True)]
    all_to_all x1 -> x0, starting transfers between devices: 6.73 us -> none  [swap_all(): return lax.all_to_all(message, AXES, 0, 0, tiled=True)]
    all_to_all x1 -> x0, waiting for transfers between devices: 6.44 us -> none  [swap_all(): return lax.all_to_all(message, AXES, 0, 0, tiled=True)]
    ppermute x12 -> x6, starting transfers between devices: 18.8 us -> 13.7 us  [swap_slot(): return lax.ppermute(message, 'fine', pairs)]
    ppermute x12 -> x6, waiting for transfers between devices: 4.46 us -> 0.46 us  [swap_slot(): return lax.ppermute(message, 'fine', pairs)]
    ppermute x2 -> x1, starting transfers between devices: 4.57 us -> 2.36 us  [swap_blocks(): lax.ppermute(messages[PLANES], 'coarse', [(0, 1), (1, 0)])]
  transfers between devices with their start and end apart: 15 -> 7, of which waited for: 4 -> 1; matrix products, arithmetic and copies ran while one was open for 0% -> 0% of each run, Pallas kernels for 0% -> 0%
where the time goes in v2:
time: 72.5 us; the launch traced here: 72.2 us
  blocking collectives  43.5 us (60%)
  starting transfers between devices  16 us (22%)
  Pallas kernels  7.4 us (10%)
  local copies, waits for them, and re-layouts  2.48 us (3%)
  other arithmetic  1.67 us (2%)
    all_to_all x4, blocking collectives, swap_all(): return lax.all_to_all(message, AXES, 0, 0, tiled=True)  43.5 us
    ppermute x6, starting transfers between devices, swap_slot(): return lax.ppermute(message, 'fine', pairs)  13.7 us
    pallas_call x7, Pallas kernels, call(): pl.pallas_call(kernel, name=name, out_shape=[jax.ShapeDtypeStruct(shape,...  7.4 us
    unnamed x4, local copies, waits for them, and re-layouts  2.48 us
    ppermute x1, starting transfers between devices, swap_blocks(): lax.ppermute(messages[PLANES], 'coarse', [(0, 1), (1, 0)])  2.36 us
  transfers between devices with their start and end apart: 7, of which 1 were waited for; matrix products, arithmetic and copies ran while one was open for 0% of the time, Pallas kernels for 0%

profile of v2, /device:TPU:1, one launch (start us, length us, event | category | flops | bytes accessed | tf_op | source)
XLA Modules:
  0.0 72.2 jit_solution(5905664738090282416)
XLA Ops:
  0.6 0.9 %pad_maximum_fusion.rows_ref = bf16[64,1024]{1,0:T(8,128)(2,1)S(1)} fusion(bf16[48,1024]{1,0:T(8,128)(2,1)} %bitcast.7, bf16[16,1024]{1,0:T(8,128)(2,1)} %bitcast.8), kind=kLoop, calls=%fused_computation | loop fusion | flops 262144 | bytes 262144 | tf_op jit(solution)/shard_map/concatenate | solution.py:359
  1.5 0.8 %pad_add_fusion.meta_ref = s32[1,18]{1,0:T(1,128)S(1)} fusion(s32[1,4]{1,0:T(1,128)} %param.11, s32[1,8]{1,0:T(1,128)} %param.13, s32[1,6]{1,0:T(1,128)} %param.12), kind=kLoop, calls=%fused_computation.1 | loop fusion | flops 36 | bytes 144 | tf_op jit(solution)/shard_map/concatenate | solution.py:358
  2.3 0.0 copy-start.1
  2.3 0.9 %copy-done.1 = f32[1,4,48,48]{3,2,1,0:T(8,128)S(1)} copy-done((f32[1,4,48,48]{3,2,1,0:T(8,128)S(1)}, f32[1,4,48,48]{3,2,1,0:T(8,128)}, u32[]{:S(2)}) %copy-start.1) | copy-done | bytes 36888
  3.2 0.7 pack_setup.1
  3.9 5.1 %collective-permute-start = (bf16[272,128]{1,0:T(8,128)(2,1)S(1)}, bf16[272,128]{1,0:T(8,128)(2,1)S(1)}, u32[]{:S(2)}, u32[]{:S(2)}) collective-permute-start(bf16[272,128]{1,0:T(8,128)(2,1)S(1)} %get-tuple-element.22), channel_id=1, source_target_pairs={{0,22},{2,12},{4,26},{6,16},{8,30},{10,20},{12,2},{14,24},{16,6},{... | collective-permute-start | bytes 208904 | tf_op jit(solution)/shard_map/ppermute | solution.py:343
  9.0 1.3 %collective-permute-start.1 = (bf16[272,128]{1,0:T(8,128)(2,1)S(1)}, bf16[272,128]{1,0:T(8,128)(2,1)S(1)}, u32[]{:S(2)}, u32[]{:S(2)}) collective-permute-start(bf16[272,128]{1,0:T(8,128)(2,1)S(1)} %get-tuple-element.23), channel_id=1, source_target_pairs={{0,18},{2,16},{4,22},{6,20},{8,26},{10,24},{12,30},{14,28},{16,2},... | collective-permute-start | bytes 208904 | tf_op jit(solution)/shard_map/ppermute | solution.py:343
  10.2 1.0 %collective-permute-start.2 = (bf16[272,128]{1,0:T(8,128)(2,1)S(1)}, bf16[272,128]{1,0:T(8,128)(2,1)S(1)}, u32[]{:S(2)}, u32[]{:S(2)}) collective-permute-start(bf16[272,128]{1,0:T(8,128)(2,1)S(1)} %get-tuple-element.24), channel_id=1, source_target_pairs={{0,14},{2,20},{4,18},{6,24},{8,22},{10,28},{12,26},{14,0},{16,30},... | collective-permute-start | bytes 208904 | tf_op jit(solution)/shard_map/ppermute | solution.py:343
  11.3 2.2 %collective-permute-start.3 = (bf16[272,128]{1,0:T(8,128)(2,1)S(1)}, bf16[272,128]{1,0:T(8,128)(2,1)S(1)}, u32[]{:S(2)}, u32[]{:S(2)}) collective-permute-start(bf16[272,128]{1,0:T(8,128)(2,1)S(1)} %get-tuple-element.25), channel_id=1, source_target_pairs={{0,10},{2,24},{4,14},{6,28},{8,18},{10,0},{12,22},{14,4},{16,26},{... | collective-permute-start | bytes 208904 | tf_op jit(solution)/shard_map/ppermute | solution.py:343
  13.4 1.9 %collective-permute-start.4 = (bf16[272,128]{1,0:T(8,128)(2,1)S(1)}, bf16[272,128]{1,0:T(8,128)(2,1)S(1)}, u32[]{:S(2)}, u32[]{:S(2)}) collective-permute-start(bf16[272,128]{1,0:T(8,128)(2,1)S(1)} %get-tuple-element.26), channel_id=1, source_target_pairs={{0,6},{2,28},{4,10},{6,0},{8,14},{10,4},{12,18},{14,8},{16,22},{18... | collective-permute-start | bytes 208904 | tf_op jit(solution)/shard_map/ppermute | solution.py:343
  15.4 0.0 collective-permute-done.refs_0_.refs_1_
  15.4 2.2 %collective-permute-start.5 = (bf16[272,128]{1,0:T(8,128)(2,1)S(1)}, bf16[272,128]{1,0:T(8,128)(2,1)S(1)}, u32[]{:S(2)}, u32[]{:S(2)}) collective-permute-start(bf16[272,128]{1,0:T(8,128)(2,1)S(1)} %get-tuple-element.27), channel_id=1, source_target_pairs={{0,2},{2,0},{4,6},{6,4},{8,10},{10,8},{12,14},{14,12},{16,18},{18,... | collective-permute-start | bytes 208904 | tf_op jit(solution)/shard_map/ppermute | solution.py:343
  17.6 0.0 collective-permute-done.1.refs_1_.refs_2_
  17.6 2.4 %collective-permute-start.6 = (bf16[272,128]{1,0:T(8,128)(2,1)S(1)}, bf16[272,128]{1,0:T(8,128)(2,1)S(1)}, u32[]{:S(2)}, u32[]{:S(2)}) collective-permute-start(bf16[272,128]{1,0:T(8,128)(2,1)S(1)} %get-tuple-element.28.after_ref.refs_0_), channel_id=1, source_target_pairs={{0,1},{1,0},{2,3},{3,2},{4,5},{5,4},{6,7},{7,6},{8,9},{9,8},{10,11... | collective-permute-start | bytes 208904 | tf_op jit(solution)/shard_map/ppermute | solution.py:348
  19.9 0.0 copy-start
  19.9 1.6 %copy-done = bf16[1,1024,1024]{2,1,0:T(8,128)(2,1)S(1)} copy-done((bf16[1,1024,1024]{2,1,0:T(8,128)(2,1)S(1)}, bf16[1,1024,1024]{2,1,0:T(8,128)(2,1)}, u32[]{:S(2)}) %copy-start) | copy-done | bytes 2097176
  21.5 0.1 fetch_dual.1.refs_7_.dual_ref
  21.7 0.0 collective-permute-done.2.refs_2_.refs_3_
  21.7 0.0 collective-permute-done.3.refs_3_.refs_4_
  21.7 0.0 collective-permute-done.4.refs_4_.refs_5_
  21.7 0.4 collective-permute-done.5.refs_5_.refs_6_
  22.1 0.0 collective-permute-done.6.refs_6_.refs_7_
  22.1 0.7 %restrict_residual.1 = (f32[16,1024]{1,0:T(8,128)S(1)}, f32[32,8,128]{2,1,0:T(8,128)S(1)}) custom-call(s32[1,18]{1,0:T(1,128)S(1)} %pad_add_fusion.meta_ref, bf16[64,1024]{1,0:T(8,128)(2,1)S(1)} %pad_maximum_fusion.rows_ref, bf16[272,128]{1,0:T(8,128)(2,1)S(1)} %collective-permute-done.refs_0_.refs_1_, ...), custom_call_target="tpu_custom_call" | custom-call | tf_op jit(solution)/shard_map/restrict_residual/pallas_call | solution.py:315
  22.9 12.4 %all_to_all.20 = f32[32,8,128]{2,1,0:T(8,128)S(1)} all-to-all(f32[32,8,128]{2,1,0:T(8,128)S(1)} %get-tuple-element.29), channel_id=1, replica_groups=mesh['fine'=16,'coarse'=2] {'fine','coarse'}, dimensions={0} | all-to-all | bytes 262144 | tf_op jit(solution)/shard_map/all_to_all | solution.py:338
  35.3 1.7 %first_direction.1 = (bf16[32,16,128]{2,1,0:T(8,128)(2,1)S(1)}, f32[16,1024]{1,0:T(8,128)S(1)}, bf16[16,1024]{1,0:T(8,128)(2,1)S(1)}, f32[8,128]{1,0:T(8,128)S(1)}) custom-call(s32[1,18]{1,0:T(1,128)S(1)} %pad_add_fusion.meta_ref, f32[256,128]{1,0:T(8,128)S(1)} %bitcast.4, f32[16,1024]{1,0:T(8,128)S(1)} %get-tuple-element.30.residual_ref, ...), custom_call_target="tpu_custom_call" | custom-call | tf_op jit(solution)/shard_map/first_direction/pallas_call | solution.py:315
  37.0 10.0 %all_to_all.21.arrived_ref = bf16[32,16,128]{2,1,0:T(8,128)(2,1)S(1)} all-to-all(bf16[32,16,128]{2,1,0:T(8,128)(2,1)S(1)} %get-tuple-element.31), channel_id=1, replica_groups=mesh['fine'=16,'coarse'=2] {'fine','coarse'}, dimensions={0} | all-to-all | bytes 262144 | tf_op jit(solution)/shard_map/all_to_all | solution.py:338
  47.0 0.7 %restrict_image.1 = (f32[16,1024]{1,0:T(8,128)S(1)}, f32[32,8,128]{2,1,0:T(8,128)S(1)}) custom-call(s32[1,18]{1,0:T(1,128)S(1)} %pad_add_fusion.meta_ref, bf16[64,1024]{1,0:T(8,128)(2,1)S(1)} %pad_maximum_fusion.rows_ref, bf16[32,16,128]{2,1,0:T(8,128)(2,1)S(1)} %all_to_all.21.arrived_ref, bf16[16,1024]{1,0:T(8,128)(2,1)S(1)} %get-tuple-element.32.applied_ref, ...), custom_call_target="tpu_custom_call" | custom-call | tf_op jit(solution)/shard_map/restrict_image/pallas_call | solution.py:315
  47.7 10.0 %all_to_all.22 = f32[32,8,128]{2,1,0:T(8,128)S(1)} all-to-all(f32[32,8,128]{2,1,0:T(8,128)S(1)} %get-tuple-element.34), channel_id=1, replica_groups=mesh['fine'=16,'coarse'=2] {'fine','coarse'}, dimensions={0} | all-to-all | bytes 262144 | tf_op jit(solution)/shard_map/all_to_all | solution.py:338
  57.7 1.9 %second_direction.1 = (bf16[32,24,128]{2,1,0:T(8,128)(2,1)S(1)}, f32[16,1024]{1,0:T(8,128)S(1)}, f32[16,1024]{1,0:T(8,128)S(1)}, f32[16,1024]{1,0:T(8,128)S(1)}, bf16[16,1024]{1,0:T(8,128)(2,1)S(1)}) custom-call(s32[1,18]{1,0:T(1,128)S(1)} %pad_add_fusion.meta_ref, f32[256,128]{1,0:T(8,128)S(1)} %bitcast.5, f32[256,128]{1,0:T(8,128)S(1)} %bitcast.6, ...), custom_call_target="tpu_custom_call" | custom-call | tf_op jit(solution)/shard_map/second_direction/pallas_call | solution.py:315
  59.7 11.0 %all_to_all.23.arrived_ref = bf16[32,24,128]{2,1,0:T(8,128)(2,1)S(1)} all-to-all(bf16[32,24,128]{2,1,0:T(8,128)(2,1)S(1)} %get-tuple-element.37), channel_id=1, replica_groups=mesh['fine'=16,'coarse'=2] {'fine','coarse'}, dimensions={0} | all-to-all | bytes 393216 | tf_op jit(solution)/shard_map/all_to_all | solution.py:338
  70.7 1.5 %finish.1 = (f32[1,16,1024]{2,1,0:T(8,128)}, f32[1,16,1024]{2,1,0:T(8,128)}) custom-call(s32[1,18]{1,0:T(1,128)S(1)} %pad_add_fusion.meta_ref, bf16[32,24,128]{2,1,0:T(8,128)(2,1)S(1)} %all_to_all.23.arrived_ref, bf16[16,1024]{1,0:T(8,128)(2,1)S(1)} %get-tuple-element.38.applied_ref, f32[16,1024]{1,0:T(8,128)S(1)} %get-tuple-element.39.residual_ref, ...), custom_call_target="tpu_custom_call" | custom-call | tf_op jit(solution)/shard_map/finish/pallas_call | solution.py:315
Async XLA Ops:
  2.3 0.9 %copy-start.1 = (f32[1,4,48,48]{3,2,1,0:T(8,128)S(1)}, f32[1,4,48,48]{3,2,1,0:T(8,128)}, u32[]{:S(2)}) copy-start(f32[1,4,48,48]{3,2,1,0:T(8,128)} %factors_ref.1) | copy-start | bytes 110596
  3.9 11.5 %collective-permute-start = (bf16[272,128]{1,0:T(8,128)(2,1)S(1)}, bf16[272,128]{1,0:T(8,128)(2,1)S(1)}, u32[]{:S(2)}, u32[]{:S(2)}) collective-permute-start(bf16[272,128]{1,0:T(8,128)(2,1)S(1)} %get-tuple-element.22), channel_id=1, source_target_pairs={{0,22},{2,12},{4,26},{6,16},{8,30},{10,20},{12,2},{14,24},{16,6},{... | collective-permute-start | bytes 208904 | tf_op jit(solution)/shard_map/ppermute | solution.py:343
  9.0 8.6 %collective-permute-start.1 = (bf16[272,128]{1,0:T(8,128)(2,1)S(1)}, bf16[272,128]{1,0:T(8,128)(2,1)S(1)}, u32[]{:S(2)}, u32[]{:S(2)}) collective-permute-start(bf16[272,128]{1,0:T(8,128)(2,1)S(1)} %get-tuple-element.23), channel_id=1, source_target_pairs={{0,18},{2,16},{4,22},{6,20},{8,26},{10,24},{12,30},{14,28},{16,2},... | collective-permute-start | bytes 208904 | tf_op jit(solution)/shard_map/ppermute | solution.py:343
  10.2 11.4 %collective-permute-start.2 = (bf16[272,128]{1,0:T(8,128)(2,1)S(1)}, bf16[272,128]{1,0:T(8,128)(2,1)S(1)}, u32[]{:S(2)}, u32[]{:S(2)}) collective-permute-start(bf16[272,128]{1,0:T(8,128)(2,1)S(1)} %get-tuple-element.24), channel_id=1, source_target_pairs={{0,14},{2,20},{4,18},{6,24},{8,22},{10,28},{12,26},{14,0},{16,30},... | collective-permute-start | bytes 208904 | tf_op jit(solution)/shard_map/ppermute | solution.py:343
  11.3 10.4 %collective-permute-start.3 = (bf16[272,128]{1,0:T(8,128)(2,1)S(1)}, bf16[272,128]{1,0:T(8,128)(2,1)S(1)}, u32[]{:S(2)}, u32[]{:S(2)}) collective-permute-start(bf16[272,128]{1,0:T(8,128)(2,1)S(1)} %get-tuple-element.25), channel_id=1, source_target_pairs={{0,10},{2,24},{4,14},{6,28},{8,18},{10,0},{12,22},{14,4},{16,26},{... | collective-permute-start | bytes 208904 | tf_op jit(solution)/shard_map/ppermute | solution.py:343
  13.4 8.2 %collective-permute-start.4 = (bf16[272,128]{1,0:T(8,128)(2,1)S(1)}, bf16[272,128]{1,0:T(8,128)(2,1)S(1)}, u32[]{:S(2)}, u32[]{:S(2)}) collective-permute-start(bf16[272,128]{1,0:T(8,128)(2,1)S(1)} %get-tuple-element.26), channel_id=1, source_target_pairs={{0,6},{2,28},{4,10},{6,0},{8,14},{10,4},{12,18},{14,8},{16,22},{18... | collective-permute-start | bytes 208904 | tf_op jit(solution)/shard_map/ppermute | solution.py:343
  15.4 6.8 %collective-permute-start.5 = (bf16[272,128]{1,0:T(8,128)(2,1)S(1)}, bf16[272,128]{1,0:T(8,128)(2,1)S(1)}, u32[]{:S(2)}, u32[]{:S(2)}) collective-permute-start(bf16[272,128]{1,0:T(8,128)(2,1)S(1)} %get-tuple-element.27), channel_id=1, source_target_pairs={{0,2},{2,0},{4,6},{6,4},{8,10},{10,8},{12,14},{14,12},{16,18},{18,... | collective-permute-start | bytes 208904 | tf_op jit(solution)/shard_map/ppermute | solution.py:343
  17.6 4.6 %collective-permute-start.6 = (bf16[272,128]{1,0:T(8,128)(2,1)S(1)}, bf16[272,128]{1,0:T(8,128)(2,1)S(1)}, u32[]{:S(2)}, u32[]{:S(2)}) collective-permute-start(bf16[272,128]{1,0:T(8,128)(2,1)S(1)} %get-tuple-element.28.after_ref.refs_0_), channel_id=1, source_target_pairs={{0,1},{1,0},{2,3},{3,2},{4,5},{5,4},{6,7},{7,6},{8,9},{9,8},{10,11... | collective-permute-start | bytes 208904 | tf_op jit(solution)/shard_map/ppermute | solution.py:348
  19.9 1.6 %copy-start = (bf16[1,1024,1024]{2,1,0:T(8,128)(2,1)S(1)}, bf16[1,1024,1024]{2,1,0:T(8,128)(2,1)}, u32[]{:S(2)}) copy-start(bf16[1,1024,1024]{2,1,0:T(8,128)(2,1)} %dual_ref.1) | copy-start | bytes 6291460

commit v3 on v2

--- a/solution.py
+++ b/solution.py
@@ -134,31 +134,102 @@
         scratch_ref[slot] = near_refs[slot][span, :]
     facing = [scratch_ref[slot_of(sizes, meta_ref[0, b])] for b in range(PLANES)]
     facing += [near_refs[PLANES][span, :], near_refs[-1][span, :]]
-    restrict(meta_ref, rows_ref[:cases, :], facing, rows_ref[cases:, :], None, out_ref, message_ref)
-
-
-def restrict_kernel(sizes, meta_ref, rows_ref, arrived_ref, applied_ref, sums_ref, out_ref, message_ref):
-    facing = [arrived_ref[target] for target in facing_subs(sizes, meta_ref)]
-    cases = out_ref.shape[0]
-    restrict(meta_ref, applied_ref[...], facing, rows_ref[cases:, :], sums_ref[...], out_ref, message_ref)
-
-
-def restrict(meta_ref, mine, facing, basis, sums, out_ref, message_ref):
+    restrict(meta_ref, rows_ref[:cases, :], facing, rows_ref[cases:, :], out_ref, message_ref)
+
+
+def twice(basis):
+    gap = jnp.zeros((HALF - basis.shape[0], basis.shape[1]), BF16)
+    return jnp.concatenate([basis, gap, basis, gap], axis=0)
+
+
+def times_basis(rows, doubled):
+    return lax.dot_general(rows, doubled, (((1,), (1,)), ((), ())), preferred_element_type=F32)
+
+
+def fold(coefficients):
+    half = coefficients.shape[0] // 2
+    return jnp.where(lane_ids(half) < HALF, coefficients[:half], coefficients[half:])
+
+
+def encode(sums):
+    top = sums.astype(BF16).astype(F32)
+    middle = (sums - top).astype(BF16).astype(F32)
+    bottom = sums - top - middle
+    return top + pltpu.roll(middle, 2, 1) + pltpu.roll(bottom, 4, 1)
+
+
+def decode(totals):
+    return totals + pltpu.roll(totals, LANES - 2, 1) + pltpu.roll(totals, LANES - 4, 1)
+
+
+def restrict(meta_ref, mine, facing, basis, out_ref, message_ref):
     cases = mine.shape[0]
-    modes = basis.shape[0]
     result, ours, theirs = difference(meta_ref, mine, facing)
     for block, values in enumerate(result):
         out_ref[:, block * LANES : (block + 1) * LANES] = values
     both = jnp.concatenate([jnp.concatenate(ours, axis=1), jnp.concatenate(theirs, axis=1)], axis=0)
-    gap = jnp.zeros((HALF - modes, basis.shape[1]), BF16)
-    twice = jnp.concatenate([basis, gap, basis, gap], axis=0)
-    coefficients = lax.dot_general(both, twice, (((1,), (1,)), ((), ())), preferred_element_type=F32)
-    coefficients = coefficients[:cases] - coefficients[cases:]
+    coefficients = times_basis(both, twice(basis))
+    message = fold(coefficients[:cases] - coefficients[cases:])
+    message_ref[...] = jnp.broadcast_to(message[None], message_ref.shape)
+
+
+def shares(sizes, dims, layers, meta_ref, applied_ref, near_refs, rows_ref, sums):
+    cases = applied_ref.shape[0]
+    span = layout_of(*dims)["basis"]
+    masked = []
+    for block in range(PLANES + 2):
+        part = applied_ref[:, block * LANES : (block + 1) * LANES].astype(F32)
+        masked.append((part * live_mask(meta_ref, block)).astype(BF16))
+    own = fold(times_basis(jnp.concatenate(masked, axis=1), twice(rows_ref[cases:, :])))
+    high = own.astype(BF16).astype(F32)
+    tiles = [high + encode(sums), own - high]
+    for near_ref, block in zip(near_refs[1:], wanted_blocks(sizes, layers, meta_ref)):
+        part = applied_ref[:, lanes_of(block)].astype(F32) * live_mask(meta_ref, block)
+        tiles.append(fold(times_basis(part.astype(BF16), twice(near_ref[span, :]))))
+    return jnp.concatenate(tiles, axis=0).astype(BF16)
+
+
+def collect(sizes, layers, cases, own_ref, others_ref, changes_ref):
+    fine_count, coarse_count = sizes
     half = cases // 2
-    message = jnp.where(lane_ids(half) < HALF, coefficients[:half], coefficients[half:])
-    if sums is not None:
-        message = message + sums
-    message_ref[...] = jnp.broadcast_to(message[None], message_ref.shape)
+    coarse = lax.axis_index("coarse")
+
+    def tile(layer, fine, index):
+        rows = slice(cases + index * half, cases + (index + 1) * half)
+        if layers == 1:
+            source = own_ref if layer == 0 else others_ref
+            return source[fine, rows, :].astype(F32)
+        return others_ref[layer, fine, rows, :].astype(F32)
+
+    def one(fine, totals):
+        for layer in range(coarse_count):
+            first = tile(layer, fine, 0)
+            totals = totals + first
+            value = first + tile(layer, fine, 1)
+            for slot in range(PLANES):
+                distance = 2 * (PLANES - slot) - 1
+                partner = jnp.where(fine % 2 == 0, fine + distance, fine - distance) if layers > 1 else (
+                    fine + distance if fine % 2 == 0 else fine - distance
+                )
+                value = value - tile(layer, (partner + fine_count) % fine_count, 2 + slot)
+            if layers == 1:
+                value = value - tile(1 - layer, fine, 2 + PLANES)
+                place = fine * 2 + (coarse if layer == 0 else 1 - coarse)
+            else:
+                if layer > 0:
+                    value = value - tile(layer - 1, fine, 3 + PLANES)
+                if layer < coarse_count - 1:
+                    value = value - tile(layer + 1, fine, 2 + PLANES)
+                place = fine * coarse_count + layer
+            changes_ref[place] = value
+        return totals
+
+    totals = jnp.zeros((half, LANES), F32)
+    if layers > 1:
+        return decode(lax.fori_loop(0, fine_count, one, totals))
+    for fine in range(fine_count):
+        totals = one(fine, totals)
+    return decode(totals)
 
 
 def solve(coeffs, near, terms, modes):
@@ -240,16 +311,21 @@
     return applied, sums
 
 
-def first_kernel(sizes, dims, count, meta_ref, coeffs_ref, residual_ref, rows_ref, dual_ref, *refs):
+def first_kernel(sizes, dims, layers, count, meta_ref, coeffs_ref, residual_ref, rows_ref, dual_ref, *refs):
     near_refs = refs[:count]
-    message_ref, direction_ref, applied_ref, sums_ref, theirs_ref = refs[count:]
+    message_ref, direction_ref, applied_ref, theirs_ref = refs[count:]
     applied, sums = advance(
         sizes, dims, meta_ref, coeffs_ref[...], residual_ref[...], near_refs, rows_ref, dual_ref, theirs_ref,
         direction_ref, applied_ref,
     )
-    message_ref[...] = jnp.zeros_like(message_ref)
-    post_blocks(message_ref, facing_subs(sizes, meta_ref), applied)
-    sums_ref[...] = sums
+    cases = applied.shape[0]
+    tiles = shares(sizes, dims, layers, meta_ref, applied_ref, near_refs, rows_ref, sums)
+    message_ref[:, :cases, :] = jnp.zeros((message_ref.shape[0], cases, LANES), BF16)
+    message_ref[:, cases:, :] = jnp.broadcast_to(tiles[None], (message_ref.shape[0],) + tiles.shape)
+    post_blocks(message_ref, [meta_ref[0, b] for b in range(PLANES)], applied)
+    if layers == 1:
+        block = wanted_blocks(sizes, layers, meta_ref)[-1]
+        message_ref[lax.axis_index("fine"), :cases, :] = applied_ref[:, lanes_of(block)]
 
 
 def steps_from(totals):
@@ -258,29 +334,31 @@
     return low, high
 
 
-def second_kernel(sizes, dims, count, meta_ref, coeffs_ref, change_ref, residual_ref, image_ref, before_ref, rows_ref,
-                  dual_ref, *refs):
+def second_kernel(sizes, dims, layers, count, meta_ref, coeffs_ref, residual_ref, before_ref, applied_before_ref,
+                  rows_ref, dual_ref, own_ref, *refs):
+    others_refs, refs = refs[: 1 if layers == 1 else 3], refs[1 if layers == 1 else 3 :]
     near_refs = refs[:count]
-    message_ref, residual_out, multipliers_out, direction_ref, applied_ref, theirs_ref = refs[count:]
-    half = residual_ref.shape[0] // 2
-    change = change_ref[...].reshape(-1, half, LANES)
-    low, high = steps_from(jnp.sum(change, axis=0))
+    message_ref, residual_out, multipliers_out, direction_ref, applied_ref, theirs_ref, changes_ref = refs[count:]
+    cases = residual_ref.shape[0]
+    half = cases // 2
+    low, high = steps_from(collect(sizes, layers, cases, own_ref, others_refs[0], changes_ref))
     step = jnp.concatenate([low, high], axis=0)
     packed_step = jnp.where(lane_ids(half) < HALF, low, high)
-    coeffs = coeffs_ref[...] - (change * packed_step[None]).reshape(coeffs_ref.shape)
-    residual = residual_ref[...] - step * image_ref[...]
+    coeffs = coeffs_ref[...] - (changes_ref[...] * packed_step[None]).reshape(coeffs_ref.shape)
+    facing = [own_ref[meta_ref[0, b], :cases, :] for b in range(PLANES)]
+    if layers == 1:
+        facing += [others_refs[0][lax.axis_index("fine"), :cases, :]] * 2
+    else:
+        facing += [ref[...] for ref in others_refs[1:]]
+    image, _, _ = difference(meta_ref, applied_before_ref[...], facing)
+    residual = residual_ref[...] - step * jnp.concatenate(image, axis=1)
     residual_out[...] = residual
     multipliers_out[...] = step * before_ref[...]
     applied, sums = advance(
         sizes, dims, meta_ref, coeffs, residual, near_refs, rows_ref, dual_ref, theirs_ref, direction_ref, applied_ref
     )
-    top = sums.astype(BF16).astype(F32)
-    middle = (sums - top).astype(BF16).astype(F32)
-    bottom = sums - top - middle
-    coded = (top + pltpu.roll(middle, 2, 1) + pltpu.roll(bottom, 4, 1)).astype(BF16)
-    cases = applied.shape[0]
     message_ref[:, :cases, :] = jnp.zeros((message_ref.shape[0], cases, LANES), BF16)
-    message_ref[:, cases:, :] = jnp.broadcast_to(coded[None], (message_ref.shape[0], half, LANES))
+    message_ref[:, cases:, :] = jnp.broadcast_to(encode(sums).astype(BF16)[None], (message_ref.shape[0], half, LANES))
     post_blocks(message_ref, facing_subs(sizes, meta_ref), applied)
 
 
@@ -288,8 +366,7 @@
                 multipliers_out, residual_out):
     cases = applied_ref.shape[0]
     totals = jnp.sum(arrived_ref[:, cases:, :].astype(F32), axis=0)
-    totals = totals + pltpu.roll(totals, LANES - 2, 1) + pltpu.roll(totals, LANES - 4, 1)
-    step = jnp.concatenate(steps_from(totals), axis=0)
+    step = jnp.concatenate(steps_from(decode(totals)), axis=0)
     facing = [arrived_ref[target, :cases, :] for target in facing_subs(sizes, meta_ref)]
     image, _, _ = difference(meta_ref, applied_ref[...], facing)
     fine = lax.axis_index("fine")
@@ -382,30 +459,31 @@
     )
     coeffs = swap_all(message).reshape(subs * half, LANES)
 
-    message, direction, applied, sums = call(
-        functools.partial(first_kernel, sizes, dims, count),
+    tiles = 2 + PLANES + layers
+    message, direction, applied = call(
+        functools.partial(first_kernel, sizes, dims, layers, count),
         "first_direction",
         (meta,),
         (coeffs, residual, rows, dual, *near),
-        [((subs, cases, LANES), BF16), full, half_full, ((half, LANES), F32)],
+        [((fine_count, cases + tiles * half, LANES), BF16), full, half_full],
         theirs,
     )
-    image, message = call(
-        functools.partial(restrict_kernel, sizes),
-        "restrict_image",
-        (meta,),
-        (rows, swap_all(message), applied, sums),
-        [full, coded],
-    )
-    change = swap_all(message).reshape(subs * half, LANES)
+    own = lax.all_to_all(message, "fine", 0, 0, tiled=True)
+    if layers == 1:
+        others = [lax.ppermute(own, "coarse", [(0, 1), (1, 0)])]
+    else:
+        up = [(i, i + 1) for i in range(coarse_count - 1)]
+        lower = lax.ppermute(applied[:, (PLANES + 1) * LANES :], "coarse", up)
+        upper = lax.ppermute(applied[:, PLANES * LANES : (PLANES + 1) * LANES], "coarse", [(j, i) for i, j in up])
+        others = [lax.all_gather(own, "coarse"), lower, upper]
 
     message, residual, multipliers, direction, applied = call(
-        functools.partial(second_kernel, sizes, dims, count),
+        functools.partial(second_kernel, sizes, dims, layers, count),
         "second_direction",
         (meta,),
-        (coeffs, change, residual, image, direction, rows, dual, *near),
+        (coeffs, residual, direction, applied, rows, dual, own, *others, *near),
         [((subs, cases + half, LANES), BF16), full, full, full, half_full],
-        theirs,
+        theirs + [pltpu.VMEM((subs, half, LANES), F32)],
     )
     arrived = swap_all(message)
     out = ((1, cases, width), F32)

time: 72.5 us -> 69.4 us (0.957)
  blocking collectives: 43.5 us -> 36.9 us
  starting transfers between devices: 16 us -> 18.7 us
  waiting for transfers between devices: 0.46 us -> 1.77 us
    all_to_all x4 -> x2, blocking collectives: 43.5 us -> 24.1 us  [swap_all(): return lax.all_to_all(message, AXES, 0, 0, tiled=True)]
    all_to_all x0 -> x1, blocking collectives: none -> 12.8 us  [body(): own = lax.all_to_all(message, 'fine', 0, 0, tiled=True)]
    ppermute x0 -> x1, starting transfers between devices: none -> 2.66 us  [body(): others = [lax.ppermute(own, 'coarse', [(0, 1), (1, 0)])]]
    ppermute x0 -> x1, waiting for transfers between devices: none -> 1.3 us  [body(): others = [lax.ppermute(own, 'coarse', [(0, 1), (1, 0)])]]
    pallas_call x7 -> x6, Pallas kernels: 7.4 us -> 6.93 us  [call(): pl.pallas_call(kernel, name=name, out_shape=[jax.ShapeDtypeStruct(shape,...]
  transfers between devices with their start and end apart: 7 -> 8, of which waited for: 1 -> 2; matrix products, arithmetic and copies ran while one was open for 0% -> 0% of each run, Pallas kernels for 0% -> 0%
where the time goes in v3:
time: 69.4 us; the launch traced here: 69.2 us
  blocking collectives  36.9 us (53%)
  starting transfers between devices  18.7 us (27%)
  Pallas kernels  6.93 us (10%)
  local copies, waits for them, and re-layouts  2.48 us (4%)
  waiting for transfers between devices  1.77 us (3%)
  other arithmetic  1.67 us (2%)
  between operations  0.7 us (1%)
    all_to_all x2, blocking collectives, swap_all(): return lax.all_to_all(message, AXES, 0, 0, tiled=True)  24.1 us
    ppermute x6, starting transfers between devices, swap_slot(): return lax.ppermute(message, 'fine', pairs)  13.7 us
    all_to_all x1, blocking collectives, body(): own = lax.all_to_all(message, 'fine', 0, 0, tiled=True)  12.8 us
    pallas_call x6, Pallas kernels, call(): pl.pallas_call(kernel, name=name, out_shape=[jax.ShapeDtypeStruct(shape,...  6.93 us
    ppermute x1, starting transfers between devices, body(): others = [lax.ppermute(own, 'coarse', [(0, 1), (1, 0)])]  2.66 us
    unnamed x4, local copies, waits for them, and re-layouts  2.48 us
    ppermute x1, starting transfers between devices, swap_blocks(): lax.ppermute(messages[PLANES], 'coarse', [(0, 1), (1, 0)])  2.36 us
  transfers between devices with their start and end apart: 8, of which 2 were waited for; matrix products, arithmetic and copies ran while one was open for 0% of the time, Pallas kernels for 0%

profile of v3, /device:TPU:1, one launch (start us, length us, event | category | flops | bytes accessed | tf_op | source)
XLA Modules:
  0.0 69.2 jit_solution(6216850644905672919)
XLA Ops:
  0.6 0.9 %pad_maximum_fusion.rows_ref = bf16[64,1024]{1,0:T(8,128)(2,1)S(1)} fusion(bf16[48,1024]{1,0:T(8,128)(2,1)} %bitcast.5, bf16[16,1024]{1,0:T(8,128)(2,1)} %bitcast.6), kind=kLoop, calls=%fused_computation | loop fusion | flops 262144 | bytes 262144 | tf_op jit(solution)/shard_map/concatenate | solution.py:436
  1.5 0.8 %pad_add_fusion.meta_ref = s32[1,18]{1,0:T(1,128)S(1)} fusion(s32[1,4]{1,0:T(1,128)} %param.11, s32[1,8]{1,0:T(1,128)} %param.13, s32[1,6]{1,0:T(1,128)} %param.12), kind=kLoop, calls=%fused_computation.1 | loop fusion | flops 36 | bytes 144 | tf_op jit(solution)/shard_map/concatenate | solution.py:435
  2.3 0.0 copy-start.1
  2.3 0.9 %copy-done.1 = f32[1,4,48,48]{3,2,1,0:T(8,128)S(1)} copy-done((f32[1,4,48,48]{3,2,1,0:T(8,128)S(1)}, f32[1,4,48,48]{3,2,1,0:T(8,128)}, u32[]{:S(2)}) %copy-start.1) | copy-done | bytes 36888
  3.2 0.7 pack_setup.1
  3.9 5.1 %collective-permute-start = (bf16[272,128]{1,0:T(8,128)(2,1)S(1)}, bf16[272,128]{1,0:T(8,128)(2,1)S(1)}, u32[]{:S(2)}, u32[]{:S(2)}) collective-permute-start(bf16[272,128]{1,0:T(8,128)(2,1)S(1)} %get-tuple-element.19), channel_id=1, source_target_pairs={{0,22},{2,12},{4,26},{6,16},{8,30},{10,20},{12,2},{14,24},{16,6},{... | collective-permute-start | bytes 208904 | tf_op jit(solution)/shard_map/ppermute | solution.py:420
  9.0 1.3 %collective-permute-start.1 = (bf16[272,128]{1,0:T(8,128)(2,1)S(1)}, bf16[272,128]{1,0:T(8,128)(2,1)S(1)}, u32[]{:S(2)}, u32[]{:S(2)}) collective-permute-start(bf16[272,128]{1,0:T(8,128)(2,1)S(1)} %get-tuple-element.20), channel_id=1, source_target_pairs={{0,18},{2,16},{4,22},{6,20},{8,26},{10,24},{12,30},{14,28},{16,2},... | collective-permute-start | bytes 208904 | tf_op jit(solution)/shard_map/ppermute | solution.py:420
  10.2 1.0 %collective-permute-start.2 = (bf16[272,128]{1,0:T(8,128)(2,1)S(1)}, bf16[272,128]{1,0:T(8,128)(2,1)S(1)}, u32[]{:S(2)}, u32[]{:S(2)}) collective-permute-start(bf16[272,128]{1,0:T(8,128)(2,1)S(1)} %get-tuple-element.21), channel_id=1, source_target_pairs={{0,14},{2,20},{4,18},{6,24},{8,22},{10,28},{12,26},{14,0},{16,30},... | collective-permute-start | bytes 208904 | tf_op jit(solution)/shard_map/ppermute | solution.py:420
  11.3 2.2 %collective-permute-start.3 = (bf16[272,128]{1,0:T(8,128)(2,1)S(1)}, bf16[272,128]{1,0:T(8,128)(2,1)S(1)}, u32[]{:S(2)}, u32[]{:S(2)}) collective-permute-start(bf16[272,128]{1,0:T(8,128)(2,1)S(1)} %get-tuple-element.22), channel_id=1, source_target_pairs={{0,10},{2,24},{4,14},{6,28},{8,18},{10,0},{12,22},{14,4},{16,26},{... | collective-permute-start | bytes 208904 | tf_op jit(solution)/shard_map/ppermute | solution.py:420
  13.4 1.9 %collective-permute-start.4 = (bf16[272,128]{1,0:T(8,128)(2,1)S(1)}, bf16[272,128]{1,0:T(8,128)(2,1)S(1)}, u32[]{:S(2)}, u32[]{:S(2)}) collective-permute-start(bf16[272,128]{1,0:T(8,128)(2,1)S(1)} %get-tuple-element.23), channel_id=1, source_target_pairs={{0,6},{2,28},{4,10},{6,0},{8,14},{10,4},{12,18},{14,8},{16,22},{18... | collective-permute-start | bytes 208904 | tf_op jit(solution)/shard_map/ppermute | solution.py:420
  15.4 0.0 collective-permute-done.refs_0_.refs_1_.refs_2_
  15.4 2.2 %collective-permute-start.5 = (bf16[272,128]{1,0:T(8,128)(2,1)S(1)}, bf16[272,128]{1,0:T(8,128)(2,1)S(1)}, u32[]{:S(2)}, u32[]{:S(2)}) collective-permute-start(bf16[272,128]{1,0:T(8,128)(2,1)S(1)} %get-tuple-element.24), channel_id=1, source_target_pairs={{0,2},{2,0},{4,6},{6,4},{8,10},{10,8},{12,14},{14,12},{16,18},{18,... | collective-permute-start | bytes 208904 | tf_op jit(solution)/shard_map/ppermute | solution.py:420
  17.6 0.0 collective-permute-done.1.refs_1_.refs_2_.refs_3_
  17.6 2.4 %collective-permute-start.6 = (bf16[272,128]{1,0:T(8,128)(2,1)S(1)}, bf16[272,128]{1,0:T(8,128)(2,1)S(1)}, u32[]{:S(2)}, u32[]{:S(2)}) collective-permute-start(bf16[272,128]{1,0:T(8,128)(2,1)S(1)} %get-tuple-element.25.after_ref.refs_0_.refs_1_), channel_id=1, source_target_pairs={{0,1},{1,0},{2,3},{3,2},{4,5},{5,4},{6,7},{7,6},{8,9},{9,8},{10,11... | collective-permute-start | bytes 208904 | tf_op jit(solution)/shard_map/ppermute | solution.py:425
  19.9 0.0 copy-start
  19.9 1.6 %copy-done = bf16[1,1024,1024]{2,1,0:T(8,128)(2,1)S(1)} copy-done((bf16[1,1024,1024]{2,1,0:T(8,128)(2,1)S(1)}, bf16[1,1024,1024]{2,1,0:T(8,128)(2,1)}, u32[]{:S(2)}) %copy-start) | copy-done | bytes 2097176
  21.5 0.1 fetch_dual.1.refs_7_.dual_ref
  21.7 0.0 collective-permute-done.2.refs_2_.refs_3_.refs_4_
  21.7 0.0 collective-permute-done.3.refs_3_.refs_4_.refs_5_
  21.7 0.0 collective-permute-done.4.refs_4_.refs_5_.refs_6_
  21.7 0.4 collective-permute-done.5.refs_5_.refs_6_.refs_7_
  22.1 0.0 collective-permute-done.6.refs_6_.refs_7_.refs_8_
  22.1 0.7 %restrict_residual.1 = (f32[16,1024]{1,0:T(8,128)S(1)}, f32[32,8,128]{2,1,0:T(8,128)S(1)}) custom-call(s32[1,18]{1,0:T(1,128)S(1)} %pad_add_fusion.meta_ref, bf16[64,1024]{1,0:T(8,128)(2,1)S(1)} %pad_maximum_fusion.rows_ref, bf16[272,128]{1,0:T(8,128)(2,1)S(1)} %collective-permute-done.refs_0_.refs_1_.refs_2_, ...), custom_call_target="tpu_custom_call" | custom-call | tf_op jit(solution)/shard_map/restrict_residual/pallas_call | solution.py:392
  22.9 12.4 %all_to_all.15 = f32[32,8,128]{2,1,0:T(8,128)S(1)} all-to-all(f32[32,8,128]{2,1,0:T(8,128)S(1)} %get-tuple-element.26), channel_id=1, replica_groups=mesh['fine'=16,'coarse'=2] {'fine','coarse'}, dimensions={0} | all-to-all | bytes 262144 | tf_op jit(solution)/shard_map/all_to_all | solution.py:415
  35.3 1.8 %first_direction.1 = (bf16[16,88,128]{2,1,0:T(8,128)(2,1)S(1)}, f32[16,1024]{1,0:T(8,128)S(1)}, bf16[16,1024]{1,0:T(8,128)(2,1)S(1)}) custom-call(s32[1,18]{1,0:T(1,128)S(1)} %pad_add_fusion.meta_ref, f32[256,128]{1,0:T(8,128)S(1)} %bitcast.3, f32[16,1024]{1,0:T(8,128)S(1)} %get-tuple-element.27.residual_ref, bf16[64,1024]{1,0:T(8,128)(2,1)S(1)} %pad_maximum_fusion.rows_ref, ...), custom_call_target="tpu_custom_call" | custom-call | tf_op jit(solution)/shard_map/first_direction/pallas_call | solution.py:392
  37.1 12.8 %all_to_all.16.own_ref = bf16[16,88,128]{2,1,0:T(8,128)(2,1)S(1)} all-to-all(bf16[16,88,128]{2,1,0:T(8,128)(2,1)S(1)} %get-tuple-element.30), channel_id=1, replica_groups=mesh['fine'=16,'coarse'=2] {'fine'}, dimensions={0} | all-to-all | bytes 720896 | tf_op jit(solution)/shard_map/all_to_all | solution.py:471
  50.0 2.7 %collective-permute-start.7 = (bf16[16,88,128]{2,1,0:T(8,128)(2,1)S(1)}, bf16[16,88,128]{2,1,0:T(8,128)(2,1)S(1)}, u32[]{:S(2)}, u32[]{:S(2)}) collective-permute-start(bf16[16,88,128]{2,1,0:T(8,128)(2,1)S(1)} %all_to_all.16.own_ref), channel_id=1, source_target_pairs={{0,1},{1,0},{2,3},{3,2},{4,5},{5,4},{6,7},{7,6},{8,9},{9,8},{10,11... | collective-permute-start | bytes 1081352 | tf_op jit(solution)/shard_map/ppermute | solution.py:473
  52.6 1.3 %collective-permute-done.7.refs_0_ = bf16[16,88,128]{2,1,0:T(8,128)(2,1)S(1)} collective-permute-done((bf16[16,88,128]{2,1,0:T(8,128)(2,1)S(1)}, bf16[16,88,128]{2,1,0:T(8,128)(2,1)S(1)}, u32[]{:S(2)}, u32[]{:S(2)}) %collective-permute-start.7) | collective-permute-done | bytes 360480 | tf_op jit(solution)/shard_map/ppermute | solution.py:473
  53.9 2.0 %second_direction.1 = (bf16[32,24,128]{2,1,0:T(8,128)(2,1)S(1)}, f32[16,1024]{1,0:T(8,128)S(1)}, f32[16,1024]{1,0:T(8,128)S(1)}, f32[16,1024]{1,0:T(8,128)S(1)}, bf16[16,1024]{1,0:T(8,128)(2,1)S(1)}) custom-call(s32[1,18]{1,0:T(1,128)S(1)} %pad_add_fusion.meta_ref, f32[256,128]{1,0:T(8,128)S(1)} %bitcast.4, f32[16,1024]{1,0:T(8,128)S(1)} %get-tuple-element.27.residual_ref, ...), custom_call_target="tpu_custom_call" | custom-call | tf_op jit(solution)/shard_map/second_direction/pallas_call | solution.py:392
  56.0 11.7 %all_to_all.17.arrived_ref = bf16[32,24,128]{2,1,0:T(8,128)(2,1)S(1)} all-to-all(bf16[32,24,128]{2,1,0:T(8,128)(2,1)S(1)} %get-tuple-element.31), channel_id=1, replica_groups=mesh['fine'=16,'coarse'=2] {'fine','coarse'}, dimensions={0} | all-to-all | bytes 393216 | tf_op jit(solution)/shard_map/all_to_all | solution.py:415
  67.6 1.5 %finish.1 = (f32[1,16,1024]{2,1,0:T(8,128)}, f32[1,16,1024]{2,1,0:T(8,128)}) custom-call(s32[1,18]{1,0:T(1,128)S(1)} %pad_add_fusion.meta_ref, bf16[32,24,128]{2,1,0:T(8,128)(2,1)S(1)} %all_to_all.17.arrived_ref, bf16[16,1024]{1,0:T(8,128)(2,1)S(1)} %get-tuple-element.32.applied_ref, f32[16,1024]{1,0:T(8,128)S(1)} %get-tuple-element.33.residual_ref, ...), custom_call_target="tpu_custom_call" | custom-call | tf_op jit(solution)/shard_map/finish/pallas_call | solution.py:392
Async XLA Ops:
  2.3 0.9 %copy-start.1 = (f32[1,4,48,48]{3,2,1,0:T(8,128)S(1)}, f32[1,4,48,48]{3,2,1,0:T(8,128)}, u32[]{:S(2)}) copy-start(f32[1,4,48,48]{3,2,1,0:T(8,128)} %factors_ref.1) | copy-start | bytes 110596
  3.9 11.5 %collective-permute-start = (bf16[272,128]{1,0:T(8,128)(2,1)S(1)}, bf16[272,128]{1,0:T(8,128)(2,1)S(1)}, u32[]{:S(2)}, u32[]{:S(2)}) collective-permute-start(bf16[272,128]{1,0:T(8,128)(2,1)S(1)} %get-tuple-element.19), channel_id=1, source_target_pairs={{0,22},{2,12},{4,26},{6,16},{8,30},{10,20},{12,2},{14,24},{16,6},{... | collective-permute-start | bytes 208904 | tf_op jit(solution)/shard_map/ppermute | solution.py:420
  9.0 8.6 %collective-permute-start.1 = (bf16[272,128]{1,0:T(8,128)(2,1)S(1)}, bf16[272,128]{1,0:T(8,128)(2,1)S(1)}, u32[]{:S(2)}, u32[]{:S(2)}) collective-permute-start(bf16[272,128]{1,0:T(8,128)(2,1)S(1)} %get-tuple-element.20), channel_id=1, source_target_pairs={{0,18},{2,16},{4,22},{6,20},{8,26},{10,24},{12,30},{14,28},{16,2},... | collective-permute-start | bytes 208904 | tf_op jit(solution)/shard_map/ppermute | solution.py:420
  10.2 11.4 %collective-permute-start.2 = (bf16[272,128]{1,0:T(8,128)(2,1)S(1)}, bf16[272,128]{1,0:T(8,128)(2,1)S(1)}, u32[]{:S(2)}, u32[]{:S(2)}) collective-permute-start(bf16[272,128]{1,0:T(8,128)(2,1)S(1)} %get-tuple-element.21), channel_id=1, source_target_pairs={{0,14},{2,20},{4,18},{6,24},{8,22},{10,28},{12,26},{14,0},{16,30},... | collective-permute-start | bytes 208904 | tf_op jit(solution)/shard_map/ppermute | solution.py:420
  11.3 10.4 %collective-permute-start.3 = (bf16[272,128]{1,0:T(8,128)(2,1)S(1)}, bf16[272,128]{1,0:T(8,128)(2,1)S(1)}, u32[]{:S(2)}, u32[]{:S(2)}) collective-permute-start(bf16[272,128]{1,0:T(8,128)(2,1)S(1)} %get-tuple-element.22), channel_id=1, source_target_pairs={{0,10},{2,24},{4,14},{6,28},{8,18},{10,0},{12,22},{14,4},{16,26},{... | collective-permute-start | bytes 208904 | tf_op jit(solution)/shard_map/ppermute | solution.py:420
  13.4 8.2 %collective-permute-start.4 = (bf16[272,128]{1,0:T(8,128)(2,1)S(1)}, bf16[272,128]{1,0:T(8,128)(2,1)S(1)}, u32[]{:S(2)}, u32[]{:S(2)}) collective-permute-start(bf16[272,128]{1,0:T(8,128)(2,1)S(1)} %get-tuple-element.23), channel_id=1, source_target_pairs={{0,6},{2,28},{4,10},{6,0},{8,14},{10,4},{12,18},{14,8},{16,22},{18... | collective-permute-start | bytes 208904 | tf_op jit(solution)/shard_map/ppermute | solution.py:420
  15.4 6.8 %collective-permute-start.5 = (bf16[272,128]{1,0:T(8,128)(2,1)S(1)}, bf16[272,128]{1,0:T(8,128)(2,1)S(1)}, u32[]{:S(2)}, u32[]{:S(2)}) collective-permute-start(bf16[272,128]{1,0:T(8,128)(2,1)S(1)} %get-tuple-element.24), channel_id=1, source_target_pairs={{0,2},{2,0},{4,6},{6,4},{8,10},{10,8},{12,14},{14,12},{16,18},{18,... | collective-permute-start | bytes 208904 | tf_op jit(solution)/shard_map/ppermute | solution.py:420
  17.6 4.6 %collective-permute-start.6 = (bf16[272,128]{1,0:T(8,128)(2,1)S(1)}, bf16[272,128]{1,0:T(8,128)(2,1)S(1)}, u32[]{:S(2)}, u32[]{:S(2)}) collective-permute-start(bf16[272,128]{1,0:T(8,128)(2,1)S(1)} %get-tuple-element.25.after_ref.refs_0_.refs_1_), channel_id=1, source_target_pairs={{0,1},{1,0},{2,3},{3,2},{4,5},{5,4},{6,7},{7,6},{8,9},{9,8},{10,11... | collective-permute-start | bytes 208904 | tf_op jit(solution)/shard_map/ppermute | solution.py:425
  19.9 1.6 %copy-start = (bf16[1,1024,1024]{2,1,0:T(8,128)(2,1)S(1)}, bf16[1,1024,1024]{2,1,0:T(8,128)(2,1)}, u32[]{:S(2)}) copy-start(bf16[1,1024,1024]{2,1,0:T(8,128)(2,1)} %dual_ref.1) | copy-start | bytes 6291460
  50.0 4.0 %collective-permute-start.7 = (bf16[16,88,128]{2,1,0:T(8,128)(2,1)S(1)}, bf16[16,88,128]{2,1,0:T(8,128)(2,1)S(1)}, u32[]{:S(2)}, u32[]{:S(2)}) collective-permute-start(bf16[16,88,128]{2,1,0:T(8,128)(2,1)S(1)} %all_to_all.16.own_ref), channel_id=1, source_target_pairs={{0,1},{1,0},{2,3},{3,2},{4,5},{5,4},{6,7},{7,6},{8,9},{9,8},{10,11... | collective-permute-start | bytes 1081352 | tf_op jit(solution)/shard_map/ppermute | solution.py:473

commit v4 on v3

--- a/solution.py
+++ b/solution.py
@@ -67,6 +67,23 @@
     cases = rows.shape[0]
     for block, target in enumerate(targets):
         out_ref[target, :cases, :] = rows[:, block * LANES : (block + 1) * LANES]
+
+
+def post_plane(sizes, layers, meta_ref, rows_ref, message_ref):
+    cases = rows_ref.shape[0]
+    message_ref[:, :cases, :] = jnp.zeros((message_ref.shape[0], cases, LANES), BF16)
+    if layers == 1:
+        block = wanted_blocks(sizes, layers, meta_ref)[-1]
+        message_ref[lax.axis_index("fine"), :cases, :] = rows_ref[:, lanes_of(block)]
+        targets = [meta_ref[0, b] for b in range(PLANES)]
+    else:
+        targets = facing_subs(sizes, meta_ref)
+    post_blocks(message_ref, targets, rows_ref[...])
+
+
+def facing_plane(meta_ref, own_ref, other_ref, cases):
+    facing = [own_ref[meta_ref[0, b], :cases, :] for b in range(PLANES)]
+    return facing + [other_ref[lax.axis_index("fine"), :cases, :]] * 2
 
 
 def fetch(pairs, sems):
@@ -311,21 +328,29 @@
     return applied, sums
 
 
-def first_kernel(sizes, dims, layers, count, meta_ref, coeffs_ref, residual_ref, rows_ref, dual_ref, *refs):
+def first_kernel(sizes, dims, layers, count, meta_ref, residual_ref, rows_ref, dual_ref, *refs):
+    gathered_refs, refs = refs[: 3 - layers], refs[3 - layers :]
     near_refs = refs[:count]
-    message_ref, direction_ref, applied_ref, theirs_ref = refs[count:]
-    applied, sums = advance(
-        sizes, dims, meta_ref, coeffs_ref[...], residual_ref[...], near_refs, rows_ref, dual_ref, theirs_ref,
-        direction_ref, applied_ref,
-    )
-    cases = applied.shape[0]
+    message_ref, direction_ref, applied_ref, coeffs_ref, theirs_ref = refs[count:]
+    if layers == 1:
+        coarse = lax.axis_index("coarse")
+        for fine in range(sizes[0]):
+            coeffs_ref[2 * fine + coarse] = gathered_refs[0][fine]
+            coeffs_ref[2 * fine + 1 - coarse] = gathered_refs[1][fine]
+    else:
+        coeffs_ref[...] = gathered_refs[0][...]
+    _, sums = advance(
+        sizes, dims, meta_ref, coeffs_ref[...].reshape(-1, LANES), residual_ref[...], near_refs, rows_ref, dual_ref,
+        theirs_ref, direction_ref, applied_ref,
+    )
+    cases = applied_ref.shape[0]
     tiles = shares(sizes, dims, layers, meta_ref, applied_ref, near_refs, rows_ref, sums)
-    message_ref[:, :cases, :] = jnp.zeros((message_ref.shape[0], cases, LANES), BF16)
     message_ref[:, cases:, :] = jnp.broadcast_to(tiles[None], (message_ref.shape[0],) + tiles.shape)
-    post_blocks(message_ref, [meta_ref[0, b] for b in range(PLANES)], applied)
     if layers == 1:
-        block = wanted_blocks(sizes, layers, meta_ref)[-1]
-        message_ref[lax.axis_index("fine"), :cases, :] = applied_ref[:, lanes_of(block)]
+        post_plane(sizes, layers, meta_ref, applied_ref, message_ref)
+    else:
+        message_ref[:, :cases, :] = jnp.zeros((message_ref.shape[0], cases, LANES), BF16)
+        post_blocks(message_ref, [meta_ref[0, b] for b in range(PLANES)], applied_ref[...])
 
 
 def steps_from(totals):
@@ -344,30 +369,30 @@
     low, high = steps_from(collect(sizes, layers, cases, own_ref, others_refs[0], changes_ref))
     step = jnp.concatenate([low, high], axis=0)
     packed_step = jnp.where(lane_ids(half) < HALF, low, high)
-    coeffs = coeffs_ref[...] - (changes_ref[...] * packed_step[None]).reshape(coeffs_ref.shape)
-    facing = [own_ref[meta_ref[0, b], :cases, :] for b in range(PLANES)]
-    if layers == 1:
-        facing += [others_refs[0][lax.axis_index("fine"), :cases, :]] * 2
-    else:
-        facing += [ref[...] for ref in others_refs[1:]]
+    coeffs = (coeffs_ref[...] - changes_ref[...] * packed_step[None]).reshape(-1, LANES)
+    facing = facing_plane(meta_ref, own_ref, others_refs[0] if layers == 1 else own_ref, cases)
+    if layers > 1:
+        facing[PLANES:] = [ref[...] for ref in others_refs[1:]]
     image, _, _ = difference(meta_ref, applied_before_ref[...], facing)
     residual = residual_ref[...] - step * jnp.concatenate(image, axis=1)
     residual_out[...] = residual
     multipliers_out[...] = step * before_ref[...]
-    applied, sums = advance(
+    _, sums = advance(
         sizes, dims, meta_ref, coeffs, residual, near_refs, rows_ref, dual_ref, theirs_ref, direction_ref, applied_ref
     )
-    message_ref[:, :cases, :] = jnp.zeros((message_ref.shape[0], cases, LANES), BF16)
     message_ref[:, cases:, :] = jnp.broadcast_to(encode(sums).astype(BF16)[None], (message_ref.shape[0], half, LANES))
-    post_blocks(message_ref, facing_subs(sizes, meta_ref), applied)
-
-
-def last_kernel(sizes, meta_ref, arrived_ref, applied_ref, residual_ref, multipliers_ref, direction_ref,
-                multipliers_out, residual_out):
+    post_plane(sizes, layers, meta_ref, applied_ref, message_ref)
+
+
+def last_kernel(sizes, layers, meta_ref, applied_ref, residual_ref, multipliers_ref, direction_ref, *refs):
+    arrived_refs, (multipliers_out, residual_out) = refs[:-2], refs[-2:]
     cases = applied_ref.shape[0]
-    totals = jnp.sum(arrived_ref[:, cases:, :].astype(F32), axis=0)
+    totals = sum(jnp.sum(ref[:, cases:, :].astype(F32), axis=0) for ref in arrived_refs)
     step = jnp.concatenate(steps_from(decode(totals)), axis=0)
-    facing = [arrived_ref[target, :cases, :] for target in facing_subs(sizes, meta_ref)]
+    if layers == 1:
+        facing = facing_plane(meta_ref, arrived_refs[0], arrived_refs[1], cases)
+    else:
+        facing = [arrived_refs[0][target, :cases, :] for target in facing_subs(sizes, meta_ref)]
     image, _, _ = difference(meta_ref, applied_ref[...], facing)
     fine = lax.axis_index("fine")
     for block in range(PLANES + 2):
@@ -411,8 +436,14 @@
     half = cases // 2
     layers = 1 if coarse_count == 2 else 2
 
+    def swap_cores(array):
+        return lax.ppermute(array, "coarse", [(0, 1), (1, 0)])
+
     def swap_all(message):
-        return lax.all_to_all(message, AXES, 0, 0, tiled=True)
+        if layers == 1:
+            own = lax.all_to_all(message, "fine", 0, 0, tiled=True)
+            return [own, swap_cores(own)]
+        return [lax.all_to_all(message, AXES, 0, 0, tiled=True)]
 
     def swap_slot(message, slot):
         distance = 2 * (PLANES - slot) - 1
@@ -422,14 +453,14 @@
     def swap_blocks(messages):
         received = [swap_slot(messages[slot], slot) for slot in range(PLANES)]
         if layers == 1:
-            return received + [lax.ppermute(messages[PLANES], "coarse", [(0, 1), (1, 0)])]
+            return received + [swap_cores(messages[PLANES])]
         up = [(i, i + 1) for i in range(coarse_count - 1)]
         lower = lax.ppermute(messages[PLANES + 1], "coarse", up)
         return received + [lower, lax.ppermute(messages[PLANES], "coarse", [(j, i) for i, j in up])]
 
     full = ((cases, width), F32)
     half_full = ((cases, width), BF16)
-    coded = ((subs, half, LANES), F32)
+    peers = fine_count if layers == 1 else subs
     dma = pltpu.SemaphoreType.DMA
 
     meta = jnp.concatenate([partners, row_counts, pattern], axis=1)
@@ -453,24 +484,24 @@
         "restrict_residual",
         (meta,),
         (rows, *received),
-        [full, coded],
+        [full, ((peers, half, LANES), F32)],
         [pltpu.VMEM((PLANES, cases, LANES), BF16)],
         after=(dual,),
     )
-    coeffs = swap_all(message).reshape(subs * half, LANES)
+    gathered = swap_all(message)
 
     tiles = 2 + PLANES + layers
-    message, direction, applied = call(
+    message, direction, applied, coeffs = call(
         functools.partial(first_kernel, sizes, dims, layers, count),
         "first_direction",
         (meta,),
-        (coeffs, residual, rows, dual, *near),
-        [((fine_count, cases + tiles * half, LANES), BF16), full, half_full],
+        (residual, rows, dual, *gathered, *near),
+        [((fine_count, cases + tiles * half, LANES), BF16), full, half_full, ((subs, half, LANES), F32)],
         theirs,
     )
     own = lax.all_to_all(message, "fine", 0, 0, tiled=True)
     if layers == 1:
-        others = [lax.ppermute(own, "coarse", [(0, 1), (1, 0)])]
+        others = [swap_cores(own)]
     else:
         up = [(i, i + 1) for i in range(coarse_count - 1)]
         lower = lax.ppermute(applied[:, (PLANES + 1) * LANES :], "coarse", up)
@@ -482,16 +513,15 @@
         "second_direction",
         (meta,),
         (coeffs, residual, direction, applied, rows, dual, own, *others, *near),
-        [((subs, cases + half, LANES), BF16), full, full, full, half_full],
+        [((peers, cases + half, LANES), BF16), full, full, full, half_full],
         theirs + [pltpu.VMEM((subs, half, LANES), F32)],
     )
-    arrived = swap_all(message)
     out = ((1, cases, width), F32)
     multipliers, residual = call(
-        functools.partial(last_kernel, sizes),
+        functools.partial(last_kernel, sizes, layers),
         "finish",
         (meta,),
-        (arrived, applied, residual, multipliers, direction),
+        (applied, residual, multipliers, direction, *swap_all(message)),
         [out, out],
     )
     return multipliers, residual

time: 69.4 us -> 72 us (1.037)
  starting transfers between devices: 18.7 us -> 22.8 us
  blocking collectives: 36.9 us -> 33.1 us
  waiting for transfers between devices: 1.77 us -> 3.61 us
    ppermute x2 -> x4, starting transfers between devices: 5.02 us -> 9.09 us  [swap_cores(): return lax.ppermute(array, 'coarse', [(0, 1), (1, 0)])]
    all_to_all x2, blocking collectives: 24.1 us -> 20.3 us  [swap_all(): own = lax.all_to_all(message, 'fine', 0, 0, tiled=True)]
    ppermute x2 -> x4, waiting for transfers between devices: 1.31 us -> 3.15 us  [swap_cores(): return lax.ppermute(array, 'coarse', [(0, 1), (1, 0)])]
  transfers between devices with their start and end apart: 8 -> 10, of which waited for: 2 -> 4; matrix products, arithmetic and copies ran while one was open for 0% -> 0% of each run, Pallas kernels for 0% -> 0%
where the time goes in v4:
time: 72 us; the launch traced here: 71.4 us
  blocking collectives  33.1 us (46%)
  starting transfers between devices  22.8 us (32%)
  Pallas kernels  6.98 us (10%)
  waiting for transfers between devices  3.61 us (5%)
  local copies, waits for them, and re-layouts  2.48 us (3%)
  other arithmetic  1.67 us (2%)
    all_to_all x2, blocking collectives, swap_all(): own = lax.all_to_all(message, 'fine', 0, 0, tiled=True)  20.3 us
    ppermute x6, starting transfers between devices, swap_slot(): return lax.ppermute(message, 'fine', pairs)  13.7 us
    all_to_all x1, blocking collectives, body(): own = lax.all_to_all(message, 'fine', 0, 0, tiled=True)  12.8 us
    ppermute x4, starting transfers between devices, swap_cores(): return lax.ppermute(array, 'coarse', [(0, 1), (1, 0)])  9.09 us
    pallas_call x6, Pallas kernels, call(): pl.pallas_call(kernel, name=name, out_shape=[jax.ShapeDtypeStruct(shape,...  6.98 us
    ppermute x4, waiting for transfers between devices, swap_cores(): return lax.ppermute(array, 'coarse', [(0, 1), (1, 0)])  3.15 us
    unnamed x4, local copies, waits for them, and re-layouts  2.48 us
  transfers between devices with their start and end apart: 10, of which 4 were waited for; matrix products, arithmetic and copies ran while one was open for 0% of the time, Pallas kernels for 0%

profile of v4, /device:TPU:1, one launch (start us, length us, event | category | flops | bytes accessed | tf_op | source)
XLA Modules:
  0.0 71.4 jit_solution(11401909564677743268)
XLA Ops:
  0.6 0.9 %pad_maximum_fusion.rows_ref = bf16[64,1024]{1,0:T(8,128)(2,1)S(1)} fusion(bf16[48,1024]{1,0:T(8,128)(2,1)} %bitcast.2, bf16[16,1024]{1,0:T(8,128)(2,1)} %bitcast.3), kind=kLoop, calls=%fused_computation | loop fusion | flops 262144 | bytes 262144 | tf_op jit(solution)/shard_map/concatenate | solution.py:467
  1.5 0.8 %pad_add_fusion.meta_ref = s32[1,18]{1,0:T(1,128)S(1)} fusion(s32[1,4]{1,0:T(1,128)} %param.11, s32[1,8]{1,0:T(1,128)} %param.13, s32[1,6]{1,0:T(1,128)} %param.12), kind=kLoop, calls=%fused_computation.1 | loop fusion | flops 36 | bytes 144 | tf_op jit(solution)/shard_map/concatenate | solution.py:466
  2.3 0.0 copy-start.1
  2.3 0.9 %copy-done.1 = f32[1,4,48,48]{3,2,1,0:T(8,128)S(1)} copy-done((f32[1,4,48,48]{3,2,1,0:T(8,128)S(1)}, f32[1,4,48,48]{3,2,1,0:T(8,128)}, u32[]{:S(2)}) %copy-start.1) | copy-done | bytes 36888
  3.2 0.7 pack_setup.1
  3.9 5.1 %collective-permute-start = (bf16[272,128]{1,0:T(8,128)(2,1)S(1)}, bf16[272,128]{1,0:T(8,128)(2,1)S(1)}, u32[]{:S(2)}, u32[]{:S(2)}) collective-permute-start(bf16[272,128]{1,0:T(8,128)(2,1)S(1)} %get-tuple-element.20), channel_id=1, source_target_pairs={{0,22},{2,12},{4,26},{6,16},{8,30},{10,20},{12,2},{14,24},{16,6},{... | collective-permute-start | bytes 208904 | tf_op jit(solution)/shard_map/ppermute | solution.py:451
  9.0 1.3 %collective-permute-start.1 = (bf16[272,128]{1,0:T(8,128)(2,1)S(1)}, bf16[272,128]{1,0:T(8,128)(2,1)S(1)}, u32[]{:S(2)}, u32[]{:S(2)}) collective-permute-start(bf16[272,128]{1,0:T(8,128)(2,1)S(1)} %get-tuple-element.21), channel_id=1, source_target_pairs={{0,18},{2,16},{4,22},{6,20},{8,26},{10,24},{12,30},{14,28},{16,2},... | collective-permute-start | bytes 208904 | tf_op jit(solution)/shard_map/ppermute | solution.py:451
  10.2 1.0 %collective-permute-start.2 = (bf16[272,128]{1,0:T(8,128)(2,1)S(1)}, bf16[272,128]{1,0:T(8,128)(2,1)S(1)}, u32[]{:S(2)}, u32[]{:S(2)}) collective-permute-start(bf16[272,128]{1,0:T(8,128)(2,1)S(1)} %get-tuple-element.22), channel_id=1, source_target_pairs={{0,14},{2,20},{4,18},{6,24},{8,22},{10,28},{12,26},{14,0},{16,30},... | collective-permute-start | bytes 208904 | tf_op jit(solution)/shard_map/ppermute | solution.py:451
  11.3 2.2 %collective-permute-start.3 = (bf16[272,128]{1,0:T(8,128)(2,1)S(1)}, bf16[272,128]{1,0:T(8,128)(2,1)S(1)}, u32[]{:S(2)}, u32[]{:S(2)}) collective-permute-start(bf16[272,128]{1,0:T(8,128)(2,1)S(1)} %get-tuple-element.23), channel_id=1, source_target_pairs={{0,10},{2,24},{4,14},{6,28},{8,18},{10,0},{12,22},{14,4},{16,26},{... | collective-permute-start | bytes 208904 | tf_op jit(solution)/shard_map/ppermute | solution.py:451
  13.4 1.9 %collective-permute-start.4 = (bf16[272,128]{1,0:T(8,128)(2,1)S(1)}, bf16[272,128]{1,0:T(8,128)(2,1)S(1)}, u32[]{:S(2)}, u32[]{:S(2)}) collective-permute-start(bf16[272,128]{1,0:T(8,128)(2,1)S(1)} %get-tuple-element.24), channel_id=1, source_target_pairs={{0,6},{2,28},{4,10},{6,0},{8,14},{10,4},{12,18},{14,8},{16,22},{18... | collective-permute-start | bytes 208904 | tf_op jit(solution)/shard_map/ppermute | solution.py:451
  15.4 0.0 collective-permute-done.refs_0_.refs_3_.refs_2_
  15.4 2.2 %collective-permute-start.5 = (bf16[272,128]{1,0:T(8,128)(2,1)S(1)}, bf16[272,128]{1,0:T(8,128)(2,1)S(1)}, u32[]{:S(2)}, u32[]{:S(2)}) collective-permute-start(bf16[272,128]{1,0:T(8,128)(2,1)S(1)} %get-tuple-element.25), channel_id=1, source_target_pairs={{0,2},{2,0},{4,6},{6,4},{8,10},{10,8},{12,14},{14,12},{16,18},{18,... | collective-permute-start | bytes 208904 | tf_op jit(solution)/shard_map/ppermute | solution.py:451
  17.6 0.0 collective-permute-done.1.refs_1_.refs_4_.refs_3_
  17.6 2.4 %collective-permute-start.6 = (bf16[272,128]{1,0:T(8,128)(2,1)S(1)}, bf16[272,128]{1,0:T(8,128)(2,1)S(1)}, u32[]{:S(2)}, u32[]{:S(2)}) collective-permute-start(bf16[272,128]{1,0:T(8,128)(2,1)S(1)} %get-tuple-element.26.after_ref.refs_2_.refs_1_), channel_id=1, source_target_pairs={{0,1},{1,0},{2,3},{3,2},{4,5},{5,4},{6,7},{7,6},{8,9},{9,8},{10,11... | collective-permute-start | bytes 208904 | tf_op jit(solution)/shard_map/ppermute | solution.py:440
  19.9 0.0 copy-start
  19.9 1.6 %copy-done = bf16[1,1024,1024]{2,1,0:T(8,128)(2,1)S(1)} copy-done((bf16[1,1024,1024]{2,1,0:T(8,128)(2,1)S(1)}, bf16[1,1024,1024]{2,1,0:T(8,128)(2,1)}, u32[]{:S(2)}) %copy-start) | copy-done | bytes 2097176
  21.5 0.1 fetch_dual.1.refs_7_.dual_ref
  21.7 0.0 collective-permute-done.2.refs_2_.refs_5_.refs_4_
  21.7 0.0 collective-permute-done.3.refs_3_.refs_6_.refs_5_
  21.7 0.0 collective-permute-done.4.refs_4_.refs_7_.refs_6_
  21.7 0.4 collective-permute-done.5.refs_5_.refs_8_.refs_7_
  22.1 0.0 collective-permute-done.6.refs_6_.refs_9_.refs_8_
  22.1 0.7 %restrict_residual.1 = (f32[16,1024]{1,0:T(8,128)S(1)}, f32[16,8,128]{2,1,0:T(8,128)S(1)}) custom-call(s32[1,18]{1,0:T(1,128)S(1)} %pad_add_fusion.meta_ref, bf16[64,1024]{1,0:T(8,128)(2,1)S(1)} %pad_maximum_fusion.rows_ref, bf16[272,128]{1,0:T(8,128)(2,1)S(1)} %collective-permute-done.refs_0_.refs_3_.refs_2_, ...), custom_call_target="tpu_custom_call" | custom-call | tf_op jit(solution)/shard_map/restrict_residual/pallas_call | solution.py:417
  22.9 10.7 %all_to_all.15.refs_0_ = f32[16,8,128]{2,1,0:T(8,128)S(1)} all-to-all(f32[16,8,128]{2,1,0:T(8,128)S(1)} %get-tuple-element.28), channel_id=1, replica_groups=mesh['fine'=16,'coarse'=2] {'fine'}, dimensions={0} | all-to-all | bytes 131072 | tf_op jit(solution)/shard_map/all_to_all | solution.py:444
  33.5 2.4 %collective-permute-start.7 = (f32[16,8,128]{2,1,0:T(8,128)S(1)}, f32[16,8,128]{2,1,0:T(8,128)S(1)}, u32[]{:S(2)}, u32[]{:S(2)}) collective-permute-start(f32[16,8,128]{2,1,0:T(8,128)S(1)} %all_to_all.15.refs_0_), channel_id=1, source_target_pairs={{0,1},{1,0},{2,3},{3,2},{4,5},{5,4},{6,7},{7,6},{8,9},{9,8},{10,11... | collective-permute-start | bytes 196616 | tf_op jit(solution)/shard_map/ppermute | solution.py:440
  35.9 0.9 %collective-permute-done.7.refs_1_ = f32[16,8,128]{2,1,0:T(8,128)S(1)} collective-permute-done((f32[16,8,128]{2,1,0:T(8,128)S(1)}, f32[16,8,128]{2,1,0:T(8,128)S(1)}, u32[]{:S(2)}, u32[]{:S(2)}) %collective-permute-start.7) | collective-permute-done | bytes 65568 | tf_op jit(solution)/shard_map/ppermute | solution.py:440
  36.8 1.9 %first_direction.1 = (bf16[16,88,128]{2,1,0:T(8,128)(2,1)S(1)}, f32[16,1024]{1,0:T(8,128)S(1)}, bf16[16,1024]{1,0:T(8,128)(2,1)S(1)}, f32[32,8,128]{2,1,0:T(8,128)S(1)}) custom-call(s32[1,18]{1,0:T(1,128)S(1)} %pad_add_fusion.meta_ref, f32[16,1024]{1,0:T(8,128)S(1)} %get-tuple-element.27.residual_ref, bf16[64,1024]{1,0:T(8,128)(2,1)S(1)} %pad_maximum_fusion.rows_ref, ...), custom_call_target="tpu_custom_call" | custom-call | tf_op jit(solution)/shard_map/first_direction/pallas_call | solution.py:417
  38.7 12.8 %all_to_all.16.own_ref = bf16[16,88,128]{2,1,0:T(8,128)(2,1)S(1)} all-to-all(bf16[16,88,128]{2,1,0:T(8,128)(2,1)S(1)} %get-tuple-element.32), channel_id=1, replica_groups=mesh['fine'=16,'coarse'=2] {'fine'}, dimensions={0} | all-to-all | bytes 720896 | tf_op jit(solution)/shard_map/all_to_all | solution.py:502
  51.5 2.7 %collective-permute-start.8 = (bf16[16,88,128]{2,1,0:T(8,128)(2,1)S(1)}, bf16[16,88,128]{2,1,0:T(8,128)(2,1)S(1)}, u32[]{:S(2)}, u32[]{:S(2)}) collective-permute-start(bf16[16,88,128]{2,1,0:T(8,128)(2,1)S(1)} %all_to_all.16.own_ref), channel_id=1, source_target_pairs={{0,1},{1,0},{2,3},{3,2},{4,5},{5,4},{6,7},{7,6},{8,9},{9,8},{10,11... | collective-permute-start | bytes 1081352 | tf_op jit(solution)/shard_map/ppermute | solution.py:440
  54.2 1.3 %collective-permute-done.8.refs_0_ = bf16[16,88,128]{2,1,0:T(8,128)(2,1)S(1)} collective-permute-done((bf16[16,88,128]{2,1,0:T(8,128)(2,1)S(1)}, bf16[16,88,128]{2,1,0:T(8,128)(2,1)S(1)}, u32[]{:S(2)}, u32[]{:S(2)}) %collective-permute-start.8) | collective-permute-done | bytes 360480 | tf_op jit(solution)/shard_map/ppermute | solution.py:440
  55.5 2.0 %second_direction.1 = (bf16[16,24,128]{2,1,0:T(8,128)(2,1)S(1)}, f32[16,1024]{1,0:T(8,128)S(1)}, f32[16,1024]{1,0:T(8,128)S(1)}, f32[16,1024]{1,0:T(8,128)S(1)}, bf16[16,1024]{1,0:T(8,128)(2,1)S(1)}) custom-call(s32[1,18]{1,0:T(1,128)S(1)} %pad_add_fusion.meta_ref, f32[32,8,128]{2,1,0:T(8,128)S(1)} %get-tuple-element.29.coeffs_ref, ...), custom_call_target="tpu_custom_call" | custom-call | tf_op jit(solution)/shard_map/second_direction/pallas_call | solution.py:417
  57.5 9.7 %all_to_all.17.refs_0_ = bf16[16,24,128]{2,1,0:T(8,128)(2,1)S(1)} all-to-all(bf16[16,24,128]{2,1,0:T(8,128)(2,1)S(1)} %get-tuple-element.37), channel_id=1, replica_groups=mesh['fine'=16,'coarse'=2] {'fine'}, dimensions={0} | all-to-all | bytes 196608 | tf_op jit(solution)/shard_map/all_to_all | solution.py:444
  67.2 1.7 %collective-permute-start.9 = (bf16[16,24,128]{2,1,0:T(8,128)(2,1)S(1)}, bf16[16,24,128]{2,1,0:T(8,128)(2,1)S(1)}, u32[]{:S(2)}, u32[]{:S(2)}) collective-permute-start(bf16[16,24,128]{2,1,0:T(8,128)(2,1)S(1)} %all_to_all.17.refs_0_), channel_id=1, source_target_pairs={{0,1},{1,0},{2,3},{3,2},{4,5},{5,4},{6,7},{7,6},{8,9},{9,8},{10,11... | collective-permute-start | bytes 294920 | tf_op jit(solution)/shard_map/ppermute | solution.py:440
  68.9 0.9 %collective-permute-done.9.refs_1_ = bf16[16,24,128]{2,1,0:T(8,128)(2,1)S(1)} collective-permute-done((bf16[16,24,128]{2,1,0:T(8,128)(2,1)S(1)}, bf16[16,24,128]{2,1,0:T(8,128)(2,1)S(1)}, u32[]{:S(2)}, u32[]{:S(2)}) %collective-permute-start.9) | collective-permute-done | bytes 98336 | tf_op jit(solution)/shard_map/ppermute | solution.py:440
  69.9 1.5 %finish.1 = (f32[1,16,1024]{2,1,0:T(8,128)}, f32[1,16,1024]{2,1,0:T(8,128)}) custom-call(s32[1,18]{1,0:T(1,128)S(1)} %pad_add_fusion.meta_ref, bf16[16,1024]{1,0:T(8,128)(2,1)S(1)} %get-tuple-element.33.applied_ref, f32[16,1024]{1,0:T(8,128)S(1)} %get-tuple-element.34.residual_ref, f32[16,1024]{1,0:T(8,128)S(1)} %get-tuple-element.35.multipliers_ref, ...), custom_call_target="tpu_custom_call" | custom-call | tf_op jit(solution)/shard_map/finish/pallas_call | solution.py:417
Async XLA Ops:
  2.3 0.9 %copy-start.1 = (f32[1,4,48,48]{3,2,1,0:T(8,128)S(1)}, f32[1,4,48,48]{3,2,1,0:T(8,128)}, u32[]{:S(2)}) copy-start(f32[1,4,48,48]{3,2,1,0:T(8,128)} %factors_ref.1) | copy-start | bytes 110596
  3.9 11.5 %collective-permute-start = (bf16[272,128]{1,0:T(8,128)(2,1)S(1)}, bf16[272,128]{1,0:T(8,128)(2,1)S(1)}, u32[]{:S(2)}, u32[]{:S(2)}) collective-permute-start(bf16[272,128]{1,0:T(8,128)(2,1)S(1)} %get-tuple-element.20), channel_id=1, source_target_pairs={{0,22},{2,12},{4,26},{6,16},{8,30},{10,20},{12,2},{14,24},{16,6},{... | collective-permute-start | bytes 208904 | tf_op jit(solution)/shard_map/ppermute | solution.py:451
  9.0 8.6 %collective-permute-start.1 = (bf16[272,128]{1,0:T(8,128)(2,1)S(1)}, bf16[272,128]{1,0:T(8,128)(2,1)S(1)}, u32[]{:S(2)}, u32[]{:S(2)}) collective-permute-start(bf16[272,128]{1,0:T(8,128)(2,1)S(1)} %get-tuple-element.21), channel_id=1, source_target_pairs={{0,18},{2,16},{4,22},{6,20},{8,26},{10,24},{12,30},{14,28},{16,2},... | collective-permute-start | bytes 208904 | tf_op jit(solution)/shard_map/ppermute | solution.py:451
  10.2 11.4 %collective-permute-start.2 = (bf16[272,128]{1,0:T(8,128)(2,1)S(1)}, bf16[272,128]{1,0:T(8,128)(2,1)S(1)}, u32[]{:S(2)}, u32[]{:S(2)}) collective-permute-start(bf16[272,128]{1,0:T(8,128)(2,1)S(1)} %get-tuple-element.22), channel_id=1, source_target_pairs={{0,14},{2,20},{4,18},{6,24},{8,22},{10,28},{12,26},{14,0},{16,30},... | collective-permute-start | bytes 208904 | tf_op jit(solution)/shard_map/ppermute | solution.py:451
  11.3 10.4 %collective-permute-start.3 = (bf16[272,128]{1,0:T(8,128)(2,1)S(1)}, bf16[272,128]{1,0:T(8,128)(2,1)S(1)}, u32[]{:S(2)}, u32[]{:S(2)}) collective-permute-start(bf16[272,128]{1,0:T(8,128)(2,1)S(1)} %get-tuple-element.23), channel_id=1, source_target_pairs={{0,10},{2,24},{4,14},{6,28},{8,18},{10,0},{12,22},{14,4},{16,26},{... | collective-permute-start | bytes 208904 | tf_op jit(solution)/shard_map/ppermute | solution.py:451
  13.4 8.2 %collective-permute-start.4 = (bf16[272,128]{1,0:T(8,128)(2,1)S(1)}, bf16[272,128]{1,0:T(8,128)(2,1)S(1)}, u32[]{:S(2)}, u32[]{:S(2)}) collective-permute-start(bf16[272,128]{1,0:T(8,128)(2,1)S(1)} %get-tuple-element.24), channel_id=1, source_target_pairs={{0,6},{2,28},{4,10},{6,0},{8,14},{10,4},{12,18},{14,8},{16,22},{18... | collective-permute-start | bytes 208904 | tf_op jit(solution)/shard_map/ppermute | solution.py:451
  15.4 6.8 %collective-permute-start.5 = (bf16[272,128]{1,0:T(8,128)(2,1)S(1)}, bf16[272,128]{1,0:T(8,128)(2,1)S(1)}, u32[]{:S(2)}, u32[]{:S(2)}) collective-permute-start(bf16[272,128]{1,0:T(8,128)(2,1)S(1)} %get-tuple-element.25), channel_id=1, source_target_pairs={{0,2},{2,0},{4,6},{6,4},{8,10},{10,8},{12,14},{14,12},{16,18},{18,... | collective-permute-start | bytes 208904 | tf_op jit(solution)/shard_map/ppermute | solution.py:451
  17.6 4.6 %collective-permute-start.6 = (bf16[272,128]{1,0:T(8,128)(2,1)S(1)}, bf16[272,128]{1,0:T(8,128)(2,1)S(1)}, u32[]{:S(2)}, u32[]{:S(2)}) collective-permute-start(bf16[272,128]{1,0:T(8,128)(2,1)S(1)} %get-tuple-element.26.after_ref.refs_2_.refs_1_), channel_id=1, source_target_pairs={{0,1},{1,0},{2,3},{3,2},{4,5},{5,4},{6,7},{7,6},{8,9},{9,8},{10,11... | collective-permute-start | bytes 208904 | tf_op jit(solution)/shard_map/ppermute | solution.py:440
  19.9 1.6 %copy-start = (bf16[1,1024,1024]{2,1,0:T(8,128)(2,1)S(1)}, bf16[1,1024,1024]{2,1,0:T(8,128)(2,1)}, u32[]{:S(2)}) copy-start(bf16[1,1024,1024]{2,1,0:T(8,128)(2,1)} %dual_ref.1) | copy-start | bytes 6291460
  33.5 3.3 %collective-permute-start.7 = (f32[16,8,128]{2,1,0:T(8,128)S(1)}, f32[16,8,128]{2,1,0:T(8,128)S(1)}, u32[]{:S(2)}, u32[]{:S(2)}) collective-permute-start(f32[16,8,128]{2,1,0:T(8,128)S(1)} %all_to_all.15.refs_0_), channel_id=1, source_target_pairs={{0,1},{1,0},{2,3},{3,2},{4,5},{5,4},{6,7},{7,6},{8,9},{9,8},{10,11... | collective-permute-start | bytes 196616 | tf_op jit(solution)/shard_map/ppermute | solution.py:440
  51.5 4.0 %collective-permute-start.8 = (bf16[16,88,128]{2,1,0:T(8,128)(2,1)S(1)}, bf16[16,88,128]{2,1,0:T(8,128)(2,1)S(1)}, u32[]{:S(2)}, u32[]{:S(2)}) collective-permute-start(bf16[16,88,128]{2,1,0:T(8,128)(2,1)S(1)} %all_to_all.16.own_ref), channel_id=1, source_target_pairs={{0,1},{1,0},{2,3},{3,2},{4,5},{5,4},{6,7},{7,6},{8,9},{9,8},{10,11... | collective-permute-start | bytes 1081352 | tf_op jit(solution)/shard_map/ppermute | solution.py:440
  67.2 2.6 %collective-permute-start.9 = (bf16[16,24,128]{2,1,0:T(8,128)(2,1)S(1)}, bf16[16,24,128]{2,1,0:T(8,128)(2,1)S(1)}, u32[]{:S(2)}, u32[]{:S(2)}) collective-permute-start(bf16[16,24,128]{2,1,0:T(8,128)(2,1)S(1)} %all_to_all.17.refs_0_), channel_id=1, source_target_pairs={{0,1},{1,0},{2,3},{3,2},{4,5},{5,4},{6,7},{7,6},{8,9},{9,8},{10,11... | collective-permute-start | bytes 294920 | tf_op jit(solution)/shard_map/ppermute | solution.py:440

commit v5 on v3

--- a/solution.py
+++ b/solution.py
@@ -8,6 +8,7 @@
 from jax.sharding import PartitionSpec as P
 
 PLANES = 6
+DISTANCES = (11, 7, 3, 5, 9, 1)
 AXES = ("fine", "coarse")
 LANES = 128
 HALF = 64
@@ -56,7 +57,7 @@
     fine = lax.axis_index("fine")
     ahead = jnp.where(fine % 2 == 0, partner - fine, fine - partner)
     ahead = jnp.where(ahead < 0, ahead + fine_count, ahead)
-    return PLANES - 1 - (ahead - 1) // 2
+    return sum(jnp.where(ahead == distance, slot, 0) for slot, distance in enumerate(DISTANCES))
 
 
 def live_mask(counts_ref, block):
@@ -173,6 +174,28 @@
     message_ref[...] = jnp.broadcast_to(message[None], message_ref.shape)
 
 
+def seat(part, modes):
+    gap = HALF - modes
+    lane = lane_ids(8) % HALF
+    return (lane >= part * gap) & (lane < (part + 1) * gap), modes - part * gap
+
+
+def board(hosts, guest, modes):
+    seated = []
+    for part, host in enumerate(hosts):
+        mask, move = seat(part, modes)
+        seated.append(host + pltpu.roll(jnp.where(mask, guest, 0.0), move, 1))
+    return seated
+
+
+def alight(hosts, modes):
+    guest = jnp.zeros((8, LANES), F32)
+    for part, host in enumerate(hosts):
+        mask, move = seat(part, modes)
+        guest = jnp.where(mask, pltpu.roll(host, LANES - move, 1), guest)
+    return guest
+
+
 def shares(sizes, dims, layers, meta_ref, applied_ref, near_refs, rows_ref, sums):
     cases = applied_ref.shape[0]
     span = layout_of(*dims)["basis"]
@@ -182,14 +205,16 @@
         masked.append((part * live_mask(meta_ref, block)).astype(BF16))
     own = fold(times_basis(jnp.concatenate(masked, axis=1), twice(rows_ref[cases:, :])))
     high = own.astype(BF16).astype(F32)
-    tiles = [high + encode(sums), own - high]
+    tiles = []
     for near_ref, block in zip(near_refs[1:], wanted_blocks(sizes, layers, meta_ref)):
         part = applied_ref[:, lanes_of(block)].astype(F32) * live_mask(meta_ref, block)
         tiles.append(fold(times_basis(part.astype(BF16), twice(near_ref[span, :]))))
-    return jnp.concatenate(tiles, axis=0).astype(BF16)
-
-
-def collect(sizes, layers, cases, own_ref, others_ref, changes_ref):
+    modes = dims[1]
+    hosts = board(tiles[:3], own - high, modes) + board(tiles[3:PLANES], tiles[PLANES], modes)
+    return jnp.concatenate([high + encode(sums)] + hosts + tiles[PLANES + 1 :], axis=0).astype(BF16)
+
+
+def collect(sizes, dims, layers, cases, own_ref, others_ref, changes_ref):
     fine_count, coarse_count = sizes
     half = cases // 2
     coarse = lax.axis_index("coarse")
@@ -205,21 +230,21 @@
         for layer in range(coarse_count):
             first = tile(layer, fine, 0)
             totals = totals + first
-            value = first + tile(layer, fine, 1)
+            value = first + alight([tile(layer, fine, 1 + slot) for slot in range(3)], dims[1])
             for slot in range(PLANES):
-                distance = 2 * (PLANES - slot) - 1
+                distance = DISTANCES[slot]
                 partner = jnp.where(fine % 2 == 0, fine + distance, fine - distance) if layers > 1 else (
                     fine + distance if fine % 2 == 0 else fine - distance
                 )
-                value = value - tile(layer, (partner + fine_count) % fine_count, 2 + slot)
+                value = value - tile(layer, (partner + fine_count) % fine_count, 1 + slot)
             if layers == 1:
-                value = value - tile(1 - layer, fine, 2 + PLANES)
+                value = value - alight([tile(1 - layer, fine, 4 + slot) for slot in range(3)], dims[1])
                 place = fine * 2 + (coarse if layer == 0 else 1 - coarse)
             else:
                 if layer > 0:
-                    value = value - tile(layer - 1, fine, 3 + PLANES)
+                    value = value - tile(layer - 1, fine, 1 + PLANES)
                 if layer < coarse_count - 1:
-                    value = value - tile(layer + 1, fine, 2 + PLANES)
+                    value = value - alight([tile(layer + 1, fine, 4 + slot) for slot in range(3)], dims[1])
                 place = fine * coarse_count + layer
             changes_ref[place] = value
         return totals
@@ -341,7 +366,7 @@
     message_ref, residual_out, multipliers_out, direction_ref, applied_ref, theirs_ref, changes_ref = refs[count:]
     cases = residual_ref.shape[0]
     half = cases // 2
-    low, high = steps_from(collect(sizes, layers, cases, own_ref, others_refs[0], changes_ref))
+    low, high = steps_from(collect(sizes, dims, layers, cases, own_ref, others_refs[0], changes_ref))
     step = jnp.concatenate([low, high], axis=0)
     packed_step = jnp.where(lane_ids(half) < HALF, low, high)
     coeffs = coeffs_ref[...] - (changes_ref[...] * packed_step[None]).reshape(coeffs_ref.shape)
@@ -415,7 +440,7 @@
         return lax.all_to_all(message, AXES, 0, 0, tiled=True)
 
     def swap_slot(message, slot):
-        distance = 2 * (PLANES - slot) - 1
+        distance = DISTANCES[slot]
         pairs = [(i, (i + distance if i % 2 == 0 else i - distance) % fine_count) for i in range(fine_count)]
         return lax.ppermute(message, "fine", pairs)
 
@@ -459,7 +484,7 @@
     )
     coeffs = swap_all(message).reshape(subs * half, LANES)
 
-    tiles = 2 + PLANES + layers
+    tiles = PLANES + layers
     message, direction, applied = call(
         functools.partial(first_kernel, sizes, dims, layers, count),
         "first_direction",

time: 69.4 us -> 68 us (0.980)
  starting transfers between devices: 18.7 us -> 15.5 us
  waiting for transfers between devices: 1.77 us -> 3.33 us
    ppermute x6, starting transfers between devices: 13.7 us -> 10.9 us  [swap_slot(): return lax.ppermute(message, 'fine', pairs)]
    ppermute x6, waiting for transfers between devices: 0.46 us -> 2.12 us  [swap_slot(): return lax.ppermute(message, 'fine', pairs)]
    all_to_all x2, blocking collectives: 24.1 us -> 25.1 us  [swap_all(): return lax.all_to_all(message, AXES, 0, 0, tiled=True)]
    all_to_all x1, blocking collectives: 12.8 us -> 11.9 us  [body(): own = lax.all_to_all(message, 'fine', 0, 0, tiled=True)]
  transfers between devices with their start and end apart: 8 -> 8, of which waited for: 2 -> 3; matrix products, arithmetic and copies ran while one was open for 0% -> 0% of each run, Pallas kernels for 0% -> 0%
where the time goes in v5:
time: 68 us; the launch traced here: 67.7 us
  blocking collectives  37 us (54%)
  starting transfers between devices  15.5 us (23%)
  Pallas kernels  6.99 us (10%)
  waiting for transfers between devices  3.33 us (5%)
  local copies, waits for them, and re-layouts  2.48 us (4%)
  other arithmetic  1.67 us (2%)
  between operations  0.7 us (1%)
    all_to_all x2, blocking collectives, swap_all(): return lax.all_to_all(message, AXES, 0, 0, tiled=True)  25.1 us
    all_to_all x1, blocking collectives, body(): own = lax.all_to_all(message, 'fine', 0, 0, tiled=True)  11.9 us
    ppermute x6, starting transfers between devices, swap_slot(): return lax.ppermute(message, 'fine', pairs)  10.9 us
    pallas_call x6, Pallas kernels, call(): pl.pallas_call(kernel, name=name, out_shape=[jax.ShapeDtypeStruct(shape,...  6.99 us
    unnamed x4, local copies, waits for them, and re-layouts  2.48 us
    ppermute x1, starting transfers between devices, swap_blocks(): lax.ppermute(messages[PLANES], 'coarse', [(0, 1), (1, 0)])  2.36 us
    ppermute x1, starting transfers between devices, body(): others = [lax.ppermute(own, 'coarse', [(0, 1), (1, 0)])]  2.29 us
    ppermute x6, waiting for transfers between devices, swap_slot(): return lax.ppermute(message, 'fine', pairs)  2.12 us
  transfers between devices with their start and end apart: 8, of which 3 were waited for; matrix products, arithmetic and copies ran while one was open for 0% of the time, Pallas kernels for 0%

profile of v5, /device:TPU:1, one launch (start us, length us, event | category | flops | bytes accessed | tf_op | source)
XLA Modules:
  0.0 67.7 jit_solution(703079022865352471)
XLA Ops:
  0.6 0.9 %pad_maximum_fusion.rows_ref = bf16[64,1024]{1,0:T(8,128)(2,1)S(1)} fusion(bf16[48,1024]{1,0:T(8,128)(2,1)} %bitcast.5, bf16[16,1024]{1,0:T(8,128)(2,1)} %bitcast.6), kind=kLoop, calls=%fused_computation | loop fusion | flops 262144 | bytes 262144 | tf_op jit(solution)/shard_map/concatenate | solution.py:461
  1.5 0.8 %pad_add_fusion.meta_ref = s32[1,18]{1,0:T(1,128)S(1)} fusion(s32[1,4]{1,0:T(1,128)} %param.11, s32[1,8]{1,0:T(1,128)} %param.13, s32[1,6]{1,0:T(1,128)} %param.12), kind=kLoop, calls=%fused_computation.1 | loop fusion | flops 36 | bytes 144 | tf_op jit(solution)/shard_map/concatenate | solution.py:460
  2.3 0.0 copy-start.1
  2.3 0.9 %copy-done.1 = f32[1,4,48,48]{3,2,1,0:T(8,128)S(1)} copy-done((f32[1,4,48,48]{3,2,1,0:T(8,128)S(1)}, f32[1,4,48,48]{3,2,1,0:T(8,128)}, u32[]{:S(2)}) %copy-start.1) | copy-done | bytes 36888
  3.2 0.7 %pack_setup.1 = (bf16[272,128]{1,0:T(8,128)(2,1)S(1)}, bf16[272,128]{1,0:T(8,128)(2,1)S(1)}, bf16[272,128]{1,0:T(8,128)(2,1)S(1)}, bf16[272,128]{1,0:T(8,128)(2,...) custom-call(s32[1,18]{1,0:T(1,128)S(1)} %pad_add_fusion.meta_ref, ...), custom_call_target="tpu_custom_call" | custom-call | tf_op jit(solution)/shard_map/pack_setup/pallas_call | solution.py:417
  3.9 5.1 %collective-permute-start = (bf16[272,128]{1,0:T(8,128)(2,1)S(1)}, bf16[272,128]{1,0:T(8,128)(2,1)S(1)}, u32[]{:S(2)}, u32[]{:S(2)}) collective-permute-start(bf16[272,128]{1,0:T(8,128)(2,1)S(1)} %get-tuple-element.19), channel_id=1, source_target_pairs={{0,22},{2,12},{4,26},{6,16},{8,30},{10,20},{12,2},{14,24},{16,6},{... | collective-permute-start | bytes 208904 | tf_op jit(solution)/shard_map/ppermute | solution.py:445
  9.0 1.2 %collective-permute-start.1 = (bf16[272,128]{1,0:T(8,128)(2,1)S(1)}, bf16[272,128]{1,0:T(8,128)(2,1)S(1)}, u32[]{:S(2)}, u32[]{:S(2)}) collective-permute-start(bf16[272,128]{1,0:T(8,128)(2,1)S(1)} %get-tuple-element.20), channel_id=1, source_target_pairs={{0,14},{2,20},{4,18},{6,24},{8,22},{10,28},{12,26},{14,0},{16,30},... | collective-permute-start | bytes 208904 | tf_op jit(solution)/shard_map/ppermute | solution.py:445
  10.2 1.9 %collective-permute-start.2 = (bf16[272,128]{1,0:T(8,128)(2,1)S(1)}, bf16[272,128]{1,0:T(8,128)(2,1)S(1)}, u32[]{:S(2)}, u32[]{:S(2)}) collective-permute-start(bf16[272,128]{1,0:T(8,128)(2,1)S(1)} %get-tuple-element.21), channel_id=1, source_target_pairs={{0,6},{2,28},{4,10},{6,0},{8,14},{10,4},{12,18},{14,8},{16,22},{18... | collective-permute-start | bytes 208904 | tf_op jit(solution)/shard_map/ppermute | solution.py:445
  12.1 1.4 %collective-permute-start.3 = (bf16[272,128]{1,0:T(8,128)(2,1)S(1)}, bf16[272,128]{1,0:T(8,128)(2,1)S(1)}, u32[]{:S(2)}, u32[]{:S(2)}) collective-permute-start(bf16[272,128]{1,0:T(8,128)(2,1)S(1)} %get-tuple-element.22), channel_id=1, source_target_pairs={{0,10},{2,24},{4,14},{6,28},{8,18},{10,0},{12,22},{14,4},{16,26},{... | collective-permute-start | bytes 208904 | tf_op jit(solution)/shard_map/ppermute | solution.py:445
  13.5 1.1 %collective-permute-start.4 = (bf16[272,128]{1,0:T(8,128)(2,1)S(1)}, bf16[272,128]{1,0:T(8,128)(2,1)S(1)}, u32[]{:S(2)}, u32[]{:S(2)}) collective-permute-start(bf16[272,128]{1,0:T(8,128)(2,1)S(1)} %get-tuple-element.23), channel_id=1, source_target_pairs={{0,18},{2,16},{4,22},{6,20},{8,26},{10,24},{12,30},{14,28},{16,2},... | collective-permute-start | bytes 208904 | tf_op jit(solution)/shard_map/ppermute | solution.py:445
  14.6 0.0 collective-permute-done.refs_0_.refs_1_.refs_2_
  14.6 0.1 collective-permute-start.5
  14.7 0.0 collective-permute-done.1.refs_1_.refs_2_.refs_3_
  14.8 2.4 %collective-permute-start.6 = (bf16[272,128]{1,0:T(8,128)(2,1)S(1)}, bf16[272,128]{1,0:T(8,128)(2,1)S(1)}, u32[]{:S(2)}, u32[]{:S(2)}) collective-permute-start(bf16[272,128]{1,0:T(8,128)(2,1)S(1)} %get-tuple-element.25.after_ref.refs_0_.refs_1_), channel_id=1, source_target_pairs={{0,1},{1,0},{2,3},{3,2},{4,5},{5,4},{6,7},{7,6},{8,9},{9,8},{10,11... | collective-permute-start | bytes 208904 | tf_op jit(solution)/shard_map/ppermute | solution.py:450
  17.1 0.0 copy-start
  17.1 1.6 %copy-done = bf16[1,1024,1024]{2,1,0:T(8,128)(2,1)S(1)} copy-done((bf16[1,1024,1024]{2,1,0:T(8,128)(2,1)S(1)}, bf16[1,1024,1024]{2,1,0:T(8,128)(2,1)}, u32[]{:S(2)}) %copy-start) | copy-done | bytes 2097176
  18.7 0.1 fetch_dual.1.refs_7_.dual_ref
  18.9 0.0 collective-permute-done.2.refs_2_.refs_3_.refs_4_
  18.9 0.0 collective-permute-done.3.refs_3_.refs_4_.refs_5_
  18.9 1.7 %collective-permute-done.4.refs_4_.refs_5_.refs_6_ = bf16[272,128]{1,0:T(8,128)(2,1)S(1)} collective-permute-done((bf16[272,128]{1,0:T(8,128)(2,1)S(1)}, bf16[272,128]{1,0:T(8,128)(2,1)S(1)}, u32[]{:S(2)}, u32[]{:S(2)}) %collective-permute-start.4) | collective-permute-done | bytes 69664 | tf_op jit(solution)/shard_map/ppermute | solution.py:445
  20.6 0.4 collective-permute-done.5.refs_5_.refs_6_.refs_7_
  21.0 0.0 collective-permute-done.6.refs_6_.refs_7_.refs_8_
  21.0 0.7 %restrict_residual.1 = (f32[16,1024]{1,0:T(8,128)S(1)}, f32[32,8,128]{2,1,0:T(8,128)S(1)}) custom-call(s32[1,18]{1,0:T(1,128)S(1)} %pad_add_fusion.meta_ref, bf16[64,1024]{1,0:T(8,128)(2,1)S(1)} %pad_maximum_fusion.rows_ref, bf16[272,128]{1,0:T(8,128)(2,1)S(1)} %collective-permute-done.refs_0_.refs_1_.refs_2_, ...), custom_call_target="tpu_custom_call" | custom-call | tf_op jit(solution)/shard_map/restrict_residual/pallas_call | solution.py:417
  21.7 13.6 %all_to_all.15 = f32[32,8,128]{2,1,0:T(8,128)S(1)} all-to-all(f32[32,8,128]{2,1,0:T(8,128)S(1)} %get-tuple-element.26), channel_id=1, replica_groups=mesh['fine'=16,'coarse'=2] {'fine','coarse'}, dimensions={0} | all-to-all | bytes 262144 | tf_op jit(solution)/shard_map/all_to_all | solution.py:440
  35.3 1.9 %first_direction.1 = (bf16[16,72,128]{2,1,0:T(8,128)(2,1)S(1)}, f32[16,1024]{1,0:T(8,128)S(1)}, bf16[16,1024]{1,0:T(8,128)(2,1)S(1)}) custom-call(s32[1,18]{1,0:T(1,128)S(1)} %pad_add_fusion.meta_ref, f32[256,128]{1,0:T(8,128)S(1)} %bitcast.3, f32[16,1024]{1,0:T(8,128)S(1)} %get-tuple-element.27.residual_ref, bf16[64,1024]{1,0:T(8,128)(2,1)S(1)} %pad_maximum_fusion.rows_ref, ...), custom_call_target="tpu_custom_call" | custom-call | tf_op jit(solution)/shard_map/first_direction/pallas_call | solution.py:417
  37.2 11.9 %all_to_all.16.own_ref = bf16[16,72,128]{2,1,0:T(8,128)(2,1)S(1)} all-to-all(bf16[16,72,128]{2,1,0:T(8,128)(2,1)S(1)} %get-tuple-element.30), channel_id=1, replica_groups=mesh['fine'=16,'coarse'=2] {'fine'}, dimensions={0} | all-to-all | bytes 589824 | tf_op jit(solution)/shard_map/all_to_all | solution.py:496
  49.1 2.3 %collective-permute-start.7 = (bf16[16,72,128]{2,1,0:T(8,128)(2,1)S(1)}, bf16[16,72,128]{2,1,0:T(8,128)(2,1)S(1)}, u32[]{:S(2)}, u32[]{:S(2)}) collective-permute-start(bf16[16,72,128]{2,1,0:T(8,128)(2,1)S(1)} %all_to_all.16.own_ref), channel_id=1, source_target_pairs={{0,1},{1,0},{2,3},{3,2},{4,5},{5,4},{6,7},{7,6},{8,9},{9,8},{10,11... | collective-permute-start | bytes 884744 | tf_op jit(solution)/shard_map/ppermute | solution.py:498
  51.4 1.2 %collective-permute-done.7.refs_0_ = bf16[16,72,128]{2,1,0:T(8,128)(2,1)S(1)} collective-permute-done((bf16[16,72,128]{2,1,0:T(8,128)(2,1)S(1)}, bf16[16,72,128]{2,1,0:T(8,128)(2,1)S(1)}, u32[]{:S(2)}, u32[]{:S(2)}) %collective-permute-start.7) | collective-permute-done | bytes 294944 | tf_op jit(solution)/shard_map/ppermute | solution.py:498
  52.6 2.0 %second_direction.1 = (bf16[32,24,128]{2,1,0:T(8,128)(2,1)S(1)}, f32[16,1024]{1,0:T(8,128)S(1)}, f32[16,1024]{1,0:T(8,128)S(1)}, f32[16,1024]{1,0:T(8,128)S(1)}, bf16[16,1024]{1,0:T(8,128)(2,1)S(1)}) custom-call(s32[1,18]{1,0:T(1,128)S(1)} %pad_add_fusion.meta_ref, f32[256,128]{1,0:T(8,128)S(1)} %bitcast.4, f32[16,1024]{1,0:T(8,128)S(1)} %get-tuple-element.27.residual_ref, ...), custom_call_target="tpu_custom_call" | custom-call | tf_op jit(solution)/shard_map/second_direction/pallas_call | solution.py:417
  54.7 11.5 %all_to_all.17.arrived_ref = bf16[32,24,128]{2,1,0:T(8,128)(2,1)S(1)} all-to-all(bf16[32,24,128]{2,1,0:T(8,128)(2,1)S(1)} %get-tuple-element.31), channel_id=1, replica_groups=mesh['fine'=16,'coarse'=2] {'fine','coarse'}, dimensions={0} | all-to-all | bytes 393216 | tf_op jit(solution)/shard_map/all_to_all | solution.py:440
  66.2 1.5 %finish.1 = (f32[1,16,1024]{2,1,0:T(8,128)}, f32[1,16,1024]{2,1,0:T(8,128)}) custom-call(s32[1,18]{1,0:T(1,128)S(1)} %pad_add_fusion.meta_ref, bf16[32,24,128]{2,1,0:T(8,128)(2,1)S(1)} %all_to_all.17.arrived_ref, bf16[16,1024]{1,0:T(8,128)(2,1)S(1)} %get-tuple-element.32.applied_ref, f32[16,1024]{1,0:T(8,128)S(1)} %get-tuple-element.33.residual_ref, ...), custom_call_target="tpu_custom_call" | custom-call | tf_op jit(solution)/shard_map/finish/pallas_call | solution.py:417
Async XLA Ops:
  2.3 0.9 %copy-start.1 = (f32[1,4,48,48]{3,2,1,0:T(8,128)S(1)}, f32[1,4,48,48]{3,2,1,0:T(8,128)}, u32[]{:S(2)}) copy-start(f32[1,4,48,48]{3,2,1,0:T(8,128)} %factors_ref.1) | copy-start | bytes 110596
  3.9 10.7 %collective-permute-start = (bf16[272,128]{1,0:T(8,128)(2,1)S(1)}, bf16[272,128]{1,0:T(8,128)(2,1)S(1)}, u32[]{:S(2)}, u32[]{:S(2)}) collective-permute-start(bf16[272,128]{1,0:T(8,128)(2,1)S(1)} %get-tuple-element.19), channel_id=1, source_target_pairs={{0,22},{2,12},{4,26},{6,16},{8,30},{10,20},{12,2},{14,24},{16,6},{... | collective-permute-start | bytes 208904 | tf_op jit(solution)/shard_map/ppermute | solution.py:445
  9.0 5.8 %collective-permute-start.1 = (bf16[272,128]{1,0:T(8,128)(2,1)S(1)}, bf16[272,128]{1,0:T(8,128)(2,1)S(1)}, u32[]{:S(2)}, u32[]{:S(2)}) collective-permute-start(bf16[272,128]{1,0:T(8,128)(2,1)S(1)} %get-tuple-element.20), channel_id=1, source_target_pairs={{0,14},{2,20},{4,18},{6,24},{8,22},{10,28},{12,26},{14,0},{16,30},... | collective-permute-start | bytes 208904 | tf_op jit(solution)/shard_map/ppermute | solution.py:445
  10.2 8.7 %collective-permute-start.2 = (bf16[272,128]{1,0:T(8,128)(2,1)S(1)}, bf16[272,128]{1,0:T(8,128)(2,1)S(1)}, u32[]{:S(2)}, u32[]{:S(2)}) collective-permute-start(bf16[272,128]{1,0:T(8,128)(2,1)S(1)} %get-tuple-element.21), channel_id=1, source_target_pairs={{0,6},{2,28},{4,10},{6,0},{8,14},{10,4},{12,18},{14,8},{16,22},{18... | collective-permute-start | bytes 208904 | tf_op jit(solution)/shard_map/ppermute | solution.py:445
  12.1 6.7 %collective-permute-start.3 = (bf16[272,128]{1,0:T(8,128)(2,1)S(1)}, bf16[272,128]{1,0:T(8,128)(2,1)S(1)}, u32[]{:S(2)}, u32[]{:S(2)}) collective-permute-start(bf16[272,128]{1,0:T(8,128)(2,1)S(1)} %get-tuple-element.22), channel_id=1, source_target_pairs={{0,10},{2,24},{4,14},{6,28},{8,18},{10,0},{12,22},{14,4},{16,26},{... | collective-permute-start | bytes 208904 | tf_op jit(solution)/shard_map/ppermute | solution.py:445
  13.5 7.1 %collective-permute-start.4 = (bf16[272,128]{1,0:T(8,128)(2,1)S(1)}, bf16[272,128]{1,0:T(8,128)(2,1)S(1)}, u32[]{:S(2)}, u32[]{:S(2)}) collective-permute-start(bf16[272,128]{1,0:T(8,128)(2,1)S(1)} %get-tuple-element.23), channel_id=1, source_target_pairs={{0,18},{2,16},{4,22},{6,20},{8,26},{10,24},{12,30},{14,28},{16,2},... | collective-permute-start | bytes 208904 | tf_op jit(solution)/shard_map/ppermute | solution.py:445
  14.6 6.4 %collective-permute-start.5 = (bf16[272,128]{1,0:T(8,128)(2,1)S(1)}, bf16[272,128]{1,0:T(8,128)(2,1)S(1)}, u32[]{:S(2)}, u32[]{:S(2)}) collective-permute-start(bf16[272,128]{1,0:T(8,128)(2,1)S(1)} %get-tuple-element.24), channel_id=1, source_target_pairs={{0,2},{2,0},{4,6},{6,4},{8,10},{10,8},{12,14},{14,12},{16,18},{18,... | collective-permute-start | bytes 208904 | tf_op jit(solution)/shard_map/ppermute | solution.py:445
  14.8 6.2 %collective-permute-start.6 = (bf16[272,128]{1,0:T(8,128)(2,1)S(1)}, bf16[272,128]{1,0:T(8,128)(2,1)S(1)}, u32[]{:S(2)}, u32[]{:S(2)}) collective-permute-start(bf16[272,128]{1,0:T(8,128)(2,1)S(1)} %get-tuple-element.25.after_ref.refs_0_.refs_1_), channel_id=1, source_target_pairs={{0,1},{1,0},{2,3},{3,2},{4,5},{5,4},{6,7},{7,6},{8,9},{9,8},{10,11... | collective-permute-start | bytes 208904 | tf_op jit(solution)/shard_map/ppermute | solution.py:450
  17.1 1.6 %copy-start = (bf16[1,1024,1024]{2,1,0:T(8,128)(2,1)S(1)}, bf16[1,1024,1024]{2,1,0:T(8,128)(2,1)}, u32[]{:S(2)}) copy-start(bf16[1,1024,1024]{2,1,0:T(8,128)(2,1)} %dual_ref.1) | copy-start | bytes 6291460
  49.1 3.5 %collective-permute-start.7 = (bf16[16,72,128]{2,1,0:T(8,128)(2,1)S(1)}, bf16[16,72,128]{2,1,0:T(8,128)(2,1)S(1)}, u32[]{:S(2)}, u32[]{:S(2)}) collective-permute-start(bf16[16,72,128]{2,1,0:T(8,128)(2,1)S(1)} %all_to_all.16.own_ref), channel_id=1, source_target_pairs={{0,1},{1,0},{2,3},{3,2},{4,5},{5,4},{6,7},{7,6},{8,9},{9,8},{10,11... | collective-permute-start | bytes 884744 | tf_op jit(solution)/shard_map/ppermute | solution.py:498

commit v6 on v5

--- a/solution.py
+++ b/solution.py
@@ -8,7 +8,7 @@
 from jax.sharding import PartitionSpec as P
 
 PLANES = 6
-DISTANCES = (11, 7, 3, 5, 9, 1)
+DISTANCES = (11, 9, 7, 3, 5, 1)
 AXES = ("fine", "coarse")
 LANES = 128
 HALF = 64

time: 68 us -> 67.6 us (level)
  blocking collectives: 37 us -> 34.4 us
  starting transfers between devices: 15.5 us -> 17.9 us
    all_to_all x2, blocking collectives: 25.1 us -> 22.5 us  [swap_all(): return lax.all_to_all(message, AXES, 0, 0, tiled=True)]
    ppermute x1, starting transfers between devices: 2.36 us -> 4.03 us  [swap_blocks(): lax.ppermute(messages[PLANES], 'coarse', [(0, 1), (1, 0)])]
    ppermute x6, starting transfers between devices: 10.9 us -> 11.6 us  [swap_slot(): return lax.ppermute(message, 'fine', pairs)]
  transfers between devices with their start and end apart: 8 -> 8, of which waited for: 3 -> 2; matrix products, arithmetic and copies ran while one was open for 0% -> 0% of each run, Pallas kernels for 0% -> 0%
where the time goes in v6:
time: 67.6 us; the launch traced here: 67.3 us
  blocking collectives  34.4 us (51%)
  starting transfers between devices  17.9 us (26%)
  Pallas kernels  6.99 us (10%)
  waiting for transfers between devices  3.01 us (4%)
  local copies, waits for them, and re-layouts  2.48 us (4%)
  other arithmetic  1.67 us (2%)
  between operations  0.71 us (1%)
    all_to_all x2, blocking collectives, swap_all(): return lax.all_to_all(message, AXES, 0, 0, tiled=True)  22.5 us
    all_to_all x1, blocking collectives, body(): own = lax.all_to_all(message, 'fine', 0, 0, tiled=True)  11.9 us
    ppermute x6, starting transfers between devices, swap_slot(): return lax.ppermute(message, 'fine', pairs)  11.6 us
    pallas_call x6, Pallas kernels, call(): pl.pallas_call(kernel, name=name, out_shape=[jax.ShapeDtypeStruct(shape,...  6.99 us
    ppermute x1, starting transfers between devices, swap_blocks(): lax.ppermute(messages[PLANES], 'coarse', [(0, 1), (1, 0)])  4.03 us
    unnamed x4, local copies, waits for them, and re-layouts  2.48 us
    ppermute x1, starting transfers between devices, body(): others = [lax.ppermute(own, 'coarse', [(0, 1), (1, 0)])]  2.3 us
    ppermute x6, waiting for transfers between devices, swap_slot(): return lax.ppermute(message, 'fine', pairs)  1.8 us
  transfers between devices with their start and end apart: 8, of which 2 were waited for; matrix products, arithmetic and copies ran while one was open for 0% of the time, Pallas kernels for 0%

profile of v6, /device:TPU:1, one launch (start us, length us, event | category | flops | bytes accessed | tf_op | source)
XLA Modules:
  0.0 67.3 jit_solution(3382365288139112082)
XLA Ops:
  0.6 0.9 %pad_maximum_fusion.rows_ref = bf16[64,1024]{1,0:T(8,128)(2,1)S(1)} fusion(bf16[48,1024]{1,0:T(8,128)(2,1)} %bitcast.5, bf16[16,1024]{1,0:T(8,128)(2,1)} %bitcast.6), kind=kLoop, calls=%fused_computation | loop fusion | flops 262144 | bytes 262144 | tf_op jit(solution)/shard_map/concatenate | solution.py:461
  1.5 0.8 %pad_add_fusion.meta_ref = s32[1,18]{1,0:T(1,128)S(1)} fusion(s32[1,4]{1,0:T(1,128)} %param.11, s32[1,8]{1,0:T(1,128)} %param.13, s32[1,6]{1,0:T(1,128)} %param.12), kind=kLoop, calls=%fused_computation.1 | loop fusion | flops 36 | bytes 144 | tf_op jit(solution)/shard_map/concatenate | solution.py:460
  2.3 0.0 copy-start.1
  2.3 0.9 %copy-done.1 = f32[1,4,48,48]{3,2,1,0:T(8,128)S(1)} copy-done((f32[1,4,48,48]{3,2,1,0:T(8,128)S(1)}, f32[1,4,48,48]{3,2,1,0:T(8,128)}, u32[]{:S(2)}) %copy-start.1) | copy-done | bytes 36888
  3.2 0.7 %pack_setup.1 = (bf16[272,128]{1,0:T(8,128)(2,1)S(1)}, bf16[272,128]{1,0:T(8,128)(2,1)S(1)}, bf16[272,128]{1,0:T(8,128)(2,1)S(1)}, bf16[272,128]{1,0:T(8,128)(2,...) custom-call(s32[1,18]{1,0:T(1,128)S(1)} %pad_add_fusion.meta_ref, ...), custom_call_target="tpu_custom_call" | custom-call | tf_op jit(solution)/shard_map/pack_setup/pallas_call | solution.py:417
  3.9 5.1 %collective-permute-start = (bf16[272,128]{1,0:T(8,128)(2,1)S(1)}, bf16[272,128]{1,0:T(8,128)(2,1)S(1)}, u32[]{:S(2)}, u32[]{:S(2)}) collective-permute-start(bf16[272,128]{1,0:T(8,128)(2,1)S(1)} %get-tuple-element.19), channel_id=1, source_target_pairs={{0,22},{2,12},{4,26},{6,16},{8,30},{10,20},{12,2},{14,24},{16,6},{... | collective-permute-start | bytes 208904 | tf_op jit(solution)/shard_map/ppermute | solution.py:445
  9.0 1.3 %collective-permute-start.1 = (bf16[272,128]{1,0:T(8,128)(2,1)S(1)}, bf16[272,128]{1,0:T(8,128)(2,1)S(1)}, u32[]{:S(2)}, u32[]{:S(2)}) collective-permute-start(bf16[272,128]{1,0:T(8,128)(2,1)S(1)} %get-tuple-element.20), channel_id=1, source_target_pairs={{0,18},{2,16},{4,22},{6,20},{8,26},{10,24},{12,30},{14,28},{16,2},... | collective-permute-start | bytes 208904 | tf_op jit(solution)/shard_map/ppermute | solution.py:445
  10.2 1.0 %collective-permute-start.2 = (bf16[272,128]{1,0:T(8,128)(2,1)S(1)}, bf16[272,128]{1,0:T(8,128)(2,1)S(1)}, u32[]{:S(2)}, u32[]{:S(2)}) collective-permute-start(bf16[272,128]{1,0:T(8,128)(2,1)S(1)} %get-tuple-element.21), channel_id=1, source_target_pairs={{0,14},{2,20},{4,18},{6,24},{8,22},{10,28},{12,26},{14,0},{16,30},... | collective-permute-start | bytes 208904 | tf_op jit(solution)/shard_map/ppermute | solution.py:445
  11.3 2.1 %collective-permute-start.3 = (bf16[272,128]{1,0:T(8,128)(2,1)S(1)}, bf16[272,128]{1,0:T(8,128)(2,1)S(1)}, u32[]{:S(2)}, u32[]{:S(2)}) collective-permute-start(bf16[272,128]{1,0:T(8,128)(2,1)S(1)} %get-tuple-element.22), channel_id=1, source_target_pairs={{0,6},{2,28},{4,10},{6,0},{8,14},{10,4},{12,18},{14,8},{16,22},{18... | collective-permute-start | bytes 208904 | tf_op jit(solution)/shard_map/ppermute | solution.py:445
  13.4 2.1 %collective-permute-start.4 = (bf16[272,128]{1,0:T(8,128)(2,1)S(1)}, bf16[272,128]{1,0:T(8,128)(2,1)S(1)}, u32[]{:S(2)}, u32[]{:S(2)}) collective-permute-start(bf16[272,128]{1,0:T(8,128)(2,1)S(1)} %get-tuple-element.23), channel_id=1, source_target_pairs={{0,10},{2,24},{4,14},{6,28},{8,18},{10,0},{12,22},{14,4},{16,26},{... | collective-permute-start | bytes 208904 | tf_op jit(solution)/shard_map/ppermute | solution.py:445
  15.5 0.0 collective-permute-done.refs_0_.refs_1_.refs_2_
  15.5 0.0 collective-permute-start.5
  15.5 0.0 collective-permute-done.1.refs_1_.refs_2_.refs_3_
  15.5 4.0 %collective-permute-start.6 = (bf16[272,128]{1,0:T(8,128)(2,1)S(1)}, bf16[272,128]{1,0:T(8,128)(2,1)S(1)}, u32[]{:S(2)}, u32[]{:S(2)}) collective-permute-start(bf16[272,128]{1,0:T(8,128)(2,1)S(1)} %get-tuple-element.25.after_ref.refs_0_.refs_1_), channel_id=1, source_target_pairs={{0,1},{1,0},{2,3},{3,2},{4,5},{5,4},{6,7},{7,6},{8,9},{9,8},{10,11... | collective-permute-start | bytes 208904 | tf_op jit(solution)/shard_map/ppermute | solution.py:450
  19.5 0.0 copy-start
  19.6 1.6 %copy-done = bf16[1,1024,1024]{2,1,0:T(8,128)(2,1)S(1)} copy-done((bf16[1,1024,1024]{2,1,0:T(8,128)(2,1)S(1)}, bf16[1,1024,1024]{2,1,0:T(8,128)(2,1)}, u32[]{:S(2)}) %copy-start) | copy-done | bytes 2097176
  21.1 0.1 fetch_dual.1.refs_7_.dual_ref
  21.3 0.0 collective-permute-done.2.refs_2_.refs_3_.refs_4_
  21.3 0.0 collective-permute-done.3.refs_3_.refs_4_.refs_5_
  21.3 0.0 collective-permute-done.4.refs_4_.refs_5_.refs_6_
  21.3 1.8 %collective-permute-done.5.refs_5_.refs_6_.refs_7_ = bf16[272,128]{1,0:T(8,128)(2,1)S(1)} collective-permute-done((bf16[272,128]{1,0:T(8,128)(2,1)S(1)}, bf16[272,128]{1,0:T(8,128)(2,1)S(1)}, u32[]{:S(2)}, u32[]{:S(2)}) %collective-permute-start.5) | collective-permute-done | bytes 69664 | tf_op jit(solution)/shard_map/ppermute | solution.py:445
  23.1 0.0 collective-permute-done.6.refs_6_.refs_7_.refs_8_
  23.1 0.7 %restrict_residual.1 = (f32[16,1024]{1,0:T(8,128)S(1)}, f32[32,8,128]{2,1,0:T(8,128)S(1)}) custom-call(s32[1,18]{1,0:T(1,128)S(1)} %pad_add_fusion.meta_ref, bf16[64,1024]{1,0:T(8,128)(2,1)S(1)} %pad_maximum_fusion.rows_ref, bf16[272,128]{1,0:T(8,128)(2,1)S(1)} %collective-permute-done.refs_0_.refs_1_.refs_2_, ...), custom_call_target="tpu_custom_call" | custom-call | tf_op jit(solution)/shard_map/restrict_residual/pallas_call | solution.py:417
  23.9 11.0 %all_to_all.15 = f32[32,8,128]{2,1,0:T(8,128)S(1)} all-to-all(f32[32,8,128]{2,1,0:T(8,128)S(1)} %get-tuple-element.26), channel_id=1, replica_groups=mesh['fine'=16,'coarse'=2] {'fine','coarse'}, dimensions={0} | all-to-all | bytes 262144 | tf_op jit(solution)/shard_map/all_to_all | solution.py:440
  34.9 1.9 %first_direction.1 = (bf16[16,72,128]{2,1,0:T(8,128)(2,1)S(1)}, f32[16,1024]{1,0:T(8,128)S(1)}, bf16[16,1024]{1,0:T(8,128)(2,1)S(1)}) custom-call(s32[1,18]{1,0:T(1,128)S(1)} %pad_add_fusion.meta_ref, f32[256,128]{1,0:T(8,128)S(1)} %bitcast.3, f32[16,1024]{1,0:T(8,128)S(1)} %get-tuple-element.27.residual_ref, bf16[64,1024]{1,0:T(8,128)(2,1)S(1)} %pad_maximum_fusion.rows_ref, ...), custom_call_target="tpu_custom_call" | custom-call | tf_op jit(solution)/shard_map/first_direction/pallas_call | solution.py:417
  36.7 11.9 %all_to_all.16.own_ref = bf16[16,72,128]{2,1,0:T(8,128)(2,1)S(1)} all-to-all(bf16[16,72,128]{2,1,0:T(8,128)(2,1)S(1)} %get-tuple-element.30), channel_id=1, replica_groups=mesh['fine'=16,'coarse'=2] {'fine'}, dimensions={0} | all-to-all | bytes 589824 | tf_op jit(solution)/shard_map/all_to_all | solution.py:496
  48.7 2.3 %collective-permute-start.7 = (bf16[16,72,128]{2,1,0:T(8,128)(2,1)S(1)}, bf16[16,72,128]{2,1,0:T(8,128)(2,1)S(1)}, u32[]{:S(2)}, u32[]{:S(2)}) collective-permute-start(bf16[16,72,128]{2,1,0:T(8,128)(2,1)S(1)} %all_to_all.16.own_ref), channel_id=1, source_target_pairs={{0,1},{1,0},{2,3},{3,2},{4,5},{5,4},{6,7},{7,6},{8,9},{9,8},{10,11... | collective-permute-start | bytes 884744 | tf_op jit(solution)/shard_map/ppermute | solution.py:498
  51.0 1.2 %collective-permute-done.7.refs_0_ = bf16[16,72,128]{2,1,0:T(8,128)(2,1)S(1)} collective-permute-done((bf16[16,72,128]{2,1,0:T(8,128)(2,1)S(1)}, bf16[16,72,128]{2,1,0:T(8,128)(2,1)S(1)}, u32[]{:S(2)}, u32[]{:S(2)}) %collective-permute-start.7) | collective-permute-done | bytes 294944 | tf_op jit(solution)/shard_map/ppermute | solution.py:498
  52.2 2.0 %second_direction.1 = (bf16[32,24,128]{2,1,0:T(8,128)(2,1)S(1)}, f32[16,1024]{1,0:T(8,128)S(1)}, f32[16,1024]{1,0:T(8,128)S(1)}, f32[16,1024]{1,0:T(8,128)S(1)}, bf16[16,1024]{1,0:T(8,128)(2,1)S(1)}) custom-call(s32[1,18]{1,0:T(1,128)S(1)} %pad_add_fusion.meta_ref, f32[256,128]{1,0:T(8,128)S(1)} %bitcast.4, f32[16,1024]{1,0:T(8,128)S(1)} %get-tuple-element.27.residual_ref, ...), custom_call_target="tpu_custom_call" | custom-call | tf_op jit(solution)/shard_map/second_direction/pallas_call | solution.py:417
  54.2 11.5 %all_to_all.17.arrived_ref = bf16[32,24,128]{2,1,0:T(8,128)(2,1)S(1)} all-to-all(bf16[32,24,128]{2,1,0:T(8,128)(2,1)S(1)} %get-tuple-element.31), channel_id=1, replica_groups=mesh['fine'=16,'coarse'=2] {'fine','coarse'}, dimensions={0} | all-to-all | bytes 393216 | tf_op jit(solution)/shard_map/all_to_all | solution.py:440
  65.7 1.5 %finish.1 = (f32[1,16,1024]{2,1,0:T(8,128)}, f32[1,16,1024]{2,1,0:T(8,128)}) custom-call(s32[1,18]{1,0:T(1,128)S(1)} %pad_add_fusion.meta_ref, bf16[32,24,128]{2,1,0:T(8,128)(2,1)S(1)} %all_to_all.17.arrived_ref, bf16[16,1024]{1,0:T(8,128)(2,1)S(1)} %get-tuple-element.32.applied_ref, f32[16,1024]{1,0:T(8,128)S(1)} %get-tuple-element.33.residual_ref, ...), custom_call_target="tpu_custom_call" | custom-call | tf_op jit(solution)/shard_map/finish/pallas_call | solution.py:417
Async XLA Ops:
  2.3 0.9 %copy-start.1 = (f32[1,4,48,48]{3,2,1,0:T(8,128)S(1)}, f32[1,4,48,48]{3,2,1,0:T(8,128)}, u32[]{:S(2)}) copy-start(f32[1,4,48,48]{3,2,1,0:T(8,128)} %factors_ref.1) | copy-start | bytes 110596
  3.9 11.6 %collective-permute-start = (bf16[272,128]{1,0:T(8,128)(2,1)S(1)}, bf16[272,128]{1,0:T(8,128)(2,1)S(1)}, u32[]{:S(2)}, u32[]{:S(2)}) collective-permute-start(bf16[272,128]{1,0:T(8,128)(2,1)S(1)} %get-tuple-element.19), channel_id=1, source_target_pairs={{0,22},{2,12},{4,26},{6,16},{8,30},{10,20},{12,2},{14,24},{16,6},{... | collective-permute-start | bytes 208904 | tf_op jit(solution)/shard_map/ppermute | solution.py:445
  9.0 6.5 %collective-permute-start.1 = (bf16[272,128]{1,0:T(8,128)(2,1)S(1)}, bf16[272,128]{1,0:T(8,128)(2,1)S(1)}, u32[]{:S(2)}, u32[]{:S(2)}) collective-permute-start(bf16[272,128]{1,0:T(8,128)(2,1)S(1)} %get-tuple-element.20), channel_id=1, source_target_pairs={{0,18},{2,16},{4,22},{6,20},{8,26},{10,24},{12,30},{14,28},{16,2},... | collective-permute-start | bytes 208904 | tf_op jit(solution)/shard_map/ppermute | solution.py:445
  10.2 11.1 %collective-permute-start.2 = (bf16[272,128]{1,0:T(8,128)(2,1)S(1)}, bf16[272,128]{1,0:T(8,128)(2,1)S(1)}, u32[]{:S(2)}, u32[]{:S(2)}) collective-permute-start(bf16[272,128]{1,0:T(8,128)(2,1)S(1)} %get-tuple-element.21), channel_id=1, source_target_pairs={{0,14},{2,20},{4,18},{6,24},{8,22},{10,28},{12,26},{14,0},{16,30},... | collective-permute-start | bytes 208904 | tf_op jit(solution)/shard_map/ppermute | solution.py:445
  11.3 10.0 %collective-permute-start.3 = (bf16[272,128]{1,0:T(8,128)(2,1)S(1)}, bf16[272,128]{1,0:T(8,128)(2,1)S(1)}, u32[]{:S(2)}, u32[]{:S(2)}) collective-permute-start(bf16[272,128]{1,0:T(8,128)(2,1)S(1)} %get-tuple-element.22), channel_id=1, source_target_pairs={{0,6},{2,28},{4,10},{6,0},{8,14},{10,4},{12,18},{14,8},{16,22},{18... | collective-permute-start | bytes 208904 | tf_op jit(solution)/shard_map/ppermute | solution.py:445
  13.4 7.9 %collective-permute-start.4 = (bf16[272,128]{1,0:T(8,128)(2,1)S(1)}, bf16[272,128]{1,0:T(8,128)(2,1)S(1)}, u32[]{:S(2)}, u32[]{:S(2)}) collective-permute-start(bf16[272,128]{1,0:T(8,128)(2,1)S(1)} %get-tuple-element.23), channel_id=1, source_target_pairs={{0,10},{2,24},{4,14},{6,28},{8,18},{10,0},{12,22},{14,4},{16,26},{... | collective-permute-start | bytes 208904 | tf_op jit(solution)/shard_map/ppermute | solution.py:445
  15.5 7.6 %collective-permute-start.5 = (bf16[272,128]{1,0:T(8,128)(2,1)S(1)}, bf16[272,128]{1,0:T(8,128)(2,1)S(1)}, u32[]{:S(2)}, u32[]{:S(2)}) collective-permute-start(bf16[272,128]{1,0:T(8,128)(2,1)S(1)} %get-tuple-element.24), channel_id=1, source_target_pairs={{0,2},{2,0},{4,6},{6,4},{8,10},{10,8},{12,14},{14,12},{16,18},{18,... | collective-permute-start | bytes 208904 | tf_op jit(solution)/shard_map/ppermute | solution.py:445
  15.5 7.6 %collective-permute-start.6 = (bf16[272,128]{1,0:T(8,128)(2,1)S(1)}, bf16[272,128]{1,0:T(8,128)(2,1)S(1)}, u32[]{:S(2)}, u32[]{:S(2)}) collective-permute-start(bf16[272,128]{1,0:T(8,128)(2,1)S(1)} %get-tuple-element.25.after_ref.refs_0_.refs_1_), channel_id=1, source_target_pairs={{0,1},{1,0},{2,3},{3,2},{4,5},{5,4},{6,7},{7,6},{8,9},{9,8},{10,11... | collective-permute-start | bytes 208904 | tf_op jit(solution)/shard_map/ppermute | solution.py:450
  19.5 1.6 %copy-start = (bf16[1,1024,1024]{2,1,0:T(8,128)(2,1)S(1)}, bf16[1,1024,1024]{2,1,0:T(8,128)(2,1)}, u32[]{:S(2)}) copy-start(bf16[1,1024,1024]{2,1,0:T(8,128)(2,1)} %dual_ref.1) | copy-start | bytes 6291460
  48.7 3.5 %collective-permute-start.7 = (bf16[16,72,128]{2,1,0:T(8,128)(2,1)S(1)}, bf16[16,72,128]{2,1,0:T(8,128)(2,1)S(1)}, u32[]{:S(2)}, u32[]{:S(2)}) collective-permute-start(bf16[16,72,128]{2,1,0:T(8,128)(2,1)S(1)} %all_to_all.16.own_ref), channel_id=1, source_target_pairs={{0,1},{1,0},{2,3},{3,2},{4,5},{5,4},{6,7},{7,6},{8,9},{9,8},{10,11... | collective-permute-start | bytes 884744 | tf_op jit(solution)/shard_map/ppermute | solution.py:498

commit v7 on v6

--- a/solution.py
+++ b/solution.py
@@ -77,6 +77,28 @@
     return copies
 
 
+def seat(part, rows, modes):
+    gap = HALF - modes
+    lane = lane_ids(rows) % HALF
+    return (lane >= part * gap) & (lane < (part + 1) * gap), modes - part * gap
+
+
+def board(hosts, guest, modes):
+    seated = []
+    for part, host in enumerate(hosts):
+        mask, move = seat(part, guest.shape[0], modes)
+        seated.append(host + pltpu.roll(jnp.where(mask, guest, 0.0), move, 1))
+    return seated
+
+
+def alight(hosts, modes):
+    guest = jnp.zeros(hosts[0].shape, F32)
+    for part, host in enumerate(hosts):
+        mask, move = seat(part, guest.shape[0], modes)
+        guest = jnp.where(mask, pltpu.roll(host, LANES - move, 1), guest)
+    return guest
+
+
 def pack_kernel(sizes, layers, cases, meta_ref, rows_ref, factors_ref, *outs):
     terms, modes = factors_ref.shape[1:3]
     gap = jnp.zeros((modes, HALF - modes), F32)
@@ -85,13 +107,13 @@
         whole = factors_ref[0, term]
         high = whole.astype(BF16).astype(F32)
         parts.append(jnp.concatenate([high, gap, whole - high, gap], axis=1))
-    factors = jnp.concatenate(parts, axis=0).astype(BF16)
-    row = lax.broadcasted_iota(jnp.int32, (16, LANES), 0)
-    ids = jnp.zeros((16, LANES), F32)
+    factors = jnp.concatenate(board(parts[:-1], parts[-1], modes), axis=0).astype(BF16)
+    row = lax.broadcasted_iota(jnp.int32, (8, LANES), 0)
+    ids = jnp.zeros((8, LANES), F32)
     for term in range(terms):
         sub = meta_ref[0, 2 * PLANES + 2 + term]
         ids = jnp.where(row == term, (sub // 16).astype(F32), ids)
-        ids = jnp.where(row == 8 + term, (sub % 16).astype(F32), ids)
+        ids = jnp.where(row == terms + term, (sub % 16).astype(F32), ids)
     ids = ids.astype(BF16)
     places = layout_of(terms, modes)
     for out_ref, block in zip(outs, wanted_blocks(sizes, layers, meta_ref)):
@@ -102,7 +124,7 @@
 
 
 def layout_of(terms, modes):
-    sizes = (("factors", terms * modes), ("basis", modes), ("ids", 16), ("loads", 16))
+    sizes = (("factors", (terms - 1) * modes), ("basis", modes), ("loads", 16), ("ids", 8))
     places, start = {}, 0
     for name, rows in sizes:
         places[name] = slice(start, start + rows)
@@ -172,28 +194,6 @@
     coefficients = times_basis(both, twice(basis))
     message = fold(coefficients[:cases] - coefficients[cases:])
     message_ref[...] = jnp.broadcast_to(message[None], message_ref.shape)
-
-
-def seat(part, modes):
-    gap = HALF - modes
-    lane = lane_ids(8) % HALF
-    return (lane >= part * gap) & (lane < (part + 1) * gap), modes - part * gap
-
-
-def board(hosts, guest, modes):
-    seated = []
-    for part, host in enumerate(hosts):
-        mask, move = seat(part, modes)
-        seated.append(host + pltpu.roll(jnp.where(mask, guest, 0.0), move, 1))
-    return seated
-
-
-def alight(hosts, modes):
-    guest = jnp.zeros((8, LANES), F32)
-    for part, host in enumerate(hosts):
-        mask, move = seat(part, modes)
-        guest = jnp.where(mask, pltpu.roll(host, LANES - move, 1), guest)
-    return guest
 
 
 def shares(sizes, dims, layers, meta_ref, applied_ref, near_refs, rows_ref, sums):
@@ -257,30 +257,41 @@
     return decode(totals)
 
 
-def solve(coeffs, near, terms, modes):
+def prepare(sizes, dims, near_refs, picks_ref, factors_ref):
+    terms, modes = dims
+    places = layout_of(terms, modes)
     half = 8
-    places = layout_of(terms, modes)
-    high = coeffs.astype(BF16)
-    low = (coeffs - high.astype(F32)).astype(BF16)
-    table = jnp.concatenate([high, low], axis=1)
-    chunks = coeffs.shape[0] // LANES
+    chunks = sizes[0] * sizes[1] * half // LANES
     lanes = lane_ids(half).astype(F32)
     step = lax.broadcasted_iota(jnp.int32, (half, LANES), 0).astype(F32)
-    picks = []
-    for packed in near:
-        ids = packed[places["ids"], :].astype(F32)
-        ids = (ids[:8] * 16.0 + ids[8:]) * float(half)
+    gap = jnp.zeros((HALF - modes, LANES), BF16)
+    for index, near_ref in enumerate(near_refs):
+        ids = near_ref[places["ids"], :].astype(F32)
+        ids = (ids[:terms] * 16.0 + ids[terms : 2 * terms]) * float(half)
+        picks = []
         for term in range(terms):
             target = ids[term : term + 1] + step
             picks.append(
                 jnp.concatenate([(target == lanes + float(LANES * c)).astype(F32) for c in range(chunks)], axis=1)
             )
-    picks = jnp.concatenate(picks, axis=0).astype(BF16)
-    picked = dot(picks, table)
+        rows = terms * half
+        picks_ref[index * rows : (index + 1) * rows, :] = jnp.concatenate(picks, axis=0).astype(BF16)
+        packed = [near_ref[term * modes : (term + 1) * modes, :] for term in range(terms - 1)]
+        packed.append(alight([part.astype(F32) for part in packed], modes).astype(BF16))
+        for term, part in enumerate(packed):
+            factors_ref[index, term * HALF : term * HALF + modes, :] = part
+            factors_ref[index, term * HALF + modes : (term + 1) * HALF, :] = gap
+
+
+def solve(coeffs, dims, picks_ref, factors_ref):
+    terms, modes = dims
+    half = 8
+    high = coeffs.astype(BF16)
+    low = (coeffs - high.astype(F32)).astype(BF16)
+    picked = dot(picks_ref[...], jnp.concatenate([high, low], axis=1))
     left = lane_ids(half) < HALF
-    gap = jnp.zeros((HALF - modes, LANES), BF16)
     solutions = []
-    for index, packed in enumerate(near):
+    for index in range(factors_ref.shape[0]):
         sides = []
         for part in range(2):
             columns = []
@@ -294,31 +305,26 @@
                 columns.append(jnp.concatenate([top, bottom], axis=0))
             sides.append(jnp.concatenate(columns, axis=1))
         rows = jnp.concatenate(sides, axis=0).astype(BF16)
-        factors = []
-        for term in range(terms):
-            factors += [packed[term * modes : (term + 1) * modes, :], gap]
-        product = dot(rows, jnp.concatenate(factors, axis=0))
+        product = dot(rows, factors_ref[index])
         product = product[: 2 * half] + product[2 * half :]
         product = product + pltpu.roll(product, HALF, 1)
         solutions.append(product[:, :modes].astype(BF16))
     return solutions
 
 
-def advance(sizes, dims, meta_ref, coeffs, residual, near_refs, rows_ref, dual_ref, theirs_ref, direction_ref,
-            applied_ref):
-    terms, modes = dims
-    span = layout_of(terms, modes)["basis"]
-    near = [ref[...] for ref in near_refs]
-    solutions = solve(coeffs, near, terms, modes)
+def advance(sizes, dims, meta_ref, coeffs, residual, near_refs, picks_ref, factors_ref, rows_ref, dual_ref, theirs_ref,
+            direction_ref, applied_ref):
+    span = layout_of(*dims)["basis"]
+    solutions = solve(coeffs, dims, picks_ref, factors_ref)
     mine = dot(solutions[0], rows_ref[residual.shape[0] :, :]).astype(BF16).astype(F32)
-    for index, packed in enumerate(near[1:]):
-        theirs_ref[index] = dot(solutions[index + 1], packed[span, :]).astype(BF16).astype(F32)
+    for index, near_ref in enumerate(near_refs[1:]):
+        theirs_ref[index] = dot(solutions[index + 1], near_ref[span, :]).astype(BF16).astype(F32)
     pieces = []
     for block in range(PLANES + 2):
         if block < PLANES:
             place = slot_of(sizes, meta_ref[0, block])
         else:
-            place = min(block, len(near) - 2)
+            place = min(block, len(near_refs) - 2)
         here = slice(block * LANES, (block + 1) * LANES)
         pieces.append(residual[:, here] + live_mask(meta_ref, block) * (mine[:, here] - theirs_ref[place]))
     direction = jnp.concatenate(pieces, axis=1)
@@ -338,10 +344,11 @@
 
 def first_kernel(sizes, dims, layers, count, meta_ref, coeffs_ref, residual_ref, rows_ref, dual_ref, *refs):
     near_refs = refs[:count]
-    message_ref, direction_ref, applied_ref, theirs_ref = refs[count:]
+    message_ref, direction_ref, applied_ref, picks_ref, factors_ref, theirs_ref = refs[count:]
+    prepare(sizes, dims, near_refs, picks_ref, factors_ref)
     applied, sums = advance(
-        sizes, dims, meta_ref, coeffs_ref[...], residual_ref[...], near_refs, rows_ref, dual_ref, theirs_ref,
-        direction_ref, applied_ref,
+        sizes, dims, meta_ref, coeffs_ref[...], residual_ref[...], near_refs, picks_ref, factors_ref, rows_ref, dual_ref,
+        theirs_ref, direction_ref, applied_ref,
     )
     cases = applied.shape[0]
     tiles = shares(sizes, dims, layers, meta_ref, applied_ref, near_refs, rows_ref, sums)
@@ -360,7 +367,7 @@
 
 
 def second_kernel(sizes, dims, layers, count, meta_ref, coeffs_ref, residual_ref, before_ref, applied_before_ref,
-                  rows_ref, dual_ref, own_ref, *refs):
+                  picks_ref, factors_ref, rows_ref, dual_ref, own_ref, *refs):
     others_refs, refs = refs[: 1 if layers == 1 else 3], refs[1 if layers == 1 else 3 :]
     near_refs = refs[:count]
     message_ref, residual_out, multipliers_out, direction_ref, applied_ref, theirs_ref, changes_ref = refs[count:]
@@ -380,7 +387,8 @@
     residual_out[...] = residual
     multipliers_out[...] = step * before_ref[...]
     applied, sums = advance(
-        sizes, dims, meta_ref, coeffs, residual, near_refs, rows_ref, dual_ref, theirs_ref, direction_ref, applied_ref
+        sizes, dims, meta_ref, coeffs, residual, near_refs, picks_ref, factors_ref, rows_ref, dual_ref, theirs_ref,
+        direction_ref, applied_ref,
     )
     message_ref[:, :cases, :] = jnp.zeros((message_ref.shape[0], cases, LANES), BF16)
     message_ref[:, cases:, :] = jnp.broadcast_to(encode(sums).astype(BF16)[None], (message_ref.shape[0], half, LANES))
@@ -459,13 +467,12 @@
 
     meta = jnp.concatenate([partners, row_counts, pattern], axis=1)
     rows = jnp.concatenate([load_cases[0], coarse_basis[0]], axis=0)
-    loads_span = layout_of(terms, modes)["loads"]
     packed = call(
         functools.partial(pack_kernel, sizes, layers, cases),
         "pack_setup",
         (meta,),
         (rows, factor_blocks),
-        [((loads_span.stop, LANES), BF16)] * (PLANES + layers),
+        [((layout_of(terms, modes)["ids"].stop, LANES), BF16)] * (PLANES + layers),
     )
     received = swap_blocks(packed)
     near = [packed[-1]] + received
@@ -485,12 +492,13 @@
     coeffs = swap_all(message).reshape(subs * half, LANES)
 
     tiles = PLANES + layers
-    message, direction, applied = call(
+    message, direction, applied, picks, factors = call(
         functools.partial(first_kernel, sizes, dims, layers, count),
         "first_direction",
         (meta,),
         (coeffs, residual, rows, dual, *near),
-        [((fine_count, cases + tiles * half, LANES), BF16), full, half_full],
+        [((fine_count, cases + tiles * half, LANES), BF16), full, half_full, ((count * terms * half, subs * half), BF16),
+         ((count, terms * HALF, LANES), BF16)],
         theirs,
     )
     own = lax.all_to_all(message, "fine", 0, 0, tiled=True)
@@ -506,7 +514,7 @@
         functools.partial(second_kernel, sizes, dims, layers, count),
         "second_direction",
         (meta,),
-        (coeffs, residual, direction, applied, rows, dual, own, *others, *near),
+        (coeffs, residual, direction, applied, picks, factors, rows, dual, own, *others, *near),
         [((subs, cases + half, LANES), BF16), full, full, full, half_full],
         theirs + [pltpu.VMEM((subs, half, LANES), F32)],
     )

time: 67.6 us -> 66.7 us (0.987)
  blocking collectives: 34.4 us -> 35.5 us
  starting transfers between devices: 17.9 us -> 16.9 us
  waiting for transfers between devices: 3.01 us -> 2.26 us
    ppermute x1, starting transfers between devices: 4.03 us -> 3.02 us  [swap_blocks(): lax.ppermute(messages[PLANES], 'coarse', [(0, 1), (1, 0)])]
    all_to_all x2, blocking collectives: 22.5 us -> 23.5 us  [swap_all(): return lax.all_to_all(message, AXES, 0, 0, tiled=True)]
    ppermute x6, waiting for transfers between devices: 1.8 us -> 1.05 us  [swap_slot(): return lax.ppermute(message, 'fine', pairs)]
where the time goes in v7:
time: 66.7 us; the launch traced here: 66.4 us
  blocking collectives  35.5 us (53%)
  starting transfers between devices  16.9 us (25%)
  Pallas kernels  6.95 us (10%)
  local copies, waits for them, and re-layouts  2.48 us (4%)
  waiting for transfers between devices  2.26 us (3%)
  other arithmetic  1.67 us (3%)
  between operations  0.7 us (1%)
    all_to_all x2, blocking collectives, swap_all(): return lax.all_to_all(message, AXES, 0, 0, tiled=True)  23.5 us
    all_to_all x1, blocking collectives, body(): own = lax.all_to_all(message, 'fine', 0, 0, tiled=True)  11.9 us
    ppermute x6, starting transfers between devices, swap_slot(): return lax.ppermute(message, 'fine', pairs)  11.6 us
    pallas_call x6, Pallas kernels, call(): pl.pallas_call(kernel, name=name, out_shape=[jax.ShapeDtypeStruct(shape,...  6.95 us
    ppermute x1, starting transfers between devices, swap_blocks(): lax.ppermute(messages[PLANES], 'coarse', [(0, 1), (1, 0)])  3.02 us
    unnamed x4, local copies, waits for them, and re-layouts  2.48 us
    ppermute x1, starting transfers between devices, body(): others = [lax.ppermute(own, 'coarse', [(0, 1), (1, 0)])]  2.29 us
  transfers between devices with their start and end apart: 8, of which 2 were waited for; matrix products, arithmetic and copies ran while one was open for 0% of the time, Pallas kernels for 0%

profile of v7, /device:TPU:1, one launch (start us, length us, event | category | flops | bytes accessed | tf_op | source)
XLA Modules:
  0.0 66.4 jit_solution(7293560854807463684)
XLA Ops:
  0.6 0.9 %pad_maximum_fusion.rows_ref = bf16[64,1024]{1,0:T(8,128)(2,1)S(1)} fusion(bf16[48,1024]{1,0:T(8,128)(2,1)} %bitcast.5, bf16[16,1024]{1,0:T(8,128)(2,1)} %bitcast.6), kind=kLoop, calls=%fused_computation | loop fusion | flops 262144 | bytes 262144 | tf_op jit(solution)/shard_map/concatenate | solution.py:469
  1.5 0.8 %pad_add_fusion.meta_ref = s32[1,18]{1,0:T(1,128)S(1)} fusion(s32[1,4]{1,0:T(1,128)} %param.11, s32[1,8]{1,0:T(1,128)} %param.13, s32[1,6]{1,0:T(1,128)} %param.12), kind=kLoop, calls=%fused_computation.1 | loop fusion | flops 36 | bytes 144 | tf_op jit(solution)/shard_map/concatenate | solution.py:468
  2.3 0.0 copy-start.1
  2.3 0.9 %copy-done.1 = f32[1,4,48,48]{3,2,1,0:T(8,128)S(1)} copy-done((f32[1,4,48,48]{3,2,1,0:T(8,128)S(1)}, f32[1,4,48,48]{3,2,1,0:T(8,128)}, u32[]{:S(2)}) %copy-start.1) | copy-done | bytes 36888
  3.2 0.7 %pack_setup.1 = (bf16[216,128]{1,0:T(8,128)(2,1)S(1)}, bf16[216,128]{1,0:T(8,128)(2,1)S(1)}, bf16[216,128]{1,0:T(8,128)(2,1)S(1)}, bf16[216,128]{1,0:T(8,128)(2,...) custom-call(s32[1,18]{1,0:T(1,128)S(1)} %pad_add_fusion.meta_ref, ...), custom_call_target="tpu_custom_call" | custom-call | tf_op jit(solution)/shard_map/pack_setup/pallas_call | solution.py:425
  3.9 5.1 %collective-permute-start = (bf16[216,128]{1,0:T(8,128)(2,1)S(1)}, bf16[216,128]{1,0:T(8,128)(2,1)S(1)}, u32[]{:S(2)}, u32[]{:S(2)}) collective-permute-start(bf16[216,128]{1,0:T(8,128)(2,1)S(1)} %get-tuple-element.21), channel_id=1, source_target_pairs={{0,22},{2,12},{4,26},{6,16},{8,30},{10,20},{12,2},{14,24},{16,6},{... | collective-permute-start | bytes 165896 | tf_op jit(solution)/shard_map/ppermute | solution.py:453
  9.0 1.3 %collective-permute-start.1 = (bf16[216,128]{1,0:T(8,128)(2,1)S(1)}, bf16[216,128]{1,0:T(8,128)(2,1)S(1)}, u32[]{:S(2)}, u32[]{:S(2)}) collective-permute-start(bf16[216,128]{1,0:T(8,128)(2,1)S(1)} %get-tuple-element.22), channel_id=1, source_target_pairs={{0,18},{2,16},{4,22},{6,20},{8,26},{10,24},{12,30},{14,28},{16,2},... | collective-permute-start | bytes 165896 | tf_op jit(solution)/shard_map/ppermute | solution.py:453
  10.3 1.0 %collective-permute-start.2 = (bf16[216,128]{1,0:T(8,128)(2,1)S(1)}, bf16[216,128]{1,0:T(8,128)(2,1)S(1)}, u32[]{:S(2)}, u32[]{:S(2)}) collective-permute-start(bf16[216,128]{1,0:T(8,128)(2,1)S(1)} %get-tuple-element.23), channel_id=1, source_target_pairs={{0,14},{2,20},{4,18},{6,24},{8,22},{10,28},{12,26},{14,0},{16,30},... | collective-permute-start | bytes 165896 | tf_op jit(solution)/shard_map/ppermute | solution.py:453
  11.3 2.1 %collective-permute-start.3 = (bf16[216,128]{1,0:T(8,128)(2,1)S(1)}, bf16[216,128]{1,0:T(8,128)(2,1)S(1)}, u32[]{:S(2)}, u32[]{:S(2)}) collective-permute-start(bf16[216,128]{1,0:T(8,128)(2,1)S(1)} %get-tuple-element.24), channel_id=1, source_target_pairs={{0,6},{2,28},{4,10},{6,0},{8,14},{10,4},{12,18},{14,8},{16,22},{18... | collective-permute-start | bytes 165896 | tf_op jit(solution)/shard_map/ppermute | solution.py:453
  13.4 2.1 %collective-permute-start.4 = (bf16[216,128]{1,0:T(8,128)(2,1)S(1)}, bf16[216,128]{1,0:T(8,128)(2,1)S(1)}, u32[]{:S(2)}, u32[]{:S(2)}) collective-permute-start(bf16[216,128]{1,0:T(8,128)(2,1)S(1)} %get-tuple-element.25), channel_id=1, source_target_pairs={{0,10},{2,24},{4,14},{6,28},{8,18},{10,0},{12,22},{14,4},{16,26},{... | collective-permute-start | bytes 165896 | tf_op jit(solution)/shard_map/ppermute | solution.py:453
  15.5 0.0 collective-permute-done.refs_0_.refs_1_.refs_2_
  15.5 0.0 collective-permute-start.5
  15.5 0.0 collective-permute-done.1.refs_1_.refs_2_.refs_3_
  15.5 3.0 %collective-permute-start.6 = (bf16[216,128]{1,0:T(8,128)(2,1)S(1)}, bf16[216,128]{1,0:T(8,128)(2,1)S(1)}, u32[]{:S(2)}, u32[]{:S(2)}) collective-permute-start(bf16[216,128]{1,0:T(8,128)(2,1)S(1)} %get-tuple-element.27.after_ref.refs_0_.refs_1_), channel_id=1, source_target_pairs={{0,1},{1,0},{2,3},{3,2},{4,5},{5,4},{6,7},{7,6},{8,9},{9,8},{10,11... | collective-permute-start | bytes 165896 | tf_op jit(solution)/shard_map/ppermute | solution.py:458
  18.6 0.0 copy-start
  18.6 1.6 %copy-done = bf16[1,1024,1024]{2,1,0:T(8,128)(2,1)S(1)} copy-done((bf16[1,1024,1024]{2,1,0:T(8,128)(2,1)S(1)}, bf16[1,1024,1024]{2,1,0:T(8,128)(2,1)}, u32[]{:S(2)}) %copy-start) | copy-done | bytes 2097176
  20.2 0.1 fetch_dual.1.refs_7_.dual_ref
  20.3 0.0 collective-permute-done.2.refs_2_.refs_3_.refs_4_
  20.3 0.0 collective-permute-done.3.refs_3_.refs_4_.refs_5_
  20.3 0.0 collective-permute-done.4.refs_4_.refs_5_.refs_6_
  20.3 1.0 %collective-permute-done.5.refs_5_.refs_6_.refs_7_ = bf16[216,128]{1,0:T(8,128)(2,1)S(1)} collective-permute-done((bf16[216,128]{1,0:T(8,128)(2,1)S(1)}, bf16[216,128]{1,0:T(8,128)(2,1)S(1)}, u32[]{:S(2)}, u32[]{:S(2)}) %collective-permute-start.5) | collective-permute-done | bytes 55328 | tf_op jit(solution)/shard_map/ppermute | solution.py:453
  21.4 0.0 collective-permute-done.6.refs_6_.refs_7_.refs_8_
  21.4 0.7 %restrict_residual.1 = (f32[16,1024]{1,0:T(8,128)S(1)}, f32[32,8,128]{2,1,0:T(8,128)S(1)}) custom-call(s32[1,18]{1,0:T(1,128)S(1)} %pad_add_fusion.meta_ref, bf16[64,1024]{1,0:T(8,128)(2,1)S(1)} %pad_maximum_fusion.rows_ref, bf16[216,128]{1,0:T(8,128)(2,1)S(1)} %collective-permute-done.refs_0_.refs_1_.refs_2_, ...), custom_call_target="tpu_custom_call" | custom-call | tf_op jit(solution)/shard_map/restrict_residual/pallas_call | solution.py:425
  22.1 12.0 %all_to_all.15 = f32[32,8,128]{2,1,0:T(8,128)S(1)} all-to-all(f32[32,8,128]{2,1,0:T(8,128)S(1)} %get-tuple-element.28), channel_id=1, replica_groups=mesh['fine'=16,'coarse'=2] {'fine','coarse'}, dimensions={0} | all-to-all | bytes 262144 | tf_op jit(solution)/shard_map/all_to_all | solution.py:448
  34.1 1.9 %first_direction.1 = (bf16[16,72,128]{2,1,0:T(8,128)(2,1)S(1)}, f32[16,1024]{1,0:T(8,128)S(1)}, bf16[16,1024]{1,0:T(8,128)(2,1)S(1)}, bf16[256,256]{1,0:T(8,128)(2,1)S(1)}, bf16[8,256,128]{2,1,0:T(8,128)(2,1)S(1)}) custom-call(s32[1,18]{1,0:T(1,128)S(1)} %pad_add_fusion.meta_ref, f32[256,128]{1,0:T(8,128)S(1)} %bitcast.3, ...), custom_call_target="tpu_custom_call" | custom-call | tf_op jit(solution)/shard_map/first_direction/pallas_call | solution.py:425
  36.0 11.9 %all_to_all.16.own_ref = bf16[16,72,128]{2,1,0:T(8,128)(2,1)S(1)} all-to-all(bf16[16,72,128]{2,1,0:T(8,128)(2,1)S(1)} %get-tuple-element.34), channel_id=1, replica_groups=mesh['fine'=16,'coarse'=2] {'fine'}, dimensions={0} | all-to-all | bytes 589824 | tf_op jit(solution)/shard_map/all_to_all | solution.py:504
  47.9 2.3 %collective-permute-start.7 = (bf16[16,72,128]{2,1,0:T(8,128)(2,1)S(1)}, bf16[16,72,128]{2,1,0:T(8,128)(2,1)S(1)}, u32[]{:S(2)}, u32[]{:S(2)}) collective-permute-start(bf16[16,72,128]{2,1,0:T(8,128)(2,1)S(1)} %all_to_all.16.own_ref), channel_id=1, source_target_pairs={{0,1},{1,0},{2,3},{3,2},{4,5},{5,4},{6,7},{7,6},{8,9},{9,8},{10,11... | collective-permute-start | bytes 884744 | tf_op jit(solution)/shard_map/ppermute | solution.py:506
  50.2 1.2 %collective-permute-done.7.refs_0_ = bf16[16,72,128]{2,1,0:T(8,128)(2,1)S(1)} collective-permute-done((bf16[16,72,128]{2,1,0:T(8,128)(2,1)S(1)}, bf16[16,72,128]{2,1,0:T(8,128)(2,1)S(1)}, u32[]{:S(2)}, u32[]{:S(2)}) %collective-permute-start.7) | collective-permute-done | bytes 294944 | tf_op jit(solution)/shard_map/ppermute | solution.py:506
  51.4 2.0 %second_direction.1 = (bf16[32,24,128]{2,1,0:T(8,128)(2,1)S(1)}, f32[16,1024]{1,0:T(8,128)S(1)}, f32[16,1024]{1,0:T(8,128)S(1)}, f32[16,1024]{1,0:T(8,128)S(1)}, bf16[16,1024]{1,0:T(8,128)(2,1)S(1)}) custom-call(s32[1,18]{1,0:T(1,128)S(1)} %pad_add_fusion.meta_ref, f32[256,128]{1,0:T(8,128)S(1)} %bitcast.4, f32[16,1024]{1,0:T(8,128)S(1)} %get-tuple-element.29.residual_ref, ...), custom_call_target="tpu_custom_call" | custom-call | tf_op jit(solution)/shard_map/second_direction/pallas_call | solution.py:425
  53.4 11.5 %all_to_all.17.arrived_ref = bf16[32,24,128]{2,1,0:T(8,128)(2,1)S(1)} all-to-all(bf16[32,24,128]{2,1,0:T(8,128)(2,1)S(1)} %get-tuple-element.35), channel_id=1, replica_groups=mesh['fine'=16,'coarse'=2] {'fine','coarse'}, dimensions={0} | all-to-all | bytes 393216 | tf_op jit(solution)/shard_map/all_to_all | solution.py:448
  64.9 1.5 %finish.1 = (f32[1,16,1024]{2,1,0:T(8,128)}, f32[1,16,1024]{2,1,0:T(8,128)}) custom-call(s32[1,18]{1,0:T(1,128)S(1)} %pad_add_fusion.meta_ref, bf16[32,24,128]{2,1,0:T(8,128)(2,1)S(1)} %all_to_all.17.arrived_ref, bf16[16,1024]{1,0:T(8,128)(2,1)S(1)} %get-tuple-element.36.applied_ref, f32[16,1024]{1,0:T(8,128)S(1)} %get-tuple-element.37.residual_ref, ...), custom_call_target="tpu_custom_call" | custom-call | tf_op jit(solution)/shard_map/finish/pallas_call | solution.py:425
Async XLA Ops:
  2.3 0.9 %copy-start.1 = (f32[1,4,48,48]{3,2,1,0:T(8,128)S(1)}, f32[1,4,48,48]{3,2,1,0:T(8,128)}, u32[]{:S(2)}) copy-start(f32[1,4,48,48]{3,2,1,0:T(8,128)} %factors_ref.1) | copy-start | bytes 110596
  3.9 11.6 %collective-permute-start = (bf16[216,128]{1,0:T(8,128)(2,1)S(1)}, bf16[216,128]{1,0:T(8,128)(2,1)S(1)}, u32[]{:S(2)}, u32[]{:S(2)}) collective-permute-start(bf16[216,128]{1,0:T(8,128)(2,1)S(1)} %get-tuple-element.21), channel_id=1, source_target_pairs={{0,22},{2,12},{4,26},{6,16},{8,30},{10,20},{12,2},{14,24},{16,6},{... | collective-permute-start | bytes 165896 | tf_op jit(solution)/shard_map/ppermute | solution.py:453
  9.0 6.5 %collective-permute-start.1 = (bf16[216,128]{1,0:T(8,128)(2,1)S(1)}, bf16[216,128]{1,0:T(8,128)(2,1)S(1)}, u32[]{:S(2)}, u32[]{:S(2)}) collective-permute-start(bf16[216,128]{1,0:T(8,128)(2,1)S(1)} %get-tuple-element.22), channel_id=1, source_target_pairs={{0,18},{2,16},{4,22},{6,20},{8,26},{10,24},{12,30},{14,28},{16,2},... | collective-permute-start | bytes 165896 | tf_op jit(solution)/shard_map/ppermute | solution.py:453
  10.3 10.0 %collective-permute-start.2 = (bf16[216,128]{1,0:T(8,128)(2,1)S(1)}, bf16[216,128]{1,0:T(8,128)(2,1)S(1)}, u32[]{:S(2)}, u32[]{:S(2)}) collective-permute-start(bf16[216,128]{1,0:T(8,128)(2,1)S(1)} %get-tuple-element.23), channel_id=1, source_target_pairs={{0,14},{2,20},{4,18},{6,24},{8,22},{10,28},{12,26},{14,0},{16,30},... | collective-permute-start | bytes 165896 | tf_op jit(solution)/shard_map/ppermute | solution.py:453
  11.3 9.0 %collective-permute-start.3 = (bf16[216,128]{1,0:T(8,128)(2,1)S(1)}, bf16[216,128]{1,0:T(8,128)(2,1)S(1)}, u32[]{:S(2)}, u32[]{:S(2)}) collective-permute-start(bf16[216,128]{1,0:T(8,128)(2,1)S(1)} %get-tuple-element.24), channel_id=1, source_target_pairs={{0,6},{2,28},{4,10},{6,0},{8,14},{10,4},{12,18},{14,8},{16,22},{18... | collective-permute-start | bytes 165896 | tf_op jit(solution)/shard_map/ppermute | solution.py:453
  13.4 6.9 %collective-permute-start.4 = (bf16[216,128]{1,0:T(8,128)(2,1)S(1)}, bf16[216,128]{1,0:T(8,128)(2,1)S(1)}, u32[]{:S(2)}, u32[]{:S(2)}) collective-permute-start(bf16[216,128]{1,0:T(8,128)(2,1)S(1)} %get-tuple-element.25), channel_id=1, source_target_pairs={{0,10},{2,24},{4,14},{6,28},{8,18},{10,0},{12,22},{14,4},{16,26},{... | collective-permute-start | bytes 165896 | tf_op jit(solution)/shard_map/ppermute | solution.py:453
  15.5 5.9 %collective-permute-start.5 = (bf16[216,128]{1,0:T(8,128)(2,1)S(1)}, bf16[216,128]{1,0:T(8,128)(2,1)S(1)}, u32[]{:S(2)}, u32[]{:S(2)}) collective-permute-start(bf16[216,128]{1,0:T(8,128)(2,1)S(1)} %get-tuple-element.26), channel_id=1, source_target_pairs={{0,2},{2,0},{4,6},{6,4},{8,10},{10,8},{12,14},{14,12},{16,18},{18,... | collective-permute-start | bytes 165896 | tf_op jit(solution)/shard_map/ppermute | solution.py:453
  15.5 5.8 %collective-permute-start.6 = (bf16[216,128]{1,0:T(8,128)(2,1)S(1)}, bf16[216,128]{1,0:T(8,128)(2,1)S(1)}, u32[]{:S(2)}, u32[]{:S(2)}) collective-permute-start(bf16[216,128]{1,0:T(8,128)(2,1)S(1)} %get-tuple-element.27.after_ref.refs_0_.refs_1_), channel_id=1, source_target_pairs={{0,1},{1,0},{2,3},{3,2},{4,5},{5,4},{6,7},{7,6},{8,9},{9,8},{10,11... | collective-permute-start | bytes 165896 | tf_op jit(solution)/shard_map/ppermute | solution.py:458
  18.6 1.6 %copy-start = (bf16[1,1024,1024]{2,1,0:T(8,128)(2,1)S(1)}, bf16[1,1024,1024]{2,1,0:T(8,128)(2,1)}, u32[]{:S(2)}) copy-start(bf16[1,1024,1024]{2,1,0:T(8,128)(2,1)} %dual_ref.1) | copy-start | bytes 6291460
  47.9 3.5 %collective-permute-start.7 = (bf16[16,72,128]{2,1,0:T(8,128)(2,1)S(1)}, bf16[16,72,128]{2,1,0:T(8,128)(2,1)S(1)}, u32[]{:S(2)}, u32[]{:S(2)}) collective-permute-start(bf16[16,72,128]{2,1,0:T(8,128)(2,1)S(1)} %all_to_all.16.own_ref), channel_id=1, source_target_pairs={{0,1},{1,0},{2,3},{3,2},{4,5},{5,4},{6,7},{7,6},{8,9},{9,8},{10,11... | collective-permute-start | bytes 884744 | tf_op jit(solution)/shard_map/ppermute | solution.py:506

commit v8 on v7

--- a/solution.py
+++ b/solution.py
@@ -99,8 +99,24 @@
     return guest
 
 
-def pack_kernel(sizes, layers, cases, meta_ref, rows_ref, factors_ref, *outs):
+def pack_kernel(sizes, layers, partners_ref, counts_ref, pattern_ref, loads_ref, basis_ref, factors_hbm, *refs):
+    meta_out, rows_ref = refs[:2]
+    outs, (partners_smem, counts_smem, pattern_smem, loads, basis, factors_ref, sems) = refs[2:-7], refs[-7:]
+    sources = (partners_ref, counts_ref, pattern_ref, loads_ref, basis_ref, factors_hbm)
+    targets = (partners_smem, counts_smem, pattern_smem, loads, basis, factors_ref)
+    for copy in fetch(list(zip(sources, targets)), sems):
+        copy.wait()
     terms, modes = factors_ref.shape[1:3]
+    cases = loads.shape[1]
+    lane = lane_ids(1)
+    meta = jnp.zeros((1, LANES), jnp.int32)
+    scalars = [partners_smem[0, b] for b in range(PLANES)]
+    scalars += [counts_smem[0, b] for b in range(PLANES + 2)]
+    for place, scalar in enumerate(scalars):
+        meta = jnp.where(lane == place, scalar, meta)
+    meta_out[...] = meta
+    rows_ref[:cases, :] = loads[0]
+    rows_ref[cases:, :] = basis[0]
     gap = jnp.zeros((modes, HALF - modes), F32)
     parts = []
     for term in range(terms):
@@ -111,12 +127,12 @@
     row = lax.broadcasted_iota(jnp.int32, (8, LANES), 0)
     ids = jnp.zeros((8, LANES), F32)
     for term in range(terms):
-        sub = meta_ref[0, 2 * PLANES + 2 + term]
+        sub = pattern_smem[0, term]
         ids = jnp.where(row == term, (sub // 16).astype(F32), ids)
         ids = jnp.where(row == terms + term, (sub % 16).astype(F32), ids)
     ids = ids.astype(BF16)
     places = layout_of(terms, modes)
-    for out_ref, block in zip(outs, wanted_blocks(sizes, layers, meta_ref)):
+    for out_ref, block in zip(outs, wanted_blocks(sizes, layers, partners_smem)):
         out_ref[places["factors"], :] = factors
         out_ref[places["ids"], :] = ids
         out_ref[places["loads"], :] = rows_ref[:cases, lanes_of(block)]
@@ -132,8 +148,9 @@
     return places
 
 
-def dual_kernel(dual_ref, after_ref, out_ref, sems):
-    for copy in fetch([(dual_ref, out_ref)], sems):
+def stage_kernel(*refs):
+    sources, targets, sems = refs[: len(refs) // 2], refs[len(refs) // 2 : -1], refs[-1]
+    for copy in fetch(list(zip(sources, targets)), sems):
         copy.wait()
 
 
@@ -421,7 +438,7 @@
 ANY = pl.BlockSpec(memory_space=pl.ANY)
 
 
-def call(kernel, name, scalars, arrays, outs, scratch=(), far=(), after=()):
+def call(kernel, name, scalars, arrays, outs, scratch=(), far=(), after=(), vmem=40):
     return pl.pallas_call(
         kernel,
         name=name,
@@ -429,7 +446,7 @@
         in_specs=[SMEM] * len(scalars) + [VMEM] * len(arrays) + [HBM] * len(far) + [ANY] * len(after),
         out_specs=[VMEM] * len(outs),
         scratch_shapes=list(scratch),
-        compiler_params=pltpu.CompilerParams(vmem_limit_bytes=40 * 1024 * 1024),
+        compiler_params=pltpu.CompilerParams(vmem_limit_bytes=vmem * 1024 * 1024),
     )(*scalars, *arrays, *far, *after)
 
 
@@ -465,21 +482,28 @@
     coded = ((subs, half, LANES), F32)
     dma = pltpu.SemaphoreType.DMA
 
-    meta = jnp.concatenate([partners, row_counts, pattern], axis=1)
-    rows = jnp.concatenate([load_cases[0], coarse_basis[0]], axis=0)
-    packed = call(
-        functools.partial(pack_kernel, sizes, layers, cases),
+    inputs = (partners, row_counts, pattern, load_cases, coarse_basis, factor_blocks)
+    spaces = (pltpu.SMEM,) * 3 + (pltpu.VMEM,) * 3
+    meta, rows, *packed = call(
+        functools.partial(pack_kernel, sizes, layers),
         "pack_setup",
-        (meta,),
-        (rows, factor_blocks),
-        [((layout_of(terms, modes)["ids"].stop, LANES), BF16)] * (PLANES + layers),
+        (),
+        (),
+        [((1, LANES), jnp.int32), ((cases + modes, width), BF16)]
+        + [((layout_of(terms, modes)["ids"].stop, LANES), BF16)] * (PLANES + layers),
+        [space(array.shape, array.dtype) for space, array in zip(spaces, inputs)] + [dma((6,))],
+        inputs,
+        vmem=60,
     )
     received = swap_blocks(packed)
-    near = [packed[-1]] + received
+    staged = (dual_ops, meta, rows, packed[-1])
+    dual, meta, rows, mine = call(
+        stage_kernel, "stage_operands", (), (), [(array.shape, array.dtype) for array in staged], [dma((4,))], staged
+    )
+    near = [mine] + received
     count = len(near)
     theirs = [pltpu.VMEM((count - 1, cases, LANES), F32)]
 
-    [dual] = call(dual_kernel, "fetch_dual", (), (), [(dual_ops.shape, BF16)], [dma((1,))], (dual_ops,), (packed[-1],))
     residual, message = call(
         functools.partial(first_restrict_kernel, sizes, dims, layers),
         "restrict_residual",

time: 66.7 us -> 66.9 us (level)
  other arithmetic: 1.67 us -> 0 us
  Pallas kernels: 6.95 us -> 8.42 us
  local copies, waits for them, and re-layouts: 2.48 us -> 3.91 us
  waiting for transfers between devices: 2.26 us -> 1.23 us
    concatenate x2 -> x0, other arithmetic: 1.67 us -> none  [the longest x1 0.91 us: body(): rows = jnp.concatenate([load_cases[0], coarse_basis[0]], axis=0)]
    pallas_call x6, Pallas kernels: 6.95 us -> 8.42 us  [call(): pl.pallas_call(kernel, name=name, out_shape=[jax.ShapeDtypeStruct(shape,...]
    unnamed x4 -> x8, local copies, waits for them, and re-layouts: 2.48 us -> 3.91 us
    ppermute x6, waiting for transfers between devices: 1.05 us -> 0.02 us  [swap_slot(): return lax.ppermute(message, 'fine', pairs)]
  transfers between devices with their start and end apart: 8 -> 8, of which waited for: 2 -> 1; matrix products, arithmetic and copies ran while one was open for 0% -> 0% of each run, Pallas kernels for 0% -> 1%
where the time goes in v8:
time: 66.9 us; the launch traced here: 66.6 us
  blocking collectives  35.1 us (52%)
  starting transfers between devices  17.1 us (26%)
  Pallas kernels  8.42 us (13%)
  local copies, waits for them, and re-layouts  3.91 us (6%)
  waiting for transfers between devices  1.23 us (2%)
  between operations  0.72 us (1%)
    all_to_all x2, blocking collectives, swap_all(): return lax.all_to_all(message, AXES, 0, 0, tiled=True)  23.2 us
    all_to_all x1, blocking collectives, body(): own = lax.all_to_all(message, 'fine', 0, 0, tiled=True)  11.9 us
    ppermute x6, starting transfers between devices, swap_slot(): return lax.ppermute(message, 'fine', pairs)  11.6 us
    pallas_call x6, Pallas kernels, call(): pl.pallas_call(kernel, name=name, out_shape=[jax.ShapeDtypeStruct(shape,...  8.42 us
    unnamed x8, local copies, waits for them, and re-layouts  3.91 us
    ppermute x1, starting transfers between devices, swap_blocks(): lax.ppermute(messages[PLANES], 'coarse', [(0, 1), (1, 0)])  3.23 us
    ppermute x1, starting transfers between devices, body(): others = [lax.ppermute(own, 'coarse', [(0, 1), (1, 0)])]  2.3 us
  transfers between devices with their start and end apart: 8, of which 1 were waited for; matrix products, arithmetic and copies ran while one was open for 0% of the time, Pallas kernels for 1%

profile of v8, /device:TPU:1, one launch (start us, length us, event | category | flops | bytes accessed | tf_op | source)
XLA Modules:
  0.0 66.6 jit_solution(3765991425694039486)
XLA Ops:
  0.6 1.9 %pack_setup.1 = (s32[1,128]{1,0:T(1,128)}, bf16[64,1024]{1,0:T(8,128)(2,1)}, bf16[216,128]{1,0:T(8,128)(2,1)}, bf16[216,128]{1,0:T(8,128)(2,1)}, bf16[216,128]{1...) custom-call(s32[1,6]{1,0:T(1,128)} %partners_ref.1, ...), custom_call_target="tpu_custom_call" | custom-call | tf_op jit(solution)/shard_map/pack_setup/pallas_call | solution.py:442
  2.6 5.1 %collective-permute-start = (bf16[216,128]{1,0:T(8,128)(2,1)}, bf16[216,128]{1,0:T(8,128)(2,1)S(1)}, u32[]{:S(2)}, u32[]{:S(2)}) collective-permute-start(bf16[216,128]{1,0:T(8,128)(2,1)} %get-tuple-element.32), channel_id=1, source_target_pairs={{0,22},{2,12},{4,26},{6,16},{8,30},{10,20},{12,2},{14,24},{16,6},{... | collective-permute-start | bytes 165896 | tf_op jit(solution)/shard_map/ppermute | solution.py:470
  7.6 1.3 %collective-permute-start.1 = (bf16[216,128]{1,0:T(8,128)(2,1)}, bf16[216,128]{1,0:T(8,128)(2,1)S(1)}, u32[]{:S(2)}, u32[]{:S(2)}) collective-permute-start(bf16[216,128]{1,0:T(8,128)(2,1)} %get-tuple-element.33), channel_id=1, source_target_pairs={{0,18},{2,16},{4,22},{6,20},{8,26},{10,24},{12,30},{14,28},{16,2},... | collective-permute-start | bytes 165896 | tf_op jit(solution)/shard_map/ppermute | solution.py:470
  8.9 1.0 %collective-permute-start.2 = (bf16[216,128]{1,0:T(8,128)(2,1)}, bf16[216,128]{1,0:T(8,128)(2,1)S(1)}, u32[]{:S(2)}, u32[]{:S(2)}) collective-permute-start(bf16[216,128]{1,0:T(8,128)(2,1)} %get-tuple-element.34), channel_id=1, source_target_pairs={{0,14},{2,20},{4,18},{6,24},{8,22},{10,28},{12,26},{14,0},{16,30},... | collective-permute-start | bytes 165896 | tf_op jit(solution)/shard_map/ppermute | solution.py:470
  10.0 2.1 %collective-permute-start.3 = (bf16[216,128]{1,0:T(8,128)(2,1)}, bf16[216,128]{1,0:T(8,128)(2,1)S(1)}, u32[]{:S(2)}, u32[]{:S(2)}) collective-permute-start(bf16[216,128]{1,0:T(8,128)(2,1)} %get-tuple-element.35), channel_id=1, source_target_pairs={{0,6},{2,28},{4,10},{6,0},{8,14},{10,4},{12,18},{14,8},{16,22},{18... | collective-permute-start | bytes 165896 | tf_op jit(solution)/shard_map/ppermute | solution.py:470
  12.1 2.1 %collective-permute-start.4 = (bf16[216,128]{1,0:T(8,128)(2,1)}, bf16[216,128]{1,0:T(8,128)(2,1)S(1)}, u32[]{:S(2)}, u32[]{:S(2)}) collective-permute-start(bf16[216,128]{1,0:T(8,128)(2,1)} %get-tuple-element.36), channel_id=1, source_target_pairs={{0,10},{2,24},{4,14},{6,28},{8,18},{10,0},{12,22},{14,4},{16,26},{... | collective-permute-start | bytes 165896 | tf_op jit(solution)/shard_map/ppermute | solution.py:470
  14.2 0.0 collective-permute-done.refs_0_.refs_1_.refs_2_
  14.2 0.0 collective-permute-start.5
  14.2 0.0 collective-permute-done.1.refs_1_.refs_2_.refs_3_
  14.2 3.2 %collective-permute-start.6 = (bf16[216,128]{1,0:T(8,128)(2,1)}, bf16[216,128]{1,0:T(8,128)(2,1)S(1)}, u32[]{:S(2)}, u32[]{:S(2)}) collective-permute-start(bf16[216,128]{1,0:T(8,128)(2,1)} %get-tuple-element.29.refs_3_), channel_id=1, source_target_pairs={{0,1},{1,0},{2,3},{3,2},{4,5},{5,4},{6,7},{7,6},{8,9},{9,8},{10,11... | collective-permute-start | bytes 165896 | tf_op jit(solution)/shard_map/ppermute | solution.py:475
  17.4 0.0 copy-start
  17.4 1.6 %copy-done = bf16[1,1024,1024]{2,1,0:T(8,128)(2,1)S(1)} copy-done((bf16[1,1024,1024]{2,1,0:T(8,128)(2,1)S(1)}, bf16[1,1024,1024]{2,1,0:T(8,128)(2,1)}, u32[]{:S(2)}) %copy-start) | copy-done | bytes 2097176
  19.0 0.0 copy-start.1
  19.0 0.9 %copy-done.1 = bf16[64,1024]{1,0:T(8,128)(2,1)S(1)} copy-done((bf16[64,1024]{1,0:T(8,128)(2,1)S(1)}, bf16[64,1024]{1,0:T(8,128)(2,1)}, u32[]{:S(2)}) %copy-start.1) | copy-done | bytes 131096
  19.9 0.0 copy-start.2
  19.9 0.8 %copy-done.2 = bf16[216,128]{1,0:T(8,128)(2,1)S(1)} copy-done((bf16[216,128]{1,0:T(8,128)(2,1)S(1)}, bf16[216,128]{1,0:T(8,128)(2,1)}, u32[]{:S(2)}) %copy-start.2) | copy-done | bytes 55320
  20.7 0.0 copy-start.3
  20.7 0.6 copy-done.3
  21.3 0.4 stage_operands.1
  21.8 0.0 collective-permute-done.2.refs_2_.refs_3_.refs_4_
  21.8 0.0 collective-permute-done.3.refs_3_.refs_4_.refs_5_
  21.8 0.0 collective-permute-done.4.refs_4_.refs_5_.refs_6_
  21.8 0.0 collective-permute-done.5.refs_5_.refs_6_.refs_7_
  21.8 0.0 collective-permute-done.6.refs_6_.refs_7_.refs_8_
  21.8 0.7 %restrict_residual.1 = (f32[16,1024]{1,0:T(8,128)S(1)}, f32[32,8,128]{2,1,0:T(8,128)S(1)}) custom-call(s32[1,128]{1,0:T(1,128)S(1)} %get-tuple-element.30.meta_ref, bf16[64,1024]{1,0:T(8,128)(2,1)S(1)} %get-tuple-element.31.rows_ref, bf16[216,128]{1,0:T(8,128)(2,1)S(1)} %collective-permute-done.refs_0_.refs_1_.refs_2_, ...), custom_call_target="tpu_custom_call" | custom-call | tf_op jit(solution)/shard_map/restrict_residual/pallas_call | solution.py:442
  22.6 11.7 %all_to_all.15 = f32[32,8,128]{2,1,0:T(8,128)S(1)} all-to-all(f32[32,8,128]{2,1,0:T(8,128)S(1)} %get-tuple-element.39), channel_id=1, replica_groups=mesh['fine'=16,'coarse'=2] {'fine','coarse'}, dimensions={0} | all-to-all | bytes 262144 | tf_op jit(solution)/shard_map/all_to_all | solution.py:465
  34.2 1.9 %first_direction.1 = (bf16[16,72,128]{2,1,0:T(8,128)(2,1)S(1)}, f32[16,1024]{1,0:T(8,128)S(1)}, bf16[16,1024]{1,0:T(8,128)(2,1)S(1)}, bf16[256,256]{1,0:T(8,128)(2,1)S(1)}, bf16[8,256,128]{2,1,0:T(8,128)(2,1)S(1)}) custom-call(s32[1,128]{1,0:T(1,128)S(1)} %get-tuple-element.30.meta_ref, f32[256,128]{1,0:T(8,128)S(1)} %bitcast.1, ...), custom_call_target="tpu_custom_call" | custom-call | tf_op jit(solution)/shard_map/first_direction/pallas_call | solution.py:442
  36.1 11.9 %all_to_all.16.own_ref = bf16[16,72,128]{2,1,0:T(8,128)(2,1)S(1)} all-to-all(bf16[16,72,128]{2,1,0:T(8,128)(2,1)S(1)} %get-tuple-element.46), channel_id=1, replica_groups=mesh['fine'=16,'coarse'=2] {'fine'}, dimensions={0} | all-to-all | bytes 589824 | tf_op jit(solution)/shard_map/all_to_all | solution.py:528
  48.0 2.3 %collective-permute-start.7 = (bf16[16,72,128]{2,1,0:T(8,128)(2,1)S(1)}, bf16[16,72,128]{2,1,0:T(8,128)(2,1)S(1)}, u32[]{:S(2)}, u32[]{:S(2)}) collective-permute-start(bf16[16,72,128]{2,1,0:T(8,128)(2,1)S(1)} %all_to_all.16.own_ref), channel_id=1, source_target_pairs={{0,1},{1,0},{2,3},{3,2},{4,5},{5,4},{6,7},{7,6},{8,9},{9,8},{10,11... | collective-permute-start | bytes 884744 | tf_op jit(solution)/shard_map/ppermute | solution.py:530
  50.3 1.2 %collective-permute-done.7.refs_0_ = bf16[16,72,128]{2,1,0:T(8,128)(2,1)S(1)} collective-permute-done((bf16[16,72,128]{2,1,0:T(8,128)(2,1)S(1)}, bf16[16,72,128]{2,1,0:T(8,128)(2,1)S(1)}, u32[]{:S(2)}, u32[]{:S(2)}) %collective-permute-start.7) | collective-permute-done | bytes 294944 | tf_op jit(solution)/shard_map/ppermute | solution.py:530
  51.5 2.0 %second_direction.1 = (bf16[32,24,128]{2,1,0:T(8,128)(2,1)S(1)}, f32[16,1024]{1,0:T(8,128)S(1)}, f32[16,1024]{1,0:T(8,128)S(1)}, f32[16,1024]{1,0:T(8,128)S(1)}, bf16[16,1024]{1,0:T(8,128)(2,1)S(1)}) custom-call(s32[1,128]{1,0:T(1,128)S(1)} %get-tuple-element.30.meta_ref, f32[256,128]{1,0:T(8,128)S(1)} %bitcast.2, ...), custom_call_target="tpu_custom_call" | custom-call | tf_op jit(solution)/shard_map/second_direction/pallas_call | solution.py:442
  53.5 11.5 %all_to_all.17.arrived_ref = bf16[32,24,128]{2,1,0:T(8,128)(2,1)S(1)} all-to-all(bf16[32,24,128]{2,1,0:T(8,128)(2,1)S(1)} %get-tuple-element.47), channel_id=1, replica_groups=mesh['fine'=16,'coarse'=2] {'fine','coarse'}, dimensions={0} | all-to-all | bytes 393216 | tf_op jit(solution)/shard_map/all_to_all | solution.py:465
  65.0 1.5 %finish.1 = (f32[1,16,1024]{2,1,0:T(8,128)}, f32[1,16,1024]{2,1,0:T(8,128)}) custom-call(s32[1,128]{1,0:T(1,128)S(1)} %get-tuple-element.30.meta_ref, bf16[32,24,128]{2,1,0:T(8,128)(2,1)S(1)} %all_to_all.17.arrived_ref, bf16[16,1024]{1,0:T(8,128)(2,1)S(1)} %get-tuple-element.48.applied_ref, f32[16,1024]{1,0:T(8,128)S(1)} %get-tuple-element.49.residual_ref, ...), custom_call_target="tpu_custom_call" | custom-call | tf_op jit(solution)/shard_map/finish/pallas_call | solution.py:442
Async XLA Ops:
  2.6 11.6 %collective-permute-start = (bf16[216,128]{1,0:T(8,128)(2,1)}, bf16[216,128]{1,0:T(8,128)(2,1)S(1)}, u32[]{:S(2)}, u32[]{:S(2)}) collective-permute-start(bf16[216,128]{1,0:T(8,128)(2,1)} %get-tuple-element.32), channel_id=1, source_target_pairs={{0,22},{2,12},{4,26},{6,16},{8,30},{10,20},{12,2},{14,24},{16,6},{... | collective-permute-start | bytes 165896 | tf_op jit(solution)/shard_map/ppermute | solution.py:470
  7.6 6.5 %collective-permute-start.1 = (bf16[216,128]{1,0:T(8,128)(2,1)}, bf16[216,128]{1,0:T(8,128)(2,1)S(1)}, u32[]{:S(2)}, u32[]{:S(2)}) collective-permute-start(bf16[216,128]{1,0:T(8,128)(2,1)} %get-tuple-element.33), channel_id=1, source_target_pairs={{0,18},{2,16},{4,22},{6,20},{8,26},{10,24},{12,30},{14,28},{16,2},... | collective-permute-start | bytes 165896 | tf_op jit(solution)/shard_map/ppermute | solution.py:470
  8.9 12.9 %collective-permute-start.2 = (bf16[216,128]{1,0:T(8,128)(2,1)}, bf16[216,128]{1,0:T(8,128)(2,1)S(1)}, u32[]{:S(2)}, u32[]{:S(2)}) collective-permute-start(bf16[216,128]{1,0:T(8,128)(2,1)} %get-tuple-element.34), channel_id=1, source_target_pairs={{0,14},{2,20},{4,18},{6,24},{8,22},{10,28},{12,26},{14,0},{16,30},... | collective-permute-start | bytes 165896 | tf_op jit(solution)/shard_map/ppermute | solution.py:470
  10.0 11.8 %collective-permute-start.3 = (bf16[216,128]{1,0:T(8,128)(2,1)}, bf16[216,128]{1,0:T(8,128)(2,1)S(1)}, u32[]{:S(2)}, u32[]{:S(2)}) collective-permute-start(bf16[216,128]{1,0:T(8,128)(2,1)} %get-tuple-element.35), channel_id=1, source_target_pairs={{0,6},{2,28},{4,10},{6,0},{8,14},{10,4},{12,18},{14,8},{16,22},{18... | collective-permute-start | bytes 165896 | tf_op jit(solution)/shard_map/ppermute | solution.py:470
  12.1 9.7 %collective-permute-start.4 = (bf16[216,128]{1,0:T(8,128)(2,1)}, bf16[216,128]{1,0:T(8,128)(2,1)S(1)}, u32[]{:S(2)}, u32[]{:S(2)}) collective-permute-start(bf16[216,128]{1,0:T(8,128)(2,1)} %get-tuple-element.36), channel_id=1, source_target_pairs={{0,10},{2,24},{4,14},{6,28},{8,18},{10,0},{12,22},{14,4},{16,26},{... | collective-permute-start | bytes 165896 | tf_op jit(solution)/shard_map/ppermute | solution.py:470
  14.2 7.6 %collective-permute-start.5 = (bf16[216,128]{1,0:T(8,128)(2,1)}, bf16[216,128]{1,0:T(8,128)(2,1)S(1)}, u32[]{:S(2)}, u32[]{:S(2)}) collective-permute-start(bf16[216,128]{1,0:T(8,128)(2,1)} %get-tuple-element.37), channel_id=1, source_target_pairs={{0,2},{2,0},{4,6},{6,4},{8,10},{10,8},{12,14},{14,12},{16,18},{18,... | collective-permute-start | bytes 165896 | tf_op jit(solution)/shard_map/ppermute | solution.py:470
  14.2 7.6 %collective-permute-start.6 = (bf16[216,128]{1,0:T(8,128)(2,1)}, bf16[216,128]{1,0:T(8,128)(2,1)S(1)}, u32[]{:S(2)}, u32[]{:S(2)}) collective-permute-start(bf16[216,128]{1,0:T(8,128)(2,1)} %get-tuple-element.29.refs_3_), channel_id=1, source_target_pairs={{0,1},{1,0},{2,3},{3,2},{4,5},{5,4},{6,7},{7,6},{8,9},{9,8},{10,11... | collective-permute-start | bytes 165896 | tf_op jit(solution)/shard_map/ppermute | solution.py:475
  17.4 1.6 %copy-start = (bf16[1,1024,1024]{2,1,0:T(8,128)(2,1)S(1)}, bf16[1,1024,1024]{2,1,0:T(8,128)(2,1)}, u32[]{:S(2)}) copy-start(bf16[1,1024,1024]{2,1,0:T(8,128)(2,1)} %refs_0_.1) | copy-start | bytes 6291460
  19.0 0.9 %copy-start.1 = (bf16[64,1024]{1,0:T(8,128)(2,1)S(1)}, bf16[64,1024]{1,0:T(8,128)(2,1)}, u32[]{:S(2)}) copy-start(bf16[64,1024]{1,0:T(8,128)(2,1)} %get-tuple-element.28.refs_2_) | copy-start | bytes 393220
  19.9 0.8 %copy-start.2 = (bf16[216,128]{1,0:T(8,128)(2,1)S(1)}, bf16[216,128]{1,0:T(8,128)(2,1)}, u32[]{:S(2)}) copy-start(bf16[216,128]{1,0:T(8,128)(2,1)} %get-tuple-element.29.refs_3_) | copy-start | bytes 165892
  20.7 0.6 copy-start.3
  48.0 3.5 %collective-permute-start.7 = (bf16[16,72,128]{2,1,0:T(8,128)(2,1)S(1)}, bf16[16,72,128]{2,1,0:T(8,128)(2,1)S(1)}, u32[]{:S(2)}, u32[]{:S(2)}) collective-permute-start(bf16[16,72,128]{2,1,0:T(8,128)(2,1)S(1)} %all_to_all.16.own_ref), channel_id=1, source_target_pairs={{0,1},{1,0},{2,3},{3,2},{4,5},{5,4},{6,7},{7,6},{8,9},{9,8},{10,11... | collective-permute-start | bytes 884744 | tf_op jit(solution)/shard_map/ppermute | solution.py:530

commit v9 on v8

--- a/solution.py
+++ b/solution.py
@@ -14,6 +14,7 @@
 HALF = 64
 BF16 = jnp.bfloat16
 F32 = jnp.float32
+SPARE = 32
 GAMMA = 48
 DELTA = 49
 
@@ -100,23 +101,24 @@
 
 
 def pack_kernel(sizes, layers, partners_ref, counts_ref, pattern_ref, loads_ref, basis_ref, factors_hbm, *refs):
-    meta_out, rows_ref = refs[:2]
-    outs, (partners_smem, counts_smem, pattern_smem, loads, basis, factors_ref, sems) = refs[2:-7], refs[-7:]
+    rows_ref, outs = refs[0], refs[1:-7]
+    partners_smem, counts_smem, pattern_smem, loads, basis, factors_ref, sems = refs[-7:]
     sources = (partners_ref, counts_ref, pattern_ref, loads_ref, basis_ref, factors_hbm)
     targets = (partners_smem, counts_smem, pattern_smem, loads, basis, factors_ref)
     for copy in fetch(list(zip(sources, targets)), sems):
         copy.wait()
     terms, modes = factors_ref.shape[1:3]
     cases = loads.shape[1]
-    lane = lane_ids(1)
-    meta = jnp.zeros((1, LANES), jnp.int32)
+    lane = lane_ids(8)
+    row = lax.broadcasted_iota(jnp.int32, (8, LANES), 0)
+    digits = jnp.zeros((8, LANES), F32)
     scalars = [partners_smem[0, b] for b in range(PLANES)]
     scalars += [counts_smem[0, b] for b in range(PLANES + 2)]
     for place, scalar in enumerate(scalars):
-        meta = jnp.where(lane == place, scalar, meta)
-    meta_out[...] = meta
+        digit = jnp.where(row == 0, scalar // 16, scalar % 16).astype(F32)
+        digits = jnp.where(lane == place, digit, digits)
     rows_ref[:cases, :] = loads[0]
-    rows_ref[cases:, :] = basis[0]
+    rows_ref[cases : cases + modes, :] = basis[0]
     gap = jnp.zeros((modes, HALF - modes), F32)
     parts = []
     for term in range(terms):
@@ -124,7 +126,6 @@
         high = whole.astype(BF16).astype(F32)
         parts.append(jnp.concatenate([high, gap, whole - high, gap], axis=1))
     factors = jnp.concatenate(board(parts[:-1], parts[-1], modes), axis=0).astype(BF16)
-    row = lax.broadcasted_iota(jnp.int32, (8, LANES), 0)
     ids = jnp.zeros((8, LANES), F32)
     for term in range(terms):
         sub = pattern_smem[0, term]
@@ -132,11 +133,18 @@
         ids = jnp.where(row == terms + term, (sub % 16).astype(F32), ids)
     ids = ids.astype(BF16)
     places = layout_of(terms, modes)
+    start = cases + modes
+    depth = modes // 2
+    rows_ref[start:, :] = jnp.zeros_like(rows_ref[start:, :])
+    for group in range(2 * (terms - 1)):
+        rows_ref[start : start + depth, group * LANES : (group + 1) * LANES] = factors[group * depth : (group + 1) * depth]
+    rows_ref[start : start + 8, 6 * LANES : 7 * LANES] = ids
+    rows_ref[start : start + 8, 7 * LANES :] = digits.astype(BF16)
     for out_ref, block in zip(outs, wanted_blocks(sizes, layers, partners_smem)):
         out_ref[places["factors"], :] = factors
         out_ref[places["ids"], :] = ids
         out_ref[places["loads"], :] = rows_ref[:cases, lanes_of(block)]
-        out_ref[places["basis"], :] = rows_ref[cases:, lanes_of(block)]
+        out_ref[places["basis"], :] = rows_ref[cases:start, lanes_of(block)]
 
 
 def layout_of(terms, modes):
@@ -148,10 +156,26 @@
     return places
 
 
-def stage_kernel(*refs):
-    sources, targets, sems = refs[: len(refs) // 2], refs[len(refs) // 2 : -1], refs[-1]
-    for copy in fetch(list(zip(sources, targets)), sems):
-        copy.wait()
+def stage_kernel(start, dual_ref, rows_ref, dual_out, rows_out, meta_out, sems):
+    copies = fetch([(dual_ref, dual_out), (rows_ref, rows_out)], sems)
+    copies[1].wait()
+    digits = rows_out[start : start + 8, 7 * LANES :].astype(F32)
+    meta_out[...] = (digits[0:1] * 16.0 + digits[1:2]).astype(jnp.int32)
+    copies[0].wait()
+
+
+def basis_of(rows_ref, cases):
+    return rows_ref[cases : rows_ref.shape[0] - SPARE, :]
+
+
+def own_setup(dims, cases, rows_ref):
+    terms, modes = dims
+    start, depth = cases + modes, modes // 2
+    groups = [
+        rows_ref[start : start + depth, group * LANES : (group + 1) * LANES] for group in range(2 * (terms - 1))
+    ]
+    parts = [jnp.concatenate(groups[2 * term : 2 * term + 2], axis=0) for term in range(terms - 1)]
+    return parts, rows_ref[start : start + 8, 6 * LANES : 7 * LANES]
 
 
 def difference(counts_ref, mine, facing):
@@ -174,7 +198,7 @@
         scratch_ref[slot] = near_refs[slot][span, :]
     facing = [scratch_ref[slot_of(sizes, meta_ref[0, b])] for b in range(PLANES)]
     facing += [near_refs[PLANES][span, :], near_refs[-1][span, :]]
-    restrict(meta_ref, rows_ref[:cases, :], facing, rows_ref[cases:, :], out_ref, message_ref)
+    restrict(meta_ref, rows_ref[:cases, :], facing, basis_of(rows_ref, cases), out_ref, message_ref)
 
 
 def twice(basis):
@@ -220,10 +244,10 @@
     for block in range(PLANES + 2):
         part = applied_ref[:, block * LANES : (block + 1) * LANES].astype(F32)
         masked.append((part * live_mask(meta_ref, block)).astype(BF16))
-    own = fold(times_basis(jnp.concatenate(masked, axis=1), twice(rows_ref[cases:, :])))
+    own = fold(times_basis(jnp.concatenate(masked, axis=1), twice(basis_of(rows_ref, cases))))
     high = own.astype(BF16).astype(F32)
     tiles = []
-    for near_ref, block in zip(near_refs[1:], wanted_blocks(sizes, layers, meta_ref)):
+    for near_ref, block in zip(near_refs, wanted_blocks(sizes, layers, meta_ref)):
         part = applied_ref[:, lanes_of(block)].astype(F32) * live_mask(meta_ref, block)
         tiles.append(fold(times_basis(part.astype(BF16), twice(near_ref[span, :]))))
     modes = dims[1]
@@ -274,7 +298,7 @@
     return decode(totals)
 
 
-def prepare(sizes, dims, near_refs, picks_ref, factors_ref):
+def prepare(sizes, dims, cases, rows_ref, near_refs, picks_ref, factors_ref):
     terms, modes = dims
     places = layout_of(terms, modes)
     half = 8
@@ -282,8 +306,12 @@
     lanes = lane_ids(half).astype(F32)
     step = lax.broadcasted_iota(jnp.int32, (half, LANES), 0).astype(F32)
     gap = jnp.zeros((HALF - modes, LANES), BF16)
-    for index, near_ref in enumerate(near_refs):
-        ids = near_ref[places["ids"], :].astype(F32)
+    setups = [own_setup(dims, cases, rows_ref)]
+    for near_ref in near_refs:
+        parts = [near_ref[term * modes : (term + 1) * modes, :] for term in range(terms - 1)]
+        setups.append((parts, near_ref[places["ids"], :]))
+    for index, (packed, ids) in enumerate(setups):
+        ids = ids.astype(F32)
         ids = (ids[:terms] * 16.0 + ids[terms : 2 * terms]) * float(half)
         picks = []
         for term in range(terms):
@@ -293,8 +321,7 @@
             )
         rows = terms * half
         picks_ref[index * rows : (index + 1) * rows, :] = jnp.concatenate(picks, axis=0).astype(BF16)
-        packed = [near_ref[term * modes : (term + 1) * modes, :] for term in range(terms - 1)]
-        packed.append(alight([part.astype(F32) for part in packed], modes).astype(BF16))
+        packed = packed + [alight([part.astype(F32) for part in packed], modes).astype(BF16)]
         for term, part in enumerate(packed):
             factors_ref[index, term * HALF : term * HALF + modes, :] = part
             factors_ref[index, term * HALF + modes : (term + 1) * HALF, :] = gap
@@ -333,15 +360,15 @@
             direction_ref, applied_ref):
     span = layout_of(*dims)["basis"]
     solutions = solve(coeffs, dims, picks_ref, factors_ref)
-    mine = dot(solutions[0], rows_ref[residual.shape[0] :, :]).astype(BF16).astype(F32)
-    for index, near_ref in enumerate(near_refs[1:]):
+    mine = dot(solutions[0], basis_of(rows_ref, residual.shape[0])).astype(BF16).astype(F32)
+    for index, near_ref in enumerate(near_refs):
         theirs_ref[index] = dot(solutions[index + 1], near_ref[span, :]).astype(BF16).astype(F32)
     pieces = []
     for block in range(PLANES + 2):
         if block < PLANES:
             place = slot_of(sizes, meta_ref[0, block])
         else:
-            place = min(block, len(near_refs) - 2)
+            place = min(block, len(near_refs) - 1)
         here = slice(block * LANES, (block + 1) * LANES)
         pieces.append(residual[:, here] + live_mask(meta_ref, block) * (mine[:, here] - theirs_ref[place]))
     direction = jnp.concatenate(pieces, axis=1)
@@ -362,7 +389,7 @@
 def first_kernel(sizes, dims, layers, count, meta_ref, coeffs_ref, residual_ref, rows_ref, dual_ref, *refs):
     near_refs = refs[:count]
     message_ref, direction_ref, applied_ref, picks_ref, factors_ref, theirs_ref = refs[count:]
-    prepare(sizes, dims, near_refs, picks_ref, factors_ref)
+    prepare(sizes, dims, residual_ref.shape[0], rows_ref, near_refs, picks_ref, factors_ref)
     applied, sums = advance(
         sizes, dims, meta_ref, coeffs_ref[...], residual_ref[...], near_refs, picks_ref, factors_ref, rows_ref, dual_ref,
         theirs_ref, direction_ref, applied_ref,
@@ -484,25 +511,29 @@
 
     inputs = (partners, row_counts, pattern, load_cases, coarse_basis, factor_blocks)
     spaces = (pltpu.SMEM,) * 3 + (pltpu.VMEM,) * 3
-    meta, rows, *packed = call(
+    rows, *packed = call(
         functools.partial(pack_kernel, sizes, layers),
         "pack_setup",
         (),
         (),
-        [((1, LANES), jnp.int32), ((cases + modes, width), BF16)]
+        [((cases + modes + SPARE, width), BF16)]
         + [((layout_of(terms, modes)["ids"].stop, LANES), BF16)] * (PLANES + layers),
         [space(array.shape, array.dtype) for space, array in zip(spaces, inputs)] + [dma((6,))],
         inputs,
         vmem=60,
     )
     received = swap_blocks(packed)
-    staged = (dual_ops, meta, rows, packed[-1])
-    dual, meta, rows, mine = call(
-        stage_kernel, "stage_operands", (), (), [(array.shape, array.dtype) for array in staged], [dma((4,))], staged
-    )
-    near = [mine] + received
-    count = len(near)
-    theirs = [pltpu.VMEM((count - 1, cases, LANES), F32)]
+    dual, rows, meta = call(
+        functools.partial(stage_kernel, cases + modes),
+        "stage_operands",
+        (),
+        (),
+        [(dual_ops.shape, BF16), (rows.shape, BF16), ((1, LANES), jnp.int32)],
+        [dma((2,))],
+        (dual_ops, rows),
+    )
+    count = len(received)
+    theirs = [pltpu.VMEM((count, cases, LANES), F32)]
 
     residual, message = call(
         functools.partial(first_restrict_kernel, sizes, dims, layers),
@@ -520,9 +551,9 @@
         functools.partial(first_kernel, sizes, dims, layers, count),
         "first_direction",
         (meta,),
-        (coeffs, residual, rows, dual, *near),
-        [((fine_count, cases + tiles * half, LANES), BF16), full, half_full, ((count * terms * half, subs * half), BF16),
-         ((count, terms * HALF, LANES), BF16)],
+        (coeffs, residual, rows, dual, *received),
+        [((fine_count, cases + tiles * half, LANES), BF16), full, half_full, (((count + 1) * terms * half, subs * half), BF16),
+         ((count + 1, terms * HALF, LANES), BF16)],
         theirs,
     )
     own = lax.all_to_all(message, "fine", 0, 0, tiled=True)
@@ -538,7 +569,7 @@
         functools.partial(second_kernel, sizes, dims, layers, count),
         "second_direction",
         (meta,),
-        (coeffs, residual, direction, applied, picks, factors, rows, dual, own, *others, *near),
+        (coeffs, residual, direction, applied, picks, factors, rows, dual, own, *others, *received),
         [((subs, cases + half, LANES), BF16), full, full, full, half_full],
         theirs + [pltpu.VMEM((subs, half, LANES), F32)],
     )

time: 66.9 us -> 65.7 us (0.982)
  local copies, waits for them, and re-layouts: 3.91 us -> 2.52 us
    unnamed x8 -> x4, local copies, waits for them, and re-layouts: 3.91 us -> 2.52 us
where the time goes in v9:
time: 65.7 us; the launch traced here: 65.4 us
  blocking collectives  35.3 us (54%)
  starting transfers between devices  17.1 us (26%)
  Pallas kernels  8.56 us (13%)
  local copies, waits for them, and re-layouts  2.52 us (4%)
  waiting for transfers between devices  1.23 us (2%)
  between operations  0.72 us (1%)
    all_to_all x2, blocking collectives, swap_all(): return lax.all_to_all(message, AXES, 0, 0, tiled=True)  23.4 us
    all_to_all x1, blocking collectives, body(): own = lax.all_to_all(message, 'fine', 0, 0, tiled=True)  11.9 us
    ppermute x6, starting transfers between devices, swap_slot(): return lax.ppermute(message, 'fine', pairs)  11.6 us
    pallas_call x6, Pallas kernels, call(): pl.pallas_call(kernel, name=name, out_shape=[jax.ShapeDtypeStruct(shape,...  8.56 us
    ppermute x1, starting transfers between devices, swap_blocks(): lax.ppermute(messages[PLANES], 'coarse', [(0, 1), (1, 0)])  3.23 us
    unnamed x4, local copies, waits for them, and re-layouts  2.52 us
    ppermute x1, starting transfers between devices, body(): others = [lax.ppermute(own, 'coarse', [(0, 1), (1, 0)])]  2.3 us
  transfers between devices with their start and end apart: 8, of which 1 were waited for; matrix products, arithmetic and copies ran while one was open for 0% of the time, Pallas kernels for 1%

profile of v9, /device:TPU:1, one launch (start us, length us, event | category | flops | bytes accessed | tf_op | source)
XLA Modules:
  0.0 65.4 jit_solution(14683620702416908366)
XLA Ops:
  0.6 2.1 %pack_setup.1 = (bf16[96,1024]{1,0:T(8,128)(2,1)}, bf16[216,128]{1,0:T(8,128)(2,1)}, bf16[216,128]{1,0:T(8,128)(2,1)}, bf16[216,128]{1,0:T(8,128)(2,1)}, bf16[21...) custom-call(s32[1,6]{1,0:T(1,128)} %partners_ref.1, ...), custom_call_target="tpu_custom_call" | custom-call | tf_op jit(solution)/shard_map/pack_setup/pallas_call | solution.py:469
  2.7 5.1 %collective-permute-start = (bf16[216,128]{1,0:T(8,128)(2,1)}, bf16[216,128]{1,0:T(8,128)(2,1)S(1)}, u32[]{:S(2)}, u32[]{:S(2)}) collective-permute-start(bf16[216,128]{1,0:T(8,128)(2,1)} %get-tuple-element.28), channel_id=1, source_target_pairs={{0,22},{2,12},{4,26},{6,16},{8,30},{10,20},{12,2},{14,24},{16,6},{... | collective-permute-start | bytes 165896 | tf_op jit(solution)/shard_map/ppermute | solution.py:497
  7.8 1.3 %collective-permute-start.1 = (bf16[216,128]{1,0:T(8,128)(2,1)}, bf16[216,128]{1,0:T(8,128)(2,1)S(1)}, u32[]{:S(2)}, u32[]{:S(2)}) collective-permute-start(bf16[216,128]{1,0:T(8,128)(2,1)} %get-tuple-element.29), channel_id=1, source_target_pairs={{0,18},{2,16},{4,22},{6,20},{8,26},{10,24},{12,30},{14,28},{16,2},... | collective-permute-start | bytes 165896 | tf_op jit(solution)/shard_map/ppermute | solution.py:497
  9.1 1.0 %collective-permute-start.2 = (bf16[216,128]{1,0:T(8,128)(2,1)}, bf16[216,128]{1,0:T(8,128)(2,1)S(1)}, u32[]{:S(2)}, u32[]{:S(2)}) collective-permute-start(bf16[216,128]{1,0:T(8,128)(2,1)} %get-tuple-element.30), channel_id=1, source_target_pairs={{0,14},{2,20},{4,18},{6,24},{8,22},{10,28},{12,26},{14,0},{16,30},... | collective-permute-start | bytes 165896 | tf_op jit(solution)/shard_map/ppermute | solution.py:497
  10.1 2.1 %collective-permute-start.3 = (bf16[216,128]{1,0:T(8,128)(2,1)}, bf16[216,128]{1,0:T(8,128)(2,1)S(1)}, u32[]{:S(2)}, u32[]{:S(2)}) collective-permute-start(bf16[216,128]{1,0:T(8,128)(2,1)} %get-tuple-element.31), channel_id=1, source_target_pairs={{0,6},{2,28},{4,10},{6,0},{8,14},{10,4},{12,18},{14,8},{16,22},{18... | collective-permute-start | bytes 165896 | tf_op jit(solution)/shard_map/ppermute | solution.py:497
  12.2 2.1 %collective-permute-start.4 = (bf16[216,128]{1,0:T(8,128)(2,1)}, bf16[216,128]{1,0:T(8,128)(2,1)S(1)}, u32[]{:S(2)}, u32[]{:S(2)}) collective-permute-start(bf16[216,128]{1,0:T(8,128)(2,1)} %get-tuple-element.32), channel_id=1, source_target_pairs={{0,10},{2,24},{4,14},{6,28},{8,18},{10,0},{12,22},{14,4},{16,26},{... | collective-permute-start | bytes 165896 | tf_op jit(solution)/shard_map/ppermute | solution.py:497
  14.3 0.0 collective-permute-done.refs_0_.refs_1_
  14.3 0.0 collective-permute-start.5
  14.3 0.0 collective-permute-done.1.refs_1_.refs_2_
  14.3 3.2 %collective-permute-start.6 = (bf16[216,128]{1,0:T(8,128)(2,1)}, bf16[216,128]{1,0:T(8,128)(2,1)S(1)}, u32[]{:S(2)}, u32[]{:S(2)}) collective-permute-start(bf16[216,128]{1,0:T(8,128)(2,1)} %get-tuple-element.34), channel_id=1, source_target_pairs={{0,1},{1,0},{2,3},{3,2},{4,5},{5,4},{6,7},{7,6},{8,9},{9,8},{10,11... | collective-permute-start | bytes 165896 | tf_op jit(solution)/shard_map/ppermute | solution.py:502
  17.6 0.0 copy-start
  17.6 1.6 %copy-done = bf16[1,1024,1024]{2,1,0:T(8,128)(2,1)S(1)} copy-done((bf16[1,1024,1024]{2,1,0:T(8,128)(2,1)S(1)}, bf16[1,1024,1024]{2,1,0:T(8,128)(2,1)}, u32[]{:S(2)}) %copy-start) | copy-done | bytes 2097176
  19.2 0.0 copy-start.1
  19.2 0.9 %copy-done.1 = bf16[96,1024]{1,0:T(8,128)(2,1)S(1)} copy-done((bf16[96,1024]{1,0:T(8,128)(2,1)S(1)}, bf16[96,1024]{1,0:T(8,128)(2,1)}, u32[]{:S(2)}) %copy-start.1) | copy-done | bytes 196632
  20.1 0.4 stage_operands.1
  20.5 0.0 collective-permute-done.2.refs_2_.refs_3_
  20.5 0.0 collective-permute-done.3.refs_3_.refs_4_
  20.5 0.0 collective-permute-done.4.refs_4_.refs_5_
  20.5 0.0 collective-permute-done.5.refs_5_.refs_6_
  20.5 0.0 collective-permute-done.6.refs_6_.refs_7_
  20.6 0.7 %restrict_residual.1 = (f32[16,1024]{1,0:T(8,128)S(1)}, f32[32,8,128]{2,1,0:T(8,128)S(1)}) custom-call(s32[1,128]{1,0:T(1,128)S(1)} %get-tuple-element.26.meta_ref, bf16[96,1024]{1,0:T(8,128)(2,1)S(1)} %get-tuple-element.27.rows_ref, bf16[216,128]{1,0:T(8,128)(2,1)S(1)} %collective-permute-done.refs_0_.refs_1_, ...), custom_call_target="tpu_custom_call" | custom-call | tf_op jit(solution)/shard_map/restrict_residual/pallas_call | solution.py:469
  21.3 11.8 %all_to_all.15 = f32[32,8,128]{2,1,0:T(8,128)S(1)} all-to-all(f32[32,8,128]{2,1,0:T(8,128)S(1)} %get-tuple-element.36), channel_id=1, replica_groups=mesh['fine'=16,'coarse'=2] {'fine','coarse'}, dimensions={0} | all-to-all | bytes 262144 | tf_op jit(solution)/shard_map/all_to_all | solution.py:492
  33.1 1.9 %first_direction.1 = (bf16[16,72,128]{2,1,0:T(8,128)(2,1)S(1)}, f32[16,1024]{1,0:T(8,128)S(1)}, bf16[16,1024]{1,0:T(8,128)(2,1)S(1)}, bf16[256,256]{1,0:T(8,128)(2,1)S(1)}, bf16[8,256,128]{2,1,0:T(8,128)(2,1)S(1)}) custom-call(s32[1,128]{1,0:T(1,128)S(1)} %get-tuple-element.26.meta_ref, f32[256,128]{1,0:T(8,128)S(1)} %bitcast.1, ...), custom_call_target="tpu_custom_call" | custom-call | tf_op jit(solution)/shard_map/first_direction/pallas_call | solution.py:469
  35.0 11.9 %all_to_all.16.own_ref = bf16[16,72,128]{2,1,0:T(8,128)(2,1)S(1)} all-to-all(bf16[16,72,128]{2,1,0:T(8,128)(2,1)S(1)} %get-tuple-element.42), channel_id=1, replica_groups=mesh['fine'=16,'coarse'=2] {'fine'}, dimensions={0} | all-to-all | bytes 589824 | tf_op jit(solution)/shard_map/all_to_all | solution.py:559
  46.9 2.3 %collective-permute-start.7 = (bf16[16,72,128]{2,1,0:T(8,128)(2,1)S(1)}, bf16[16,72,128]{2,1,0:T(8,128)(2,1)S(1)}, u32[]{:S(2)}, u32[]{:S(2)}) collective-permute-start(bf16[16,72,128]{2,1,0:T(8,128)(2,1)S(1)} %all_to_all.16.own_ref), channel_id=1, source_target_pairs={{0,1},{1,0},{2,3},{3,2},{4,5},{5,4},{6,7},{7,6},{8,9},{9,8},{10,11... | collective-permute-start | bytes 884744 | tf_op jit(solution)/shard_map/ppermute | solution.py:561
  49.2 1.2 %collective-permute-done.7.refs_0_ = bf16[16,72,128]{2,1,0:T(8,128)(2,1)S(1)} collective-permute-done((bf16[16,72,128]{2,1,0:T(8,128)(2,1)S(1)}, bf16[16,72,128]{2,1,0:T(8,128)(2,1)S(1)}, u32[]{:S(2)}, u32[]{:S(2)}) %collective-permute-start.7) | collective-permute-done | bytes 294944 | tf_op jit(solution)/shard_map/ppermute | solution.py:561
  50.4 2.0 %second_direction.1 = (bf16[32,24,128]{2,1,0:T(8,128)(2,1)S(1)}, f32[16,1024]{1,0:T(8,128)S(1)}, f32[16,1024]{1,0:T(8,128)S(1)}, f32[16,1024]{1,0:T(8,128)S(1)}, bf16[16,1024]{1,0:T(8,128)(2,1)S(1)}) custom-call(s32[1,128]{1,0:T(1,128)S(1)} %get-tuple-element.26.meta_ref, f32[256,128]{1,0:T(8,128)S(1)} %bitcast.2, ...), custom_call_target="tpu_custom_call" | custom-call | tf_op jit(solution)/shard_map/second_direction/pallas_call | solution.py:469
  52.4 11.5 %all_to_all.17.arrived_ref = bf16[32,24,128]{2,1,0:T(8,128)(2,1)S(1)} all-to-all(bf16[32,24,128]{2,1,0:T(8,128)(2,1)S(1)} %get-tuple-element.43), channel_id=1, replica_groups=mesh['fine'=16,'coarse'=2] {'fine','coarse'}, dimensions={0} | all-to-all | bytes 393216 | tf_op jit(solution)/shard_map/all_to_all | solution.py:492
  63.9 1.5 %finish.1 = (f32[1,16,1024]{2,1,0:T(8,128)}, f32[1,16,1024]{2,1,0:T(8,128)}) custom-call(s32[1,128]{1,0:T(1,128)S(1)} %get-tuple-element.26.meta_ref, bf16[32,24,128]{2,1,0:T(8,128)(2,1)S(1)} %all_to_all.17.arrived_ref, bf16[16,1024]{1,0:T(8,128)(2,1)S(1)} %get-tuple-element.44.applied_ref, f32[16,1024]{1,0:T(8,128)S(1)} %get-tuple-element.45.residual_ref, ...), custom_call_target="tpu_custom_call" | custom-call | tf_op jit(solution)/shard_map/finish/pallas_call | solution.py:469
Async XLA Ops:
  2.7 11.6 %collective-permute-start = (bf16[216,128]{1,0:T(8,128)(2,1)}, bf16[216,128]{1,0:T(8,128)(2,1)S(1)}, u32[]{:S(2)}, u32[]{:S(2)}) collective-permute-start(bf16[216,128]{1,0:T(8,128)(2,1)} %get-tuple-element.28), channel_id=1, source_target_pairs={{0,22},{2,12},{4,26},{6,16},{8,30},{10,20},{12,2},{14,24},{16,6},{... | collective-permute-start | bytes 165896 | tf_op jit(solution)/shard_map/ppermute | solution.py:497
  7.8 6.5 %collective-permute-start.1 = (bf16[216,128]{1,0:T(8,128)(2,1)}, bf16[216,128]{1,0:T(8,128)(2,1)S(1)}, u32[]{:S(2)}, u32[]{:S(2)}) collective-permute-start(bf16[216,128]{1,0:T(8,128)(2,1)} %get-tuple-element.29), channel_id=1, source_target_pairs={{0,18},{2,16},{4,22},{6,20},{8,26},{10,24},{12,30},{14,28},{16,2},... | collective-permute-start | bytes 165896 | tf_op jit(solution)/shard_map/ppermute | solution.py:497
  9.1 11.5 %collective-permute-start.2 = (bf16[216,128]{1,0:T(8,128)(2,1)}, bf16[216,128]{1,0:T(8,128)(2,1)S(1)}, u32[]{:S(2)}, u32[]{:S(2)}) collective-permute-start(bf16[216,128]{1,0:T(8,128)(2,1)} %get-tuple-element.30), channel_id=1, source_target_pairs={{0,14},{2,20},{4,18},{6,24},{8,22},{10,28},{12,26},{14,0},{16,30},... | collective-permute-start | bytes 165896 | tf_op jit(solution)/shard_map/ppermute | solution.py:497
  10.1 10.4 %collective-permute-start.3 = (bf16[216,128]{1,0:T(8,128)(2,1)}, bf16[216,128]{1,0:T(8,128)(2,1)S(1)}, u32[]{:S(2)}, u32[]{:S(2)}) collective-permute-start(bf16[216,128]{1,0:T(8,128)(2,1)} %get-tuple-element.31), channel_id=1, source_target_pairs={{0,6},{2,28},{4,10},{6,0},{8,14},{10,4},{12,18},{14,8},{16,22},{18... | collective-permute-start | bytes 165896 | tf_op jit(solution)/shard_map/ppermute | solution.py:497
  12.2 8.3 %collective-permute-start.4 = (bf16[216,128]{1,0:T(8,128)(2,1)}, bf16[216,128]{1,0:T(8,128)(2,1)S(1)}, u32[]{:S(2)}, u32[]{:S(2)}) collective-permute-start(bf16[216,128]{1,0:T(8,128)(2,1)} %get-tuple-element.32), channel_id=1, source_target_pairs={{0,10},{2,24},{4,14},{6,28},{8,18},{10,0},{12,22},{14,4},{16,26},{... | collective-permute-start | bytes 165896 | tf_op jit(solution)/shard_map/ppermute | solution.py:497
  14.3 6.2 %collective-permute-start.5 = (bf16[216,128]{1,0:T(8,128)(2,1)}, bf16[216,128]{1,0:T(8,128)(2,1)S(1)}, u32[]{:S(2)}, u32[]{:S(2)}) collective-permute-start(bf16[216,128]{1,0:T(8,128)(2,1)} %get-tuple-element.33), channel_id=1, source_target_pairs={{0,2},{2,0},{4,6},{6,4},{8,10},{10,8},{12,14},{14,12},{16,18},{18,... | collective-permute-start | bytes 165896 | tf_op jit(solution)/shard_map/ppermute | solution.py:497
  14.3 6.2 %collective-permute-start.6 = (bf16[216,128]{1,0:T(8,128)(2,1)}, bf16[216,128]{1,0:T(8,128)(2,1)S(1)}, u32[]{:S(2)}, u32[]{:S(2)}) collective-permute-start(bf16[216,128]{1,0:T(8,128)(2,1)} %get-tuple-element.34), channel_id=1, source_target_pairs={{0,1},{1,0},{2,3},{3,2},{4,5},{5,4},{6,7},{7,6},{8,9},{9,8},{10,11... | collective-permute-start | bytes 165896 | tf_op jit(solution)/shard_map/ppermute | solution.py:502
  17.6 1.6 %copy-start = (bf16[1,1024,1024]{2,1,0:T(8,128)(2,1)S(1)}, bf16[1,1024,1024]{2,1,0:T(8,128)(2,1)}, u32[]{:S(2)}) copy-start(bf16[1,1024,1024]{2,1,0:T(8,128)(2,1)} %dual_ref.1) | copy-start | bytes 6291460
  19.2 0.9 %copy-start.1 = (bf16[96,1024]{1,0:T(8,128)(2,1)S(1)}, bf16[96,1024]{1,0:T(8,128)(2,1)}, u32[]{:S(2)}) copy-start(bf16[96,1024]{1,0:T(8,128)(2,1)} %get-tuple-element.25.rows_ref) | copy-start | bytes 589828
  46.9 3.5 %collective-permute-start.7 = (bf16[16,72,128]{2,1,0:T(8,128)(2,1)S(1)}, bf16[16,72,128]{2,1,0:T(8,128)(2,1)S(1)}, u32[]{:S(2)}, u32[]{:S(2)}) collective-permute-start(bf16[16,72,128]{2,1,0:T(8,128)(2,1)S(1)} %all_to_all.16.own_ref), channel_id=1, source_target_pairs={{0,1},{1,0},{2,3},{3,2},{4,5},{5,4},{6,7},{7,6},{8,9},{9,8},{10,11... | collective-permute-start | bytes 884744 | tf_op jit(solution)/shard_map/ppermute | solution.py:561

commit v10 on v9

--- a/solution.py
+++ b/solution.py
@@ -8,7 +8,7 @@
 from jax.sharding import PartitionSpec as P
 
 PLANES = 6
-DISTANCES = (11, 9, 7, 3, 5, 1)
+DISTANCES = (11, 7, 3, 5, 9, 1)
 AXES = ("fine", "coarse")
 LANES = 128
 HALF = 64

time: 65.7 us -> 65 us (0.989)
  starting transfers between devices: 17.1 us -> 15.5 us
  blocking collectives: 35.3 us -> 36.2 us
    all_to_all x2, blocking collectives: 23.4 us -> 24.2 us  [swap_all(): return lax.all_to_all(message, AXES, 0, 0, tiled=True)]
    ppermute x1, starting transfers between devices: 3.23 us -> 2.36 us  [swap_blocks(): lax.ppermute(messages[PLANES], 'coarse', [(0, 1), (1, 0)])]
    ppermute x6, starting transfers between devices: 11.6 us -> 10.9 us  [swap_slot(): return lax.ppermute(message, 'fine', pairs)]
where the time goes in v10:
time: 65 us; the launch traced here: 64.7 us
  blocking collectives  36.2 us (56%)
  starting transfers between devices  15.5 us (24%)
  Pallas kernels  8.55 us (13%)
  local copies, waits for them, and re-layouts  2.52 us (4%)
  waiting for transfers between devices  1.23 us (2%)
  between operations  0.72 us (1%)
    all_to_all x2, blocking collectives, swap_all(): return lax.all_to_all(message, AXES, 0, 0, tiled=True)  24.2 us
    all_to_all x1, blocking collectives, body(): own = lax.all_to_all(message, 'fine', 0, 0, tiled=True)  11.9 us
    ppermute x6, starting transfers between devices, swap_slot(): return lax.ppermute(message, 'fine', pairs)  10.9 us
    pallas_call x6, Pallas kernels, call(): pl.pallas_call(kernel, name=name, out_shape=[jax.ShapeDtypeStruct(shape,...  8.55 us
    unnamed x4, local copies, waits for them, and re-layouts  2.52 us
    ppermute x1, starting transfers between devices, swap_blocks(): lax.ppermute(messages[PLANES], 'coarse', [(0, 1), (1, 0)])  2.36 us
    ppermute x1, starting transfers between devices, body(): others = [lax.ppermute(own, 'coarse', [(0, 1), (1, 0)])]  2.3 us
  transfers between devices with their start and end apart: 8, of which 1 were waited for; matrix products, arithmetic and copies ran while one was open for 0% of the time, Pallas kernels for 1%

profile of v10, /device:TPU:1, one launch (start us, length us, event | category | flops | bytes accessed | tf_op | source)
XLA Modules:
  0.0 64.7 jit_solution(7429702959692883747)
XLA Ops:
  0.6 2.1 %pack_setup.1 = (bf16[96,1024]{1,0:T(8,128)(2,1)}, bf16[216,128]{1,0:T(8,128)(2,1)}, bf16[216,128]{1,0:T(8,128)(2,1)}, bf16[216,128]{1,0:T(8,128)(2,1)}, bf16[21...) custom-call(s32[1,6]{1,0:T(1,128)} %partners_ref.1, ...), custom_call_target="tpu_custom_call" | custom-call | tf_op jit(solution)/shard_map/pack_setup/pallas_call | solution.py:469
  2.7 5.1 %collective-permute-start = (bf16[216,128]{1,0:T(8,128)(2,1)}, bf16[216,128]{1,0:T(8,128)(2,1)S(1)}, u32[]{:S(2)}, u32[]{:S(2)}) collective-permute-start(bf16[216,128]{1,0:T(8,128)(2,1)} %get-tuple-element.28), channel_id=1, source_target_pairs={{0,22},{2,12},{4,26},{6,16},{8,30},{10,20},{12,2},{14,24},{16,6},{... | collective-permute-start | bytes 165896 | tf_op jit(solution)/shard_map/ppermute | solution.py:497
  7.8 1.2 %collective-permute-start.1 = (bf16[216,128]{1,0:T(8,128)(2,1)}, bf16[216,128]{1,0:T(8,128)(2,1)S(1)}, u32[]{:S(2)}, u32[]{:S(2)}) collective-permute-start(bf16[216,128]{1,0:T(8,128)(2,1)} %get-tuple-element.29), channel_id=1, source_target_pairs={{0,14},{2,20},{4,18},{6,24},{8,22},{10,28},{12,26},{14,0},{16,30},... | collective-permute-start | bytes 165896 | tf_op jit(solution)/shard_map/ppermute | solution.py:497
  9.0 1.9 %collective-permute-start.2 = (bf16[216,128]{1,0:T(8,128)(2,1)}, bf16[216,128]{1,0:T(8,128)(2,1)S(1)}, u32[]{:S(2)}, u32[]{:S(2)}) collective-permute-start(bf16[216,128]{1,0:T(8,128)(2,1)} %get-tuple-element.30), channel_id=1, source_target_pairs={{0,6},{2,28},{4,10},{6,0},{8,14},{10,4},{12,18},{14,8},{16,22},{18... | collective-permute-start | bytes 165896 | tf_op jit(solution)/shard_map/ppermute | solution.py:497
  10.9 1.4 %collective-permute-start.3 = (bf16[216,128]{1,0:T(8,128)(2,1)}, bf16[216,128]{1,0:T(8,128)(2,1)S(1)}, u32[]{:S(2)}, u32[]{:S(2)}) collective-permute-start(bf16[216,128]{1,0:T(8,128)(2,1)} %get-tuple-element.31), channel_id=1, source_target_pairs={{0,10},{2,24},{4,14},{6,28},{8,18},{10,0},{12,22},{14,4},{16,26},{... | collective-permute-start | bytes 165896 | tf_op jit(solution)/shard_map/ppermute | solution.py:497
  12.3 1.1 %collective-permute-start.4 = (bf16[216,128]{1,0:T(8,128)(2,1)}, bf16[216,128]{1,0:T(8,128)(2,1)S(1)}, u32[]{:S(2)}, u32[]{:S(2)}) collective-permute-start(bf16[216,128]{1,0:T(8,128)(2,1)} %get-tuple-element.32), channel_id=1, source_target_pairs={{0,18},{2,16},{4,22},{6,20},{8,26},{10,24},{12,30},{14,28},{16,2},... | collective-permute-start | bytes 165896 | tf_op jit(solution)/shard_map/ppermute | solution.py:497
  13.4 0.0 collective-permute-done.refs_0_.refs_1_
  13.4 0.1 collective-permute-start.5
  13.6 0.0 collective-permute-done.1.refs_1_.refs_2_
  13.6 2.4 %collective-permute-start.6 = (bf16[216,128]{1,0:T(8,128)(2,1)}, bf16[216,128]{1,0:T(8,128)(2,1)S(1)}, u32[]{:S(2)}, u32[]{:S(2)}) collective-permute-start(bf16[216,128]{1,0:T(8,128)(2,1)} %get-tuple-element.34), channel_id=1, source_target_pairs={{0,1},{1,0},{2,3},{3,2},{4,5},{5,4},{6,7},{7,6},{8,9},{9,8},{10,11... | collective-permute-start | bytes 165896 | tf_op jit(solution)/shard_map/ppermute | solution.py:502
  15.9 0.0 copy-start
  15.9 1.6 %copy-done = bf16[1,1024,1024]{2,1,0:T(8,128)(2,1)S(1)} copy-done((bf16[1,1024,1024]{2,1,0:T(8,128)(2,1)S(1)}, bf16[1,1024,1024]{2,1,0:T(8,128)(2,1)}, u32[]{:S(2)}) %copy-start) | copy-done | bytes 2097176
  17.5 0.0 copy-start.1
  17.5 0.9 %copy-done.1 = bf16[96,1024]{1,0:T(8,128)(2,1)S(1)} copy-done((bf16[96,1024]{1,0:T(8,128)(2,1)S(1)}, bf16[96,1024]{1,0:T(8,128)(2,1)}, u32[]{:S(2)}) %copy-start.1) | copy-done | bytes 196632
  18.4 0.4 stage_operands.1
  18.9 0.0 collective-permute-done.2.refs_2_.refs_3_
  18.9 0.0 collective-permute-done.3.refs_3_.refs_4_
  18.9 0.0 collective-permute-done.4.refs_4_.refs_5_
  18.9 0.0 collective-permute-done.5.refs_5_.refs_6_
  18.9 0.0 collective-permute-done.6.refs_6_.refs_7_
  18.9 0.7 %restrict_residual.1 = (f32[16,1024]{1,0:T(8,128)S(1)}, f32[32,8,128]{2,1,0:T(8,128)S(1)}) custom-call(s32[1,128]{1,0:T(1,128)S(1)} %get-tuple-element.26.meta_ref, bf16[96,1024]{1,0:T(8,128)(2,1)S(1)} %get-tuple-element.27.rows_ref, bf16[216,128]{1,0:T(8,128)(2,1)S(1)} %collective-permute-done.refs_0_.refs_1_, ...), custom_call_target="tpu_custom_call" | custom-call | tf_op jit(solution)/shard_map/restrict_residual/pallas_call | solution.py:469
  19.7 12.7 %all_to_all.15 = f32[32,8,128]{2,1,0:T(8,128)S(1)} all-to-all(f32[32,8,128]{2,1,0:T(8,128)S(1)} %get-tuple-element.36), channel_id=1, replica_groups=mesh['fine'=16,'coarse'=2] {'fine','coarse'}, dimensions={0} | all-to-all | bytes 262144 | tf_op jit(solution)/shard_map/all_to_all | solution.py:492
  32.4 1.9 %first_direction.1 = (bf16[16,72,128]{2,1,0:T(8,128)(2,1)S(1)}, f32[16,1024]{1,0:T(8,128)S(1)}, bf16[16,1024]{1,0:T(8,128)(2,1)S(1)}, bf16[256,256]{1,0:T(8,128)(2,1)S(1)}, bf16[8,256,128]{2,1,0:T(8,128)(2,1)S(1)}) custom-call(s32[1,128]{1,0:T(1,128)S(1)} %get-tuple-element.26.meta_ref, f32[256,128]{1,0:T(8,128)S(1)} %bitcast.1, ...), custom_call_target="tpu_custom_call" | custom-call | tf_op jit(solution)/shard_map/first_direction/pallas_call | solution.py:469
  34.2 11.9 %all_to_all.16.own_ref = bf16[16,72,128]{2,1,0:T(8,128)(2,1)S(1)} all-to-all(bf16[16,72,128]{2,1,0:T(8,128)(2,1)S(1)} %get-tuple-element.42), channel_id=1, replica_groups=mesh['fine'=16,'coarse'=2] {'fine'}, dimensions={0} | all-to-all | bytes 589824 | tf_op jit(solution)/shard_map/all_to_all | solution.py:559
  46.2 2.3 %collective-permute-start.7 = (bf16[16,72,128]{2,1,0:T(8,128)(2,1)S(1)}, bf16[16,72,128]{2,1,0:T(8,128)(2,1)S(1)}, u32[]{:S(2)}, u32[]{:S(2)}) collective-permute-start(bf16[16,72,128]{2,1,0:T(8,128)(2,1)S(1)} %all_to_all.16.own_ref), channel_id=1, source_target_pairs={{0,1},{1,0},{2,3},{3,2},{4,5},{5,4},{6,7},{7,6},{8,9},{9,8},{10,11... | collective-permute-start | bytes 884744 | tf_op jit(solution)/shard_map/ppermute | solution.py:561
  48.4 1.2 %collective-permute-done.7.refs_0_ = bf16[16,72,128]{2,1,0:T(8,128)(2,1)S(1)} collective-permute-done((bf16[16,72,128]{2,1,0:T(8,128)(2,1)S(1)}, bf16[16,72,128]{2,1,0:T(8,128)(2,1)S(1)}, u32[]{:S(2)}, u32[]{:S(2)}) %collective-permute-start.7) | collective-permute-done | bytes 294944 | tf_op jit(solution)/shard_map/ppermute | solution.py:561
  49.7 2.0 %second_direction.1 = (bf16[32,24,128]{2,1,0:T(8,128)(2,1)S(1)}, f32[16,1024]{1,0:T(8,128)S(1)}, f32[16,1024]{1,0:T(8,128)S(1)}, f32[16,1024]{1,0:T(8,128)S(1)}, bf16[16,1024]{1,0:T(8,128)(2,1)S(1)}) custom-call(s32[1,128]{1,0:T(1,128)S(1)} %get-tuple-element.26.meta_ref, f32[256,128]{1,0:T(8,128)S(1)} %bitcast.2, ...), custom_call_target="tpu_custom_call" | custom-call | tf_op jit(solution)/shard_map/second_direction/pallas_call | solution.py:469
  51.6 11.5 %all_to_all.17.arrived_ref = bf16[32,24,128]{2,1,0:T(8,128)(2,1)S(1)} all-to-all(bf16[32,24,128]{2,1,0:T(8,128)(2,1)S(1)} %get-tuple-element.43), channel_id=1, replica_groups=mesh['fine'=16,'coarse'=2] {'fine','coarse'}, dimensions={0} | all-to-all | bytes 393216 | tf_op jit(solution)/shard_map/all_to_all | solution.py:492
  63.2 1.5 %finish.1 = (f32[1,16,1024]{2,1,0:T(8,128)}, f32[1,16,1024]{2,1,0:T(8,128)}) custom-call(s32[1,128]{1,0:T(1,128)S(1)} %get-tuple-element.26.meta_ref, bf16[32,24,128]{2,1,0:T(8,128)(2,1)S(1)} %all_to_all.17.arrived_ref, bf16[16,1024]{1,0:T(8,128)(2,1)S(1)} %get-tuple-element.44.applied_ref, f32[16,1024]{1,0:T(8,128)S(1)} %get-tuple-element.45.residual_ref, ...), custom_call_target="tpu_custom_call" | custom-call | tf_op jit(solution)/shard_map/finish/pallas_call | solution.py:469
Async XLA Ops:
  2.7 10.7 %collective-permute-start = (bf16[216,128]{1,0:T(8,128)(2,1)}, bf16[216,128]{1,0:T(8,128)(2,1)S(1)}, u32[]{:S(2)}, u32[]{:S(2)}) collective-permute-start(bf16[216,128]{1,0:T(8,128)(2,1)} %get-tuple-element.28), channel_id=1, source_target_pairs={{0,22},{2,12},{4,26},{6,16},{8,30},{10,20},{12,2},{14,24},{16,6},{... | collective-permute-start | bytes 165896 | tf_op jit(solution)/shard_map/ppermute | solution.py:497
  7.8 5.8 %collective-permute-start.1 = (bf16[216,128]{1,0:T(8,128)(2,1)}, bf16[216,128]{1,0:T(8,128)(2,1)S(1)}, u32[]{:S(2)}, u32[]{:S(2)}) collective-permute-start(bf16[216,128]{1,0:T(8,128)(2,1)} %get-tuple-element.29), channel_id=1, source_target_pairs={{0,14},{2,20},{4,18},{6,24},{8,22},{10,28},{12,26},{14,0},{16,30},... | collective-permute-start | bytes 165896 | tf_op jit(solution)/shard_map/ppermute | solution.py:497
  9.0 9.9 %collective-permute-start.2 = (bf16[216,128]{1,0:T(8,128)(2,1)}, bf16[216,128]{1,0:T(8,128)(2,1)S(1)}, u32[]{:S(2)}, u32[]{:S(2)}) collective-permute-start(bf16[216,128]{1,0:T(8,128)(2,1)} %get-tuple-element.30), channel_id=1, source_target_pairs={{0,6},{2,28},{4,10},{6,0},{8,14},{10,4},{12,18},{14,8},{16,22},{18... | collective-permute-start | bytes 165896 | tf_op jit(solution)/shard_map/ppermute | solution.py:497
  10.9 7.9 %collective-permute-start.3 = (bf16[216,128]{1,0:T(8,128)(2,1)}, bf16[216,128]{1,0:T(8,128)(2,1)S(1)}, u32[]{:S(2)}, u32[]{:S(2)}) collective-permute-start(bf16[216,128]{1,0:T(8,128)(2,1)} %get-tuple-element.31), channel_id=1, source_target_pairs={{0,10},{2,24},{4,14},{6,28},{8,18},{10,0},{12,22},{14,4},{16,26},{... | collective-permute-start | bytes 165896 | tf_op jit(solution)/shard_map/ppermute | solution.py:497
  12.3 6.6 %collective-permute-start.4 = (bf16[216,128]{1,0:T(8,128)(2,1)}, bf16[216,128]{1,0:T(8,128)(2,1)S(1)}, u32[]{:S(2)}, u32[]{:S(2)}) collective-permute-start(bf16[216,128]{1,0:T(8,128)(2,1)} %get-tuple-element.32), channel_id=1, source_target_pairs={{0,18},{2,16},{4,22},{6,20},{8,26},{10,24},{12,30},{14,28},{16,2},... | collective-permute-start | bytes 165896 | tf_op jit(solution)/shard_map/ppermute | solution.py:497
  13.4 5.5 %collective-permute-start.5 = (bf16[216,128]{1,0:T(8,128)(2,1)}, bf16[216,128]{1,0:T(8,128)(2,1)S(1)}, u32[]{:S(2)}, u32[]{:S(2)}) collective-permute-start(bf16[216,128]{1,0:T(8,128)(2,1)} %get-tuple-element.33), channel_id=1, source_target_pairs={{0,2},{2,0},{4,6},{6,4},{8,10},{10,8},{12,14},{14,12},{16,18},{18,... | collective-permute-start | bytes 165896 | tf_op jit(solution)/shard_map/ppermute | solution.py:497
  13.6 5.3 %collective-permute-start.6 = (bf16[216,128]{1,0:T(8,128)(2,1)}, bf16[216,128]{1,0:T(8,128)(2,1)S(1)}, u32[]{:S(2)}, u32[]{:S(2)}) collective-permute-start(bf16[216,128]{1,0:T(8,128)(2,1)} %get-tuple-element.34), channel_id=1, source_target_pairs={{0,1},{1,0},{2,3},{3,2},{4,5},{5,4},{6,7},{7,6},{8,9},{9,8},{10,11... | collective-permute-start | bytes 165896 | tf_op jit(solution)/shard_map/ppermute | solution.py:502
  15.9 1.6 %copy-start = (bf16[1,1024,1024]{2,1,0:T(8,128)(2,1)S(1)}, bf16[1,1024,1024]{2,1,0:T(8,128)(2,1)}, u32[]{:S(2)}) copy-start(bf16[1,1024,1024]{2,1,0:T(8,128)(2,1)} %dual_ref.1) | copy-start | bytes 6291460
  17.5 0.9 %copy-start.1 = (bf16[96,1024]{1,0:T(8,128)(2,1)S(1)}, bf16[96,1024]{1,0:T(8,128)(2,1)}, u32[]{:S(2)}) copy-start(bf16[96,1024]{1,0:T(8,128)(2,1)} %get-tuple-element.25.rows_ref) | copy-start | bytes 589828
  46.2 3.5 %collective-permute-start.7 = (bf16[16,72,128]{2,1,0:T(8,128)(2,1)S(1)}, bf16[16,72,128]{2,1,0:T(8,128)(2,1)S(1)}, u32[]{:S(2)}, u32[]{:S(2)}) collective-permute-start(bf16[16,72,128]{2,1,0:T(8,128)(2,1)S(1)} %all_to_all.16.own_ref), channel_id=1, source_target_pairs={{0,1},{1,0},{2,3},{3,2},{4,5},{5,4},{6,7},{7,6},{8,9},{9,8},{10,11... | collective-permute-start | bytes 884744 | tf_op jit(solution)/shard_map/ppermute | solution.py:561

commit v11 on v10

--- a/solution.py
+++ b/solution.py
@@ -8,7 +8,7 @@
 from jax.sharding import PartitionSpec as P
 
 PLANES = 6
-DISTANCES = (11, 7, 3, 5, 9, 1)
+DISTANCES = (7, 11, 3, 5, 9, 1)
 AXES = ("fine", "coarse")
 LANES = 128
 HALF = 64

time: 65 us -> 65.7 us (1.011)
  starting transfers between devices: 15.5 us -> 16.6 us
    ppermute x6, starting transfers between devices: 10.9 us -> 12 us  [swap_slot(): return lax.ppermute(message, 'fine', pairs)]
where the time goes in v11:
time: 65.7 us; the launch traced here: 65.5 us
  blocking collectives  35.8 us (54%)
  starting transfers between devices  16.6 us (25%)
  Pallas kernels  8.56 us (13%)
  local copies, waits for them, and re-layouts  2.52 us (4%)
  waiting for transfers between devices  1.23 us (2%)
  between operations  0.72 us (1%)
    all_to_all x2, blocking collectives, swap_all(): return lax.all_to_all(message, AXES, 0, 0, tiled=True)  23.9 us
    ppermute x6, starting transfers between devices, swap_slot(): return lax.ppermute(message, 'fine', pairs)  12 us
    all_to_all x1, blocking collectives, body(): own = lax.all_to_all(message, 'fine', 0, 0, tiled=True)  11.9 us
    pallas_call x6, Pallas kernels, call(): pl.pallas_call(kernel, name=name, out_shape=[jax.ShapeDtypeStruct(shape,...  8.56 us
    unnamed x4, local copies, waits for them, and re-layouts  2.52 us
    ppermute x1, starting transfers between devices, swap_blocks(): lax.ppermute(messages[PLANES], 'coarse', [(0, 1), (1, 0)])  2.36 us
    ppermute x1, starting transfers between devices, body(): others = [lax.ppermute(own, 'coarse', [(0, 1), (1, 0)])]  2.29 us
  transfers between devices with their start and end apart: 8, of which 1 were waited for; matrix products, arithmetic and copies ran while one was open for 0% of the time, Pallas kernels for 1%

profile of v11, /device:TPU:1, one launch (start us, length us, event | category | flops | bytes accessed | tf_op | source)
XLA Modules:
  0.0 65.5 jit_solution(4172789209192031779)
XLA Ops:
  0.6 2.1 %pack_setup.1 = (bf16[96,1024]{1,0:T(8,128)(2,1)}, bf16[216,128]{1,0:T(8,128)(2,1)}, bf16[216,128]{1,0:T(8,128)(2,1)}, bf16[216,128]{1,0:T(8,128)(2,1)}, bf16[21...) custom-call(s32[1,6]{1,0:T(1,128)} %partners_ref.1, ...), custom_call_target="tpu_custom_call" | custom-call | tf_op jit(solution)/shard_map/pack_setup/pallas_call | solution.py:469
  2.7 4.1 %collective-permute-start = (bf16[216,128]{1,0:T(8,128)(2,1)}, bf16[216,128]{1,0:T(8,128)(2,1)S(1)}, u32[]{:S(2)}, u32[]{:S(2)}) collective-permute-start(bf16[216,128]{1,0:T(8,128)(2,1)} %get-tuple-element.28), channel_id=1, source_target_pairs={{0,14},{2,20},{4,18},{6,24},{8,22},{10,28},{12,26},{14,0},{16,30},... | collective-permute-start | bytes 165896 | tf_op jit(solution)/shard_map/ppermute | solution.py:497
  6.8 1.1 %collective-permute-start.1 = (bf16[216,128]{1,0:T(8,128)(2,1)}, bf16[216,128]{1,0:T(8,128)(2,1)S(1)}, u32[]{:S(2)}, u32[]{:S(2)}) collective-permute-start(bf16[216,128]{1,0:T(8,128)(2,1)} %get-tuple-element.29), channel_id=1, source_target_pairs={{0,22},{2,12},{4,26},{6,16},{8,30},{10,20},{12,2},{14,24},{16,6},{... | collective-permute-start | bytes 165896 | tf_op jit(solution)/shard_map/ppermute | solution.py:497
  7.9 3.3 %collective-permute-start.2 = (bf16[216,128]{1,0:T(8,128)(2,1)}, bf16[216,128]{1,0:T(8,128)(2,1)S(1)}, u32[]{:S(2)}, u32[]{:S(2)}) collective-permute-start(bf16[216,128]{1,0:T(8,128)(2,1)} %get-tuple-element.30), channel_id=1, source_target_pairs={{0,6},{2,28},{4,10},{6,0},{8,14},{10,4},{12,18},{14,8},{16,22},{18... | collective-permute-start | bytes 165896 | tf_op jit(solution)/shard_map/ppermute | solution.py:497
  11.2 0.9 %collective-permute-start.3 = (bf16[216,128]{1,0:T(8,128)(2,1)}, bf16[216,128]{1,0:T(8,128)(2,1)S(1)}, u32[]{:S(2)}, u32[]{:S(2)}) collective-permute-start(bf16[216,128]{1,0:T(8,128)(2,1)} %get-tuple-element.31), channel_id=1, source_target_pairs={{0,10},{2,24},{4,14},{6,28},{8,18},{10,0},{12,22},{14,4},{16,26},{... | collective-permute-start | bytes 165896 | tf_op jit(solution)/shard_map/ppermute | solution.py:497
  12.1 1.1 %collective-permute-start.4 = (bf16[216,128]{1,0:T(8,128)(2,1)}, bf16[216,128]{1,0:T(8,128)(2,1)S(1)}, u32[]{:S(2)}, u32[]{:S(2)}) collective-permute-start(bf16[216,128]{1,0:T(8,128)(2,1)} %get-tuple-element.32), channel_id=1, source_target_pairs={{0,18},{2,16},{4,22},{6,20},{8,26},{10,24},{12,30},{14,28},{16,2},... | collective-permute-start | bytes 165896 | tf_op jit(solution)/shard_map/ppermute | solution.py:497
  13.2 0.0 collective-permute-done.refs_0_.refs_1_
  13.2 1.5 %collective-permute-start.5 = (bf16[216,128]{1,0:T(8,128)(2,1)}, bf16[216,128]{1,0:T(8,128)(2,1)S(1)}, u32[]{:S(2)}, u32[]{:S(2)}) collective-permute-start(bf16[216,128]{1,0:T(8,128)(2,1)} %get-tuple-element.33), channel_id=1, source_target_pairs={{0,2},{2,0},{4,6},{6,4},{8,10},{10,8},{12,14},{14,12},{16,18},{18,... | collective-permute-start | bytes 165896 | tf_op jit(solution)/shard_map/ppermute | solution.py:497
  14.7 0.0 collective-permute-done.1.refs_1_.refs_2_
  14.7 2.4 %collective-permute-start.6 = (bf16[216,128]{1,0:T(8,128)(2,1)}, bf16[216,128]{1,0:T(8,128)(2,1)S(1)}, u32[]{:S(2)}, u32[]{:S(2)}) collective-permute-start(bf16[216,128]{1,0:T(8,128)(2,1)} %get-tuple-element.34), channel_id=1, source_target_pairs={{0,1},{1,0},{2,3},{3,2},{4,5},{5,4},{6,7},{7,6},{8,9},{9,8},{10,11... | collective-permute-start | bytes 165896 | tf_op jit(solution)/shard_map/ppermute | solution.py:502
  17.0 0.0 copy-start
  17.0 1.6 %copy-done = bf16[1,1024,1024]{2,1,0:T(8,128)(2,1)S(1)} copy-done((bf16[1,1024,1024]{2,1,0:T(8,128)(2,1)S(1)}, bf16[1,1024,1024]{2,1,0:T(8,128)(2,1)}, u32[]{:S(2)}) %copy-start) | copy-done | bytes 2097176
  18.6 0.0 copy-start.1
  18.6 0.9 %copy-done.1 = bf16[96,1024]{1,0:T(8,128)(2,1)S(1)} copy-done((bf16[96,1024]{1,0:T(8,128)(2,1)S(1)}, bf16[96,1024]{1,0:T(8,128)(2,1)}, u32[]{:S(2)}) %copy-start.1) | copy-done | bytes 196632
  19.6 0.4 stage_operands.1
  20.0 0.0 collective-permute-done.2.refs_2_.refs_3_
  20.0 0.0 collective-permute-done.3.refs_3_.refs_4_
  20.0 0.0 collective-permute-done.4.refs_4_.refs_5_
  20.0 0.0 collective-permute-done.5.refs_5_.refs_6_
  20.0 0.0 collective-permute-done.6.refs_6_.refs_7_
  20.0 0.7 %restrict_residual.1 = (f32[16,1024]{1,0:T(8,128)S(1)}, f32[32,8,128]{2,1,0:T(8,128)S(1)}) custom-call(s32[1,128]{1,0:T(1,128)S(1)} %get-tuple-element.26.meta_ref, bf16[96,1024]{1,0:T(8,128)(2,1)S(1)} %get-tuple-element.27.rows_ref, bf16[216,128]{1,0:T(8,128)(2,1)S(1)} %collective-permute-done.refs_0_.refs_1_, ...), custom_call_target="tpu_custom_call" | custom-call | tf_op jit(solution)/shard_map/restrict_residual/pallas_call | solution.py:469
  20.8 12.4 %all_to_all.15 = f32[32,8,128]{2,1,0:T(8,128)S(1)} all-to-all(f32[32,8,128]{2,1,0:T(8,128)S(1)} %get-tuple-element.36), channel_id=1, replica_groups=mesh['fine'=16,'coarse'=2] {'fine','coarse'}, dimensions={0} | all-to-all | bytes 262144 | tf_op jit(solution)/shard_map/all_to_all | solution.py:492
  33.1 1.9 %first_direction.1 = (bf16[16,72,128]{2,1,0:T(8,128)(2,1)S(1)}, f32[16,1024]{1,0:T(8,128)S(1)}, bf16[16,1024]{1,0:T(8,128)(2,1)S(1)}, bf16[256,256]{1,0:T(8,128)(2,1)S(1)}, bf16[8,256,128]{2,1,0:T(8,128)(2,1)S(1)}) custom-call(s32[1,128]{1,0:T(1,128)S(1)} %get-tuple-element.26.meta_ref, f32[256,128]{1,0:T(8,128)S(1)} %bitcast.1, ...), custom_call_target="tpu_custom_call" | custom-call | tf_op jit(solution)/shard_map/first_direction/pallas_call | solution.py:469
  35.0 11.9 %all_to_all.16.own_ref = bf16[16,72,128]{2,1,0:T(8,128)(2,1)S(1)} all-to-all(bf16[16,72,128]{2,1,0:T(8,128)(2,1)S(1)} %get-tuple-element.42), channel_id=1, replica_groups=mesh['fine'=16,'coarse'=2] {'fine'}, dimensions={0} | all-to-all | bytes 589824 | tf_op jit(solution)/shard_map/all_to_all | solution.py:559
  46.9 2.3 %collective-permute-start.7 = (bf16[16,72,128]{2,1,0:T(8,128)(2,1)S(1)}, bf16[16,72,128]{2,1,0:T(8,128)(2,1)S(1)}, u32[]{:S(2)}, u32[]{:S(2)}) collective-permute-start(bf16[16,72,128]{2,1,0:T(8,128)(2,1)S(1)} %all_to_all.16.own_ref), channel_id=1, source_target_pairs={{0,1},{1,0},{2,3},{3,2},{4,5},{5,4},{6,7},{7,6},{8,9},{9,8},{10,11... | collective-permute-start | bytes 884744 | tf_op jit(solution)/shard_map/ppermute | solution.py:561
  49.2 1.2 %collective-permute-done.7.refs_0_ = bf16[16,72,128]{2,1,0:T(8,128)(2,1)S(1)} collective-permute-done((bf16[16,72,128]{2,1,0:T(8,128)(2,1)S(1)}, bf16[16,72,128]{2,1,0:T(8,128)(2,1)S(1)}, u32[]{:S(2)}, u32[]{:S(2)}) %collective-permute-start.7) | collective-permute-done | bytes 294944 | tf_op jit(solution)/shard_map/ppermute | solution.py:561
  50.4 2.0 %second_direction.1 = (bf16[32,24,128]{2,1,0:T(8,128)(2,1)S(1)}, f32[16,1024]{1,0:T(8,128)S(1)}, f32[16,1024]{1,0:T(8,128)S(1)}, f32[16,1024]{1,0:T(8,128)S(1)}, bf16[16,1024]{1,0:T(8,128)(2,1)S(1)}) custom-call(s32[1,128]{1,0:T(1,128)S(1)} %get-tuple-element.26.meta_ref, f32[256,128]{1,0:T(8,128)S(1)} %bitcast.2, ...), custom_call_target="tpu_custom_call" | custom-call | tf_op jit(solution)/shard_map/second_direction/pallas_call | solution.py:469
  52.4 11.5 %all_to_all.17.arrived_ref = bf16[32,24,128]{2,1,0:T(8,128)(2,1)S(1)} all-to-all(bf16[32,24,128]{2,1,0:T(8,128)(2,1)S(1)} %get-tuple-element.43), channel_id=1, replica_groups=mesh['fine'=16,'coarse'=2] {'fine','coarse'}, dimensions={0} | all-to-all | bytes 393216 | tf_op jit(solution)/shard_map/all_to_all | solution.py:492
  63.9 1.5 %finish.1 = (f32[1,16,1024]{2,1,0:T(8,128)}, f32[1,16,1024]{2,1,0:T(8,128)}) custom-call(s32[1,128]{1,0:T(1,128)S(1)} %get-tuple-element.26.meta_ref, bf16[32,24,128]{2,1,0:T(8,128)(2,1)S(1)} %all_to_all.17.arrived_ref, bf16[16,1024]{1,0:T(8,128)(2,1)S(1)} %get-tuple-element.44.applied_ref, f32[16,1024]{1,0:T(8,128)S(1)} %get-tuple-element.45.residual_ref, ...), custom_call_target="tpu_custom_call" | custom-call | tf_op jit(solution)/shard_map/finish/pallas_call | solution.py:469
Async XLA Ops:
  2.7 10.5 %collective-permute-start = (bf16[216,128]{1,0:T(8,128)(2,1)}, bf16[216,128]{1,0:T(8,128)(2,1)S(1)}, u32[]{:S(2)}, u32[]{:S(2)}) collective-permute-start(bf16[216,128]{1,0:T(8,128)(2,1)} %get-tuple-element.28), channel_id=1, source_target_pairs={{0,14},{2,20},{4,18},{6,24},{8,22},{10,28},{12,26},{14,0},{16,30},... | collective-permute-start | bytes 165896 | tf_op jit(solution)/shard_map/ppermute | solution.py:497
  6.8 7.9 %collective-permute-start.1 = (bf16[216,128]{1,0:T(8,128)(2,1)}, bf16[216,128]{1,0:T(8,128)(2,1)S(1)}, u32[]{:S(2)}, u32[]{:S(2)}) collective-permute-start(bf16[216,128]{1,0:T(8,128)(2,1)} %get-tuple-element.29), channel_id=1, source_target_pairs={{0,22},{2,12},{4,26},{6,16},{8,30},{10,20},{12,2},{14,24},{16,6},{... | collective-permute-start | bytes 165896 | tf_op jit(solution)/shard_map/ppermute | solution.py:497
  7.9 12.1 %collective-permute-start.2 = (bf16[216,128]{1,0:T(8,128)(2,1)}, bf16[216,128]{1,0:T(8,128)(2,1)S(1)}, u32[]{:S(2)}, u32[]{:S(2)}) collective-permute-start(bf16[216,128]{1,0:T(8,128)(2,1)} %get-tuple-element.30), channel_id=1, source_target_pairs={{0,6},{2,28},{4,10},{6,0},{8,14},{10,4},{12,18},{14,8},{16,22},{18... | collective-permute-start | bytes 165896 | tf_op jit(solution)/shard_map/ppermute | solution.py:497
  11.2 8.8 %collective-permute-start.3 = (bf16[216,128]{1,0:T(8,128)(2,1)}, bf16[216,128]{1,0:T(8,128)(2,1)S(1)}, u32[]{:S(2)}, u32[]{:S(2)}) collective-permute-start(bf16[216,128]{1,0:T(8,128)(2,1)} %get-tuple-element.31), channel_id=1, source_target_pairs={{0,10},{2,24},{4,14},{6,28},{8,18},{10,0},{12,22},{14,4},{16,26},{... | collective-permute-start | bytes 165896 | tf_op jit(solution)/shard_map/ppermute | solution.py:497
  12.1 7.9 %collective-permute-start.4 = (bf16[216,128]{1,0:T(8,128)(2,1)}, bf16[216,128]{1,0:T(8,128)(2,1)S(1)}, u32[]{:S(2)}, u32[]{:S(2)}) collective-permute-start(bf16[216,128]{1,0:T(8,128)(2,1)} %get-tuple-element.32), channel_id=1, source_target_pairs={{0,18},{2,16},{4,22},{6,20},{8,26},{10,24},{12,30},{14,28},{16,2},... | collective-permute-start | bytes 165896 | tf_op jit(solution)/shard_map/ppermute | solution.py:497
  13.2 6.8 %collective-permute-start.5 = (bf16[216,128]{1,0:T(8,128)(2,1)}, bf16[216,128]{1,0:T(8,128)(2,1)S(1)}, u32[]{:S(2)}, u32[]{:S(2)}) collective-permute-start(bf16[216,128]{1,0:T(8,128)(2,1)} %get-tuple-element.33), channel_id=1, source_target_pairs={{0,2},{2,0},{4,6},{6,4},{8,10},{10,8},{12,14},{14,12},{16,18},{18,... | collective-permute-start | bytes 165896 | tf_op jit(solution)/shard_map/ppermute | solution.py:497
  14.7 5.3 %collective-permute-start.6 = (bf16[216,128]{1,0:T(8,128)(2,1)}, bf16[216,128]{1,0:T(8,128)(2,1)S(1)}, u32[]{:S(2)}, u32[]{:S(2)}) collective-permute-start(bf16[216,128]{1,0:T(8,128)(2,1)} %get-tuple-element.34), channel_id=1, source_target_pairs={{0,1},{1,0},{2,3},{3,2},{4,5},{5,4},{6,7},{7,6},{8,9},{9,8},{10,11... | collective-permute-start | bytes 165896 | tf_op jit(solution)/shard_map/ppermute | solution.py:502
  17.0 1.6 %copy-start = (bf16[1,1024,1024]{2,1,0:T(8,128)(2,1)S(1)}, bf16[1,1024,1024]{2,1,0:T(8,128)(2,1)}, u32[]{:S(2)}) copy-start(bf16[1,1024,1024]{2,1,0:T(8,128)(2,1)} %dual_ref.1) | copy-start | bytes 6291460
  18.6 0.9 %copy-start.1 = (bf16[96,1024]{1,0:T(8,128)(2,1)S(1)}, bf16[96,1024]{1,0:T(8,128)(2,1)}, u32[]{:S(2)}) copy-start(bf16[96,1024]{1,0:T(8,128)(2,1)} %get-tuple-element.25.rows_ref) | copy-start | bytes 589828
  46.9 3.5 %collective-permute-start.7 = (bf16[16,72,128]{2,1,0:T(8,128)(2,1)S(1)}, bf16[16,72,128]{2,1,0:T(8,128)(2,1)S(1)}, u32[]{:S(2)}, u32[]{:S(2)}) collective-permute-start(bf16[16,72,128]{2,1,0:T(8,128)(2,1)S(1)} %all_to_all.16.own_ref), channel_id=1, source_target_pairs={{0,1},{1,0},{2,3},{3,2},{4,5},{5,4},{6,7},{7,6},{8,9},{9,8},{10,11... | collective-permute-start | bytes 884744 | tf_op jit(solution)/shard_map/ppermute | solution.py:561

commit v12 on v11

--- a/solution.py
+++ b/solution.py
@@ -8,7 +8,7 @@
 from jax.sharding import PartitionSpec as P
 
 PLANES = 6
-DISTANCES = (7, 11, 3, 5, 9, 1)
+DISTANCES = (11, 7, 3, 9, 5, 1)
 AXES = ("fine", "coarse")
 LANES = 128
 HALF = 64

time: 65.7 us -> 65.3 us (level)
  blocking collectives: 35.8 us -> 34.5 us
  starting transfers between devices: 16.6 us -> 17.5 us
    all_to_all x2, blocking collectives: 23.9 us -> 22.5 us  [swap_all(): return lax.all_to_all(message, AXES, 0, 0, tiled=True)]
    ppermute x6, starting transfers between devices: 12 us -> 12.9 us  [swap_slot(): return lax.ppermute(message, 'fine', pairs)]
where the time goes in v12:
time: 65.3 us; the launch traced here: 65 us
  blocking collectives  34.5 us (53%)
  starting transfers between devices  17.5 us (27%)
  Pallas kernels  8.56 us (13%)
  local copies, waits for them, and re-layouts  2.52 us (4%)
  waiting for transfers between devices  1.23 us (2%)
  between operations  0.72 us (1%)
    all_to_all x2, blocking collectives, swap_all(): return lax.all_to_all(message, AXES, 0, 0, tiled=True)  22.5 us
    ppermute x6, starting transfers between devices, swap_slot(): return lax.ppermute(message, 'fine', pairs)  12.9 us
    all_to_all x1, blocking collectives, body(): own = lax.all_to_all(message, 'fine', 0, 0, tiled=True)  11.9 us
    pallas_call x6, Pallas kernels, call(): pl.pallas_call(kernel, name=name, out_shape=[jax.ShapeDtypeStruct(shape,...  8.56 us
    unnamed x4, local copies, waits for them, and re-layouts  2.52 us
    ppermute x1, starting transfers between devices, swap_blocks(): lax.ppermute(messages[PLANES], 'coarse', [(0, 1), (1, 0)])  2.36 us
    ppermute x1, starting transfers between devices, body(): others = [lax.ppermute(own, 'coarse', [(0, 1), (1, 0)])]  2.29 us
  transfers between devices with their start and end apart: 8, of which 1 were waited for; matrix products, arithmetic and copies ran while one was open for 0% of the time, Pallas kernels for 1%

profile of v12, /device:TPU:1, one launch (start us, length us, event | category | flops | bytes accessed | tf_op | source)
XLA Modules:
  0.0 65.0 jit_solution(16235316454468270610)
XLA Ops:
  0.6 2.1 %pack_setup.1 = (bf16[96,1024]{1,0:T(8,128)(2,1)}, bf16[216,128]{1,0:T(8,128)(2,1)}, bf16[216,128]{1,0:T(8,128)(2,1)}, bf16[216,128]{1,0:T(8,128)(2,1)}, bf16[21...) custom-call(s32[1,6]{1,0:T(1,128)} %partners_ref.1, ...), custom_call_target="tpu_custom_call" | custom-call | tf_op jit(solution)/shard_map/pack_setup/pallas_call | solution.py:469
  2.7 5.1 %collective-permute-start = (bf16[216,128]{1,0:T(8,128)(2,1)}, bf16[216,128]{1,0:T(8,128)(2,1)S(1)}, u32[]{:S(2)}, u32[]{:S(2)}) collective-permute-start(bf16[216,128]{1,0:T(8,128)(2,1)} %get-tuple-element.28), channel_id=1, source_target_pairs={{0,22},{2,12},{4,26},{6,16},{8,30},{10,20},{12,2},{14,24},{16,6},{... | collective-permute-start | bytes 165896 | tf_op jit(solution)/shard_map/ppermute | solution.py:497
  7.8 1.2 %collective-permute-start.1 = (bf16[216,128]{1,0:T(8,128)(2,1)}, bf16[216,128]{1,0:T(8,128)(2,1)S(1)}, u32[]{:S(2)}, u32[]{:S(2)}) collective-permute-start(bf16[216,128]{1,0:T(8,128)(2,1)} %get-tuple-element.29), channel_id=1, source_target_pairs={{0,14},{2,20},{4,18},{6,24},{8,22},{10,28},{12,26},{14,0},{16,30},... | collective-permute-start | bytes 165896 | tf_op jit(solution)/shard_map/ppermute | solution.py:497
  9.0 1.9 %collective-permute-start.2 = (bf16[216,128]{1,0:T(8,128)(2,1)}, bf16[216,128]{1,0:T(8,128)(2,1)S(1)}, u32[]{:S(2)}, u32[]{:S(2)}) collective-permute-start(bf16[216,128]{1,0:T(8,128)(2,1)} %get-tuple-element.30), channel_id=1, source_target_pairs={{0,6},{2,28},{4,10},{6,0},{8,14},{10,4},{12,18},{14,8},{16,22},{18... | collective-permute-start | bytes 165896 | tf_op jit(solution)/shard_map/ppermute | solution.py:497
  10.9 1.1 %collective-permute-start.3 = (bf16[216,128]{1,0:T(8,128)(2,1)}, bf16[216,128]{1,0:T(8,128)(2,1)S(1)}, u32[]{:S(2)}, u32[]{:S(2)}) collective-permute-start(bf16[216,128]{1,0:T(8,128)(2,1)} %get-tuple-element.31), channel_id=1, source_target_pairs={{0,18},{2,16},{4,22},{6,20},{8,26},{10,24},{12,30},{14,28},{16,2},... | collective-permute-start | bytes 165896 | tf_op jit(solution)/shard_map/ppermute | solution.py:497
  12.0 0.3 collective-permute-start.4
  12.3 0.0 collective-permute-done.refs_0_.refs_1_
  12.3 3.3 %collective-permute-start.5 = (bf16[216,128]{1,0:T(8,128)(2,1)}, bf16[216,128]{1,0:T(8,128)(2,1)S(1)}, u32[]{:S(2)}, u32[]{:S(2)}) collective-permute-start(bf16[216,128]{1,0:T(8,128)(2,1)} %get-tuple-element.33), channel_id=1, source_target_pairs={{0,2},{2,0},{4,6},{6,4},{8,10},{10,8},{12,14},{14,12},{16,18},{18,... | collective-permute-start | bytes 165896 | tf_op jit(solution)/shard_map/ppermute | solution.py:497
  15.6 0.0 collective-permute-done.1.refs_1_.refs_2_
  15.6 2.4 %collective-permute-start.6 = (bf16[216,128]{1,0:T(8,128)(2,1)}, bf16[216,128]{1,0:T(8,128)(2,1)S(1)}, u32[]{:S(2)}, u32[]{:S(2)}) collective-permute-start(bf16[216,128]{1,0:T(8,128)(2,1)} %get-tuple-element.34), channel_id=1, source_target_pairs={{0,1},{1,0},{2,3},{3,2},{4,5},{5,4},{6,7},{7,6},{8,9},{9,8},{10,11... | collective-permute-start | bytes 165896 | tf_op jit(solution)/shard_map/ppermute | solution.py:502
  17.9 0.0 copy-start
  17.9 1.6 %copy-done = bf16[1,1024,1024]{2,1,0:T(8,128)(2,1)S(1)} copy-done((bf16[1,1024,1024]{2,1,0:T(8,128)(2,1)S(1)}, bf16[1,1024,1024]{2,1,0:T(8,128)(2,1)}, u32[]{:S(2)}) %copy-start) | copy-done | bytes 2097176
  19.5 0.0 copy-start.1
  19.5 0.9 %copy-done.1 = bf16[96,1024]{1,0:T(8,128)(2,1)S(1)} copy-done((bf16[96,1024]{1,0:T(8,128)(2,1)S(1)}, bf16[96,1024]{1,0:T(8,128)(2,1)}, u32[]{:S(2)}) %copy-start.1) | copy-done | bytes 196632
  20.5 0.4 stage_operands.1
  20.9 0.0 collective-permute-done.2.refs_2_.refs_3_
  20.9 0.0 collective-permute-done.3.refs_3_.refs_4_
  20.9 0.0 collective-permute-done.4.refs_4_.refs_5_
  20.9 0.0 collective-permute-done.5.refs_5_.refs_6_
  20.9 0.0 collective-permute-done.6.refs_6_.refs_7_
  20.9 0.7 %restrict_residual.1 = (f32[16,1024]{1,0:T(8,128)S(1)}, f32[32,8,128]{2,1,0:T(8,128)S(1)}) custom-call(s32[1,128]{1,0:T(1,128)S(1)} %get-tuple-element.26.meta_ref, bf16[96,1024]{1,0:T(8,128)(2,1)S(1)} %get-tuple-element.27.rows_ref, bf16[216,128]{1,0:T(8,128)(2,1)S(1)} %collective-permute-done.refs_0_.refs_1_, ...), custom_call_target="tpu_custom_call" | custom-call | tf_op jit(solution)/shard_map/restrict_residual/pallas_call | solution.py:469
  21.7 11.0 %all_to_all.15 = f32[32,8,128]{2,1,0:T(8,128)S(1)} all-to-all(f32[32,8,128]{2,1,0:T(8,128)S(1)} %get-tuple-element.36), channel_id=1, replica_groups=mesh['fine'=16,'coarse'=2] {'fine','coarse'}, dimensions={0} | all-to-all | bytes 262144 | tf_op jit(solution)/shard_map/all_to_all | solution.py:492
  32.7 1.9 %first_direction.1 = (bf16[16,72,128]{2,1,0:T(8,128)(2,1)S(1)}, f32[16,1024]{1,0:T(8,128)S(1)}, bf16[16,1024]{1,0:T(8,128)(2,1)S(1)}, bf16[256,256]{1,0:T(8,128)(2,1)S(1)}, bf16[8,256,128]{2,1,0:T(8,128)(2,1)S(1)}) custom-call(s32[1,128]{1,0:T(1,128)S(1)} %get-tuple-element.26.meta_ref, f32[256,128]{1,0:T(8,128)S(1)} %bitcast.1, ...), custom_call_target="tpu_custom_call" | custom-call | tf_op jit(solution)/shard_map/first_direction/pallas_call | solution.py:469
  34.5 11.9 %all_to_all.16.own_ref = bf16[16,72,128]{2,1,0:T(8,128)(2,1)S(1)} all-to-all(bf16[16,72,128]{2,1,0:T(8,128)(2,1)S(1)} %get-tuple-element.42), channel_id=1, replica_groups=mesh['fine'=16,'coarse'=2] {'fine'}, dimensions={0} | all-to-all | bytes 589824 | tf_op jit(solution)/shard_map/all_to_all | solution.py:559
  46.5 2.3 %collective-permute-start.7 = (bf16[16,72,128]{2,1,0:T(8,128)(2,1)S(1)}, bf16[16,72,128]{2,1,0:T(8,128)(2,1)S(1)}, u32[]{:S(2)}, u32[]{:S(2)}) collective-permute-start(bf16[16,72,128]{2,1,0:T(8,128)(2,1)S(1)} %all_to_all.16.own_ref), channel_id=1, source_target_pairs={{0,1},{1,0},{2,3},{3,2},{4,5},{5,4},{6,7},{7,6},{8,9},{9,8},{10,11... | collective-permute-start | bytes 884744 | tf_op jit(solution)/shard_map/ppermute | solution.py:561
  48.8 1.2 %collective-permute-done.7.refs_0_ = bf16[16,72,128]{2,1,0:T(8,128)(2,1)S(1)} collective-permute-done((bf16[16,72,128]{2,1,0:T(8,128)(2,1)S(1)}, bf16[16,72,128]{2,1,0:T(8,128)(2,1)S(1)}, u32[]{:S(2)}, u32[]{:S(2)}) %collective-permute-start.7) | collective-permute-done | bytes 294944 | tf_op jit(solution)/shard_map/ppermute | solution.py:561
  50.0 2.0 %second_direction.1 = (bf16[32,24,128]{2,1,0:T(8,128)(2,1)S(1)}, f32[16,1024]{1,0:T(8,128)S(1)}, f32[16,1024]{1,0:T(8,128)S(1)}, f32[16,1024]{1,0:T(8,128)S(1)}, bf16[16,1024]{1,0:T(8,128)(2,1)S(1)}) custom-call(s32[1,128]{1,0:T(1,128)S(1)} %get-tuple-element.26.meta_ref, f32[256,128]{1,0:T(8,128)S(1)} %bitcast.2, ...), custom_call_target="tpu_custom_call" | custom-call | tf_op jit(solution)/shard_map/second_direction/pallas_call | solution.py:469
  52.0 11.5 %all_to_all.17.arrived_ref = bf16[32,24,128]{2,1,0:T(8,128)(2,1)S(1)} all-to-all(bf16[32,24,128]{2,1,0:T(8,128)(2,1)S(1)} %get-tuple-element.43), channel_id=1, replica_groups=mesh['fine'=16,'coarse'=2] {'fine','coarse'}, dimensions={0} | all-to-all | bytes 393216 | tf_op jit(solution)/shard_map/all_to_all | solution.py:492
  63.5 1.5 %finish.1 = (f32[1,16,1024]{2,1,0:T(8,128)}, f32[1,16,1024]{2,1,0:T(8,128)}) custom-call(s32[1,128]{1,0:T(1,128)S(1)} %get-tuple-element.26.meta_ref, bf16[32,24,128]{2,1,0:T(8,128)(2,1)S(1)} %all_to_all.17.arrived_ref, bf16[16,1024]{1,0:T(8,128)(2,1)S(1)} %get-tuple-element.44.applied_ref, f32[16,1024]{1,0:T(8,128)S(1)} %get-tuple-element.45.residual_ref, ...), custom_call_target="tpu_custom_call" | custom-call | tf_op jit(solution)/shard_map/finish/pallas_call | solution.py:469
Async XLA Ops:
  2.7 9.6 %collective-permute-start = (bf16[216,128]{1,0:T(8,128)(2,1)}, bf16[216,128]{1,0:T(8,128)(2,1)S(1)}, u32[]{:S(2)}, u32[]{:S(2)}) collective-permute-start(bf16[216,128]{1,0:T(8,128)(2,1)} %get-tuple-element.28), channel_id=1, source_target_pairs={{0,22},{2,12},{4,26},{6,16},{8,30},{10,20},{12,2},{14,24},{16,6},{... | collective-permute-start | bytes 165896 | tf_op jit(solution)/shard_map/ppermute | solution.py:497
  7.8 7.8 %collective-permute-start.1 = (bf16[216,128]{1,0:T(8,128)(2,1)}, bf16[216,128]{1,0:T(8,128)(2,1)S(1)}, u32[]{:S(2)}, u32[]{:S(2)}) collective-permute-start(bf16[216,128]{1,0:T(8,128)(2,1)} %get-tuple-element.29), channel_id=1, source_target_pairs={{0,14},{2,20},{4,18},{6,24},{8,22},{10,28},{12,26},{14,0},{16,30},... | collective-permute-start | bytes 165896 | tf_op jit(solution)/shard_map/ppermute | solution.py:497
  9.0 11.9 %collective-permute-start.2 = (bf16[216,128]{1,0:T(8,128)(2,1)}, bf16[216,128]{1,0:T(8,128)(2,1)S(1)}, u32[]{:S(2)}, u32[]{:S(2)}) collective-permute-start(bf16[216,128]{1,0:T(8,128)(2,1)} %get-tuple-element.30), channel_id=1, source_target_pairs={{0,6},{2,28},{4,10},{6,0},{8,14},{10,4},{12,18},{14,8},{16,22},{18... | collective-permute-start | bytes 165896 | tf_op jit(solution)/shard_map/ppermute | solution.py:497
  10.9 10.0 %collective-permute-start.3 = (bf16[216,128]{1,0:T(8,128)(2,1)}, bf16[216,128]{1,0:T(8,128)(2,1)S(1)}, u32[]{:S(2)}, u32[]{:S(2)}) collective-permute-start(bf16[216,128]{1,0:T(8,128)(2,1)} %get-tuple-element.31), channel_id=1, source_target_pairs={{0,18},{2,16},{4,22},{6,20},{8,26},{10,24},{12,30},{14,28},{16,2},... | collective-permute-start | bytes 165896 | tf_op jit(solution)/shard_map/ppermute | solution.py:497
  12.0 8.9 %collective-permute-start.4 = (bf16[216,128]{1,0:T(8,128)(2,1)}, bf16[216,128]{1,0:T(8,128)(2,1)S(1)}, u32[]{:S(2)}, u32[]{:S(2)}) collective-permute-start(bf16[216,128]{1,0:T(8,128)(2,1)} %get-tuple-element.32), channel_id=1, source_target_pairs={{0,10},{2,24},{4,14},{6,28},{8,18},{10,0},{12,22},{14,4},{16,26},{... | collective-permute-start | bytes 165896 | tf_op jit(solution)/shard_map/ppermute | solution.py:497
  12.3 8.6 %collective-permute-start.5 = (bf16[216,128]{1,0:T(8,128)(2,1)}, bf16[216,128]{1,0:T(8,128)(2,1)S(1)}, u32[]{:S(2)}, u32[]{:S(2)}) collective-permute-start(bf16[216,128]{1,0:T(8,128)(2,1)} %get-tuple-element.33), channel_id=1, source_target_pairs={{0,2},{2,0},{4,6},{6,4},{8,10},{10,8},{12,14},{14,12},{16,18},{18,... | collective-permute-start | bytes 165896 | tf_op jit(solution)/shard_map/ppermute | solution.py:497
  15.6 5.3 %collective-permute-start.6 = (bf16[216,128]{1,0:T(8,128)(2,1)}, bf16[216,128]{1,0:T(8,128)(2,1)S(1)}, u32[]{:S(2)}, u32[]{:S(2)}) collective-permute-start(bf16[216,128]{1,0:T(8,128)(2,1)} %get-tuple-element.34), channel_id=1, source_target_pairs={{0,1},{1,0},{2,3},{3,2},{4,5},{5,4},{6,7},{7,6},{8,9},{9,8},{10,11... | collective-permute-start | bytes 165896 | tf_op jit(solution)/shard_map/ppermute | solution.py:502
  17.9 1.6 %copy-start = (bf16[1,1024,1024]{2,1,0:T(8,128)(2,1)S(1)}, bf16[1,1024,1024]{2,1,0:T(8,128)(2,1)}, u32[]{:S(2)}) copy-start(bf16[1,1024,1024]{2,1,0:T(8,128)(2,1)} %dual_ref.1) | copy-start | bytes 6291460
  19.5 0.9 %copy-start.1 = (bf16[96,1024]{1,0:T(8,128)(2,1)S(1)}, bf16[96,1024]{1,0:T(8,128)(2,1)}, u32[]{:S(2)}) copy-start(bf16[96,1024]{1,0:T(8,128)(2,1)} %get-tuple-element.25.rows_ref) | copy-start | bytes 589828
  46.5 3.5 %collective-permute-start.7 = (bf16[16,72,128]{2,1,0:T(8,128)(2,1)S(1)}, bf16[16,72,128]{2,1,0:T(8,128)(2,1)S(1)}, u32[]{:S(2)}, u32[]{:S(2)}) collective-permute-start(bf16[16,72,128]{2,1,0:T(8,128)(2,1)S(1)} %all_to_all.16.own_ref), channel_id=1, source_target_pairs={{0,1},{1,0},{2,3},{3,2},{4,5},{5,4},{6,7},{7,6},{8,9},{9,8},{10,11... | collective-permute-start | bytes 884744 | tf_op jit(solution)/shard_map/ppermute | solution.py:561

commit v13 on v12

--- a/solution.py
+++ b/solution.py
@@ -8,7 +8,7 @@
 from jax.sharding import PartitionSpec as P
 
 PLANES = 6
-DISTANCES = (11, 7, 3, 9, 5, 1)
+DISTANCES = (11, 5, 3, 7, 9, 1)
 AXES = ("fine", "coarse")
 LANES = 128
 HALF = 64

time: 65.3 us -> 65.6 us (level)
  blocking collectives: 34.5 us -> 36.2 us
  starting transfers between devices: 17.5 us -> 16 us
    all_to_all x2, blocking collectives: 22.5 us -> 24.3 us  [swap_all(): return lax.all_to_all(message, AXES, 0, 0, tiled=True)]
    ppermute x6, starting transfers between devices: 12.9 us -> 11.6 us  [swap_slot(): return lax.ppermute(message, 'fine', pairs)]
where the time goes in v13:
time: 65.6 us; the launch traced here: 65.3 us
  blocking collectives  36.2 us (55%)
  starting transfers between devices  16 us (24%)
  Pallas kernels  8.56 us (13%)
  local copies, waits for them, and re-layouts  2.52 us (4%)
  waiting for transfers between devices  1.23 us (2%)
  between operations  0.72 us (1%)
    all_to_all x2, blocking collectives, swap_all(): return lax.all_to_all(message, AXES, 0, 0, tiled=True)  24.3 us
    all_to_all x1, blocking collectives, body(): own = lax.all_to_all(message, 'fine', 0, 0, tiled=True)  11.9 us
    ppermute x6, starting transfers between devices, swap_slot(): return lax.ppermute(message, 'fine', pairs)  11.6 us
    pallas_call x6, Pallas kernels, call(): pl.pallas_call(kernel, name=name, out_shape=[jax.ShapeDtypeStruct(shape,...  8.56 us
    unnamed x4, local copies, waits for them, and re-layouts  2.52 us
    ppermute x1, starting transfers between devices, body(): others = [lax.ppermute(own, 'coarse', [(0, 1), (1, 0)])]  2.29 us
    ppermute x1, starting transfers between devices, swap_blocks(): lax.ppermute(messages[PLANES], 'coarse', [(0, 1), (1, 0)])  2.14 us
  transfers between devices with their start and end apart: 8, of which 1 were waited for; matrix products, arithmetic and copies ran while one was open for 0% of the time, Pallas kernels for 1%

profile of v13, /device:TPU:1, one launch (start us, length us, event | category | flops | bytes accessed | tf_op | source)
XLA Modules:
  0.0 65.3 jit_solution(8087382593160209767)
XLA Ops:
  0.6 2.1 %pack_setup.1 = (bf16[96,1024]{1,0:T(8,128)(2,1)}, bf16[216,128]{1,0:T(8,128)(2,1)}, bf16[216,128]{1,0:T(8,128)(2,1)}, bf16[216,128]{1,0:T(8,128)(2,1)}, bf16[21...) custom-call(s32[1,6]{1,0:T(1,128)} %partners_ref.1, ...), custom_call_target="tpu_custom_call" | custom-call | tf_op jit(solution)/shard_map/pack_setup/pallas_call | solution.py:469
  2.7 5.1 %collective-permute-start = (bf16[216,128]{1,0:T(8,128)(2,1)}, bf16[216,128]{1,0:T(8,128)(2,1)S(1)}, u32[]{:S(2)}, u32[]{:S(2)}) collective-permute-start(bf16[216,128]{1,0:T(8,128)(2,1)} %get-tuple-element.28), channel_id=1, source_target_pairs={{0,22},{2,12},{4,26},{6,16},{8,30},{10,20},{12,2},{14,24},{16,6},{... | collective-permute-start | bytes 165896 | tf_op jit(solution)/shard_map/ppermute | solution.py:497
  7.8 0.3 collective-permute-start.1
  8.0 2.1 %collective-permute-start.2 = (bf16[216,128]{1,0:T(8,128)(2,1)}, bf16[216,128]{1,0:T(8,128)(2,1)S(1)}, u32[]{:S(2)}, u32[]{:S(2)}) collective-permute-start(bf16[216,128]{1,0:T(8,128)(2,1)} %get-tuple-element.30), channel_id=1, source_target_pairs={{0,6},{2,28},{4,10},{6,0},{8,14},{10,4},{12,18},{14,8},{16,22},{18... | collective-permute-start | bytes 165896 | tf_op jit(solution)/shard_map/ppermute | solution.py:497
  10.1 1.3 %collective-permute-start.3 = (bf16[216,128]{1,0:T(8,128)(2,1)}, bf16[216,128]{1,0:T(8,128)(2,1)S(1)}, u32[]{:S(2)}, u32[]{:S(2)}) collective-permute-start(bf16[216,128]{1,0:T(8,128)(2,1)} %get-tuple-element.31), channel_id=1, source_target_pairs={{0,14},{2,20},{4,18},{6,24},{8,22},{10,28},{12,26},{14,0},{16,30},... | collective-permute-start | bytes 165896 | tf_op jit(solution)/shard_map/ppermute | solution.py:497
  11.4 2.9 %collective-permute-start.4 = (bf16[216,128]{1,0:T(8,128)(2,1)}, bf16[216,128]{1,0:T(8,128)(2,1)S(1)}, u32[]{:S(2)}, u32[]{:S(2)}) collective-permute-start(bf16[216,128]{1,0:T(8,128)(2,1)} %get-tuple-element.32), channel_id=1, source_target_pairs={{0,18},{2,16},{4,22},{6,20},{8,26},{10,24},{12,30},{14,28},{16,2},... | collective-permute-start | bytes 165896 | tf_op jit(solution)/shard_map/ppermute | solution.py:497
  14.3 0.0 collective-permute-done.refs_0_.refs_1_
  14.3 0.0 collective-permute-start.5
  14.3 0.0 collective-permute-done.1.refs_1_.refs_2_
  14.3 2.1 %collective-permute-start.6 = (bf16[216,128]{1,0:T(8,128)(2,1)}, bf16[216,128]{1,0:T(8,128)(2,1)S(1)}, u32[]{:S(2)}, u32[]{:S(2)}) collective-permute-start(bf16[216,128]{1,0:T(8,128)(2,1)} %get-tuple-element.34), channel_id=1, source_target_pairs={{0,1},{1,0},{2,3},{3,2},{4,5},{5,4},{6,7},{7,6},{8,9},{9,8},{10,11... | collective-permute-start | bytes 165896 | tf_op jit(solution)/shard_map/ppermute | solution.py:502
  16.5 0.0 copy-start
  16.5 1.6 %copy-done = bf16[1,1024,1024]{2,1,0:T(8,128)(2,1)S(1)} copy-done((bf16[1,1024,1024]{2,1,0:T(8,128)(2,1)S(1)}, bf16[1,1024,1024]{2,1,0:T(8,128)(2,1)}, u32[]{:S(2)}) %copy-start) | copy-done | bytes 2097176
  18.1 0.0 copy-start.1
  18.1 0.9 %copy-done.1 = bf16[96,1024]{1,0:T(8,128)(2,1)S(1)} copy-done((bf16[96,1024]{1,0:T(8,128)(2,1)S(1)}, bf16[96,1024]{1,0:T(8,128)(2,1)}, u32[]{:S(2)}) %copy-start.1) | copy-done | bytes 196632
  19.0 0.4 stage_operands.1
  19.4 0.0 collective-permute-done.2.refs_2_.refs_3_
  19.4 0.0 collective-permute-done.3.refs_3_.refs_4_
  19.4 0.0 collective-permute-done.4.refs_4_.refs_5_
  19.4 0.0 collective-permute-done.5.refs_5_.refs_6_
  19.4 0.0 collective-permute-done.6.refs_6_.refs_7_
  19.5 0.7 %restrict_residual.1 = (f32[16,1024]{1,0:T(8,128)S(1)}, f32[32,8,128]{2,1,0:T(8,128)S(1)}) custom-call(s32[1,128]{1,0:T(1,128)S(1)} %get-tuple-element.26.meta_ref, bf16[96,1024]{1,0:T(8,128)(2,1)S(1)} %get-tuple-element.27.rows_ref, bf16[216,128]{1,0:T(8,128)(2,1)S(1)} %collective-permute-done.refs_0_.refs_1_, ...), custom_call_target="tpu_custom_call" | custom-call | tf_op jit(solution)/shard_map/restrict_residual/pallas_call | solution.py:469
  20.2 12.8 %all_to_all.15 = f32[32,8,128]{2,1,0:T(8,128)S(1)} all-to-all(f32[32,8,128]{2,1,0:T(8,128)S(1)} %get-tuple-element.36), channel_id=1, replica_groups=mesh['fine'=16,'coarse'=2] {'fine','coarse'}, dimensions={0} | all-to-all | bytes 262144 | tf_op jit(solution)/shard_map/all_to_all | solution.py:492
  33.0 1.9 %first_direction.1 = (bf16[16,72,128]{2,1,0:T(8,128)(2,1)S(1)}, f32[16,1024]{1,0:T(8,128)S(1)}, bf16[16,1024]{1,0:T(8,128)(2,1)S(1)}, bf16[256,256]{1,0:T(8,128)(2,1)S(1)}, bf16[8,256,128]{2,1,0:T(8,128)(2,1)S(1)}) custom-call(s32[1,128]{1,0:T(1,128)S(1)} %get-tuple-element.26.meta_ref, f32[256,128]{1,0:T(8,128)S(1)} %bitcast.1, ...), custom_call_target="tpu_custom_call" | custom-call | tf_op jit(solution)/shard_map/first_direction/pallas_call | solution.py:469
  34.8 11.9 %all_to_all.16.own_ref = bf16[16,72,128]{2,1,0:T(8,128)(2,1)S(1)} all-to-all(bf16[16,72,128]{2,1,0:T(8,128)(2,1)S(1)} %get-tuple-element.42), channel_id=1, replica_groups=mesh['fine'=16,'coarse'=2] {'fine'}, dimensions={0} | all-to-all | bytes 589824 | tf_op jit(solution)/shard_map/all_to_all | solution.py:559
  46.8 2.3 %collective-permute-start.7 = (bf16[16,72,128]{2,1,0:T(8,128)(2,1)S(1)}, bf16[16,72,128]{2,1,0:T(8,128)(2,1)S(1)}, u32[]{:S(2)}, u32[]{:S(2)}) collective-permute-start(bf16[16,72,128]{2,1,0:T(8,128)(2,1)S(1)} %all_to_all.16.own_ref), channel_id=1, source_target_pairs={{0,1},{1,0},{2,3},{3,2},{4,5},{5,4},{6,7},{7,6},{8,9},{9,8},{10,11... | collective-permute-start | bytes 884744 | tf_op jit(solution)/shard_map/ppermute | solution.py:561
  49.0 1.2 %collective-permute-done.7.refs_0_ = bf16[16,72,128]{2,1,0:T(8,128)(2,1)S(1)} collective-permute-done((bf16[16,72,128]{2,1,0:T(8,128)(2,1)S(1)}, bf16[16,72,128]{2,1,0:T(8,128)(2,1)S(1)}, u32[]{:S(2)}, u32[]{:S(2)}) %collective-permute-start.7) | collective-permute-done | bytes 294944 | tf_op jit(solution)/shard_map/ppermute | solution.py:561
  50.3 2.0 %second_direction.1 = (bf16[32,24,128]{2,1,0:T(8,128)(2,1)S(1)}, f32[16,1024]{1,0:T(8,128)S(1)}, f32[16,1024]{1,0:T(8,128)S(1)}, f32[16,1024]{1,0:T(8,128)S(1)}, bf16[16,1024]{1,0:T(8,128)(2,1)S(1)}) custom-call(s32[1,128]{1,0:T(1,128)S(1)} %get-tuple-element.26.meta_ref, f32[256,128]{1,0:T(8,128)S(1)} %bitcast.2, ...), custom_call_target="tpu_custom_call" | custom-call | tf_op jit(solution)/shard_map/second_direction/pallas_call | solution.py:469
  52.2 11.5 %all_to_all.17.arrived_ref = bf16[32,24,128]{2,1,0:T(8,128)(2,1)S(1)} all-to-all(bf16[32,24,128]{2,1,0:T(8,128)(2,1)S(1)} %get-tuple-element.43), channel_id=1, replica_groups=mesh['fine'=16,'coarse'=2] {'fine','coarse'}, dimensions={0} | all-to-all | bytes 393216 | tf_op jit(solution)/shard_map/all_to_all | solution.py:492
  63.8 1.5 %finish.1 = (f32[1,16,1024]{2,1,0:T(8,128)}, f32[1,16,1024]{2,1,0:T(8,128)}) custom-call(s32[1,128]{1,0:T(1,128)S(1)} %get-tuple-element.26.meta_ref, bf16[32,24,128]{2,1,0:T(8,128)(2,1)S(1)} %all_to_all.17.arrived_ref, bf16[16,1024]{1,0:T(8,128)(2,1)S(1)} %get-tuple-element.44.applied_ref, f32[16,1024]{1,0:T(8,128)S(1)} %get-tuple-element.45.residual_ref, ...), custom_call_target="tpu_custom_call" | custom-call | tf_op jit(solution)/shard_map/finish/pallas_call | solution.py:469
Async XLA Ops:
  2.7 11.6 %collective-permute-start = (bf16[216,128]{1,0:T(8,128)(2,1)}, bf16[216,128]{1,0:T(8,128)(2,1)S(1)}, u32[]{:S(2)}, u32[]{:S(2)}) collective-permute-start(bf16[216,128]{1,0:T(8,128)(2,1)} %get-tuple-element.28), channel_id=1, source_target_pairs={{0,22},{2,12},{4,26},{6,16},{8,30},{10,20},{12,2},{14,24},{16,6},{... | collective-permute-start | bytes 165896 | tf_op jit(solution)/shard_map/ppermute | solution.py:497
  7.8 6.5 %collective-permute-start.1 = (bf16[216,128]{1,0:T(8,128)(2,1)}, bf16[216,128]{1,0:T(8,128)(2,1)S(1)}, u32[]{:S(2)}, u32[]{:S(2)}) collective-permute-start(bf16[216,128]{1,0:T(8,128)(2,1)} %get-tuple-element.29), channel_id=1, source_target_pairs={{0,10},{2,24},{4,14},{6,28},{8,18},{10,0},{12,22},{14,4},{16,26},{... | collective-permute-start | bytes 165896 | tf_op jit(solution)/shard_map/ppermute | solution.py:497
  8.0 11.4 %collective-permute-start.2 = (bf16[216,128]{1,0:T(8,128)(2,1)}, bf16[216,128]{1,0:T(8,128)(2,1)S(1)}, u32[]{:S(2)}, u32[]{:S(2)}) collective-permute-start(bf16[216,128]{1,0:T(8,128)(2,1)} %get-tuple-element.30), channel_id=1, source_target_pairs={{0,6},{2,28},{4,10},{6,0},{8,14},{10,4},{12,18},{14,8},{16,22},{18... | collective-permute-start | bytes 165896 | tf_op jit(solution)/shard_map/ppermute | solution.py:497
  10.1 9.3 %collective-permute-start.3 = (bf16[216,128]{1,0:T(8,128)(2,1)}, bf16[216,128]{1,0:T(8,128)(2,1)S(1)}, u32[]{:S(2)}, u32[]{:S(2)}) collective-permute-start(bf16[216,128]{1,0:T(8,128)(2,1)} %get-tuple-element.31), channel_id=1, source_target_pairs={{0,14},{2,20},{4,18},{6,24},{8,22},{10,28},{12,26},{14,0},{16,30},... | collective-permute-start | bytes 165896 | tf_op jit(solution)/shard_map/ppermute | solution.py:497
  11.4 8.0 %collective-permute-start.4 = (bf16[216,128]{1,0:T(8,128)(2,1)}, bf16[216,128]{1,0:T(8,128)(2,1)S(1)}, u32[]{:S(2)}, u32[]{:S(2)}) collective-permute-start(bf16[216,128]{1,0:T(8,128)(2,1)} %get-tuple-element.32), channel_id=1, source_target_pairs={{0,18},{2,16},{4,22},{6,20},{8,26},{10,24},{12,30},{14,28},{16,2},... | collective-permute-start | bytes 165896 | tf_op jit(solution)/shard_map/ppermute | solution.py:497
  14.3 5.1 %collective-permute-start.5 = (bf16[216,128]{1,0:T(8,128)(2,1)}, bf16[216,128]{1,0:T(8,128)(2,1)S(1)}, u32[]{:S(2)}, u32[]{:S(2)}) collective-permute-start(bf16[216,128]{1,0:T(8,128)(2,1)} %get-tuple-element.33), channel_id=1, source_target_pairs={{0,2},{2,0},{4,6},{6,4},{8,10},{10,8},{12,14},{14,12},{16,18},{18,... | collective-permute-start | bytes 165896 | tf_op jit(solution)/shard_map/ppermute | solution.py:497
  14.3 5.1 %collective-permute-start.6 = (bf16[216,128]{1,0:T(8,128)(2,1)}, bf16[216,128]{1,0:T(8,128)(2,1)S(1)}, u32[]{:S(2)}, u32[]{:S(2)}) collective-permute-start(bf16[216,128]{1,0:T(8,128)(2,1)} %get-tuple-element.34), channel_id=1, source_target_pairs={{0,1},{1,0},{2,3},{3,2},{4,5},{5,4},{6,7},{7,6},{8,9},{9,8},{10,11... | collective-permute-start | bytes 165896 | tf_op jit(solution)/shard_map/ppermute | solution.py:502
  16.5 1.6 %copy-start = (bf16[1,1024,1024]{2,1,0:T(8,128)(2,1)S(1)}, bf16[1,1024,1024]{2,1,0:T(8,128)(2,1)}, u32[]{:S(2)}) copy-start(bf16[1,1024,1024]{2,1,0:T(8,128)(2,1)} %dual_ref.1) | copy-start | bytes 6291460
  18.1 0.9 %copy-start.1 = (bf16[96,1024]{1,0:T(8,128)(2,1)S(1)}, bf16[96,1024]{1,0:T(8,128)(2,1)}, u32[]{:S(2)}) copy-start(bf16[96,1024]{1,0:T(8,128)(2,1)} %get-tuple-element.25.rows_ref) | copy-start | bytes 589828
  46.8 3.5 %collective-permute-start.7 = (bf16[16,72,128]{2,1,0:T(8,128)(2,1)S(1)}, bf16[16,72,128]{2,1,0:T(8,128)(2,1)S(1)}, u32[]{:S(2)}, u32[]{:S(2)}) collective-permute-start(bf16[16,72,128]{2,1,0:T(8,128)(2,1)S(1)} %all_to_all.16.own_ref), channel_id=1, source_target_pairs={{0,1},{1,0},{2,3},{3,2},{4,5},{5,4},{6,7},{7,6},{8,9},{9,8},{10,11... | collective-permute-start | bytes 884744 | tf_op jit(solution)/shard_map/ppermute | solution.py:561
